TPU v7x, 512 devices: a whole 4x8x8 slice. The times are simulated.
512 devices in a mesh: section: 32 (over y, z_lo, core), seq: 16 (over x, z_hi).
Axes of the slice: x: 4, y: 8, z: 8 (z_hi: 4, z_lo: 2; z = z_hi * 2 + z_lo), core: 2. Of those that a mesh axis runs over, the one named last changes fastest.
Arguments:
- latents: bfloat16 [32, 512, 3072], P('section', None, 'seq'), may hold values from -400 to 400
- patch_order: int32 [8], replicated, may hold values from 0 to 7, each once
- timestep: int32 [1], replicated, may hold values from 0 to 63
- mod_table: float32 [64, 32, 3, 3072], P(None, 'section', None, 'seq'), may hold values from -4 to 4
- w_qkv: bfloat16 [32, 3072, 3, 2048], P('section', None, None, 'seq'), may hold values from -0.36084392 to 0.36084392
- w_out: bfloat16 [32, 2048, 3072], P('section', None, 'seq'), may hold values from -0.125 to 0.125
- kv_cache: bfloat16 [32, 2, 512, 2048], P('section', None, None, 'seq'), may hold values from -9 to 9
Outputs:
- block_out: bfloat16 [32, 512, 3072], P('section', None, 'seq')
- cache_out: bfloat16 [32, 2, 512, 2048], P('section', None, None, 'seq')
Inputs may be any that keep to these rules, and one draw needn't show every extreme that they name: `patch_order`: each of the 8 patches once.
All inputs are finite; a program needn't handle non-finite values.
Results may differ from a plain program's by a relative error of at most 0.015.
Values may be sent and summed in bfloat16 or wider, within the bound.
No kernel may reach another device: no remote copies, remote signals or barrier semaphores. Data moves between devices by JAX's collectives and lax.ppermute only.
A program may use at most 64 MiB of HBM per device.

v0:
```python
import jax
import jax.numpy as jnp
from jax import lax
from jax.sharding import PartitionSpec as P

HEAD_DIM = 128
PATCHES = 8
CHAIN = 4


EPSILON = 1e-06


def from_behind(array, axis, by):
    size = lax.axis_size(axis)
    pairs = [(i, i + by) for i in range(size) if 0 <= i + by < size]
    return lax.ppermute(array, axis, pairs)


def body(latents, patch_order, timestep, mod_table, w_qkv, w_out, kv_cache):
    section_id = lax.axis_index("section")
    position = section_id % CHAIN
    stale_rows = latents[0]
    rows_total, columns = stale_rows.shape
    patch_rows = rows_total // PATCHES
    model_width = w_qkv.shape[1]
    local_att = w_qkv.shape[3]
    heads_local = local_att // HEAD_DIM
    w_flat = w_qkv[0].reshape(model_width, 3 * local_att)
    w_proj = w_out[0]
    picker = (jnp.arange(mod_table.shape[0]) == timestep[0]).astype(jnp.float32)
    mod_now = jnp.einsum("n,nkd->kd", picker, mod_table[:, 0], precision=lax.Precision.HIGHEST)
    score_scale = HEAD_DIM ** (-0.5)

    def add_rows(segment):
        return jnp.dot(segment, w_flat, preferred_element_type=jnp.float32)

    def add_heads(segment):
        return jnp.dot(segment, w_proj, preferred_element_type=jnp.float32)

    def advance(clock, state_now):
        incoming, kv_now, out_rows = state_now
        item_index = clock - position
        active = (item_index >= 0) & (item_index < PATCHES)
        patch_id = patch_order[jnp.clip(item_index, 0, PATCHES - 1)]
        row_start = patch_id * patch_rows
        entering = lax.dynamic_slice_in_dim(stale_rows, row_start, patch_rows, 0)
        rows_in = jnp.where(position == 0, entering, incoming)
        rows_f = rows_in.astype(jnp.float32)
        totals = lax.psum((jnp.sum(rows_f, axis=1), jnp.sum(rows_f * rows_f, axis=1)), "seq")
        row_mean = (totals[0] / model_width)[:, None]
        row_var = (totals[1] / model_width)[:, None] - row_mean * row_mean
        normed = (
            (rows_f - row_mean) * lax.rsqrt(row_var + EPSILON) * (1.0 + mod_now[1]) + mod_now[0]
        ).astype(jnp.bfloat16)
        projected = add_rows(lax.all_gather(normed, "seq", axis=1, tiled=True))
        triple = projected.astype(jnp.bfloat16).reshape(patch_rows, 3, local_att)
        fresh_kv = jnp.stack([triple[:, 1], triple[:, 2]])
        kept_kv = lax.dynamic_slice_in_dim(kv_now, row_start, patch_rows, 1)
        kv_now = lax.dynamic_update_slice_in_dim(
            kv_now, jnp.where(active, fresh_kv, kept_kv), row_start, 1
        )
        queries = triple[:, 0].reshape(patch_rows, heads_local, HEAD_DIM)
        cached_keys = kv_now[0].reshape(rows_total, heads_local, HEAD_DIM)
        values = kv_now[1].reshape(rows_total, heads_local, HEAD_DIM)
        scores = (
            jnp.einsum("rhd,lhd->hrl", queries, cached_keys, preferred_element_type=jnp.float32)
            * score_scale
        )
        row_top = jnp.max(scores, axis=2, keepdims=True)
        exp_terms = jnp.exp(scores - row_top)
        weights_bf = (exp_terms / jnp.sum(exp_terms, axis=2, keepdims=True)).astype(jnp.bfloat16)
        mixed = jnp.einsum("hrl,lhd->rhd", weights_bf, values, preferred_element_type=jnp.float32)
        mixed = mixed.astype(jnp.bfloat16).reshape(patch_rows, local_att)
        projection = add_heads(lax.all_gather(mixed, "seq", axis=1, tiled=True))
        result = (rows_f + mod_now[2] * projection).astype(jnp.bfloat16)
        kept_rows = lax.dynamic_slice_in_dim(out_rows, row_start, patch_rows, 0)
        out_rows = lax.dynamic_update_slice_in_dim(
            out_rows, jnp.where(active, result, kept_rows), row_start, 0
        )
        passed = from_behind(result, "section", 1)
        return (passed, kv_now, out_rows)

    initial = (
        jnp.zeros((patch_rows, columns), jnp.bfloat16),
        kv_cache[0],
        jnp.zeros_like(stale_rows),
    )
    _, kv_final, out_final = lax.fori_loop(0, PATCHES + CHAIN - 1, advance, initial)
    return (out_final[None], kv_final[None])


def solution(mesh):
    return jax.shard_map(
        body,
        mesh=mesh,
        in_specs=(
            P("section", None, "seq"),
            P(),
            P(),
            P(None, "section", None, "seq"),
            P("section", None, None, "seq"),
            P("section", None, "seq"),
            P("section", None, None, "seq"),
        ),
        out_specs=(P("section", None, "seq"), P("section", None, None, "seq")),
        check_vma=False,
    )
```

profile of v0, /device:TPU:32, one launch (start us, length us, event | category | flops | bytes accessed | tf_op | source)
XLA Modules:
  0.0 1548.0 jit_solution(7086668558806170586)
XLA Ops:
  13.5 1532.7 %while.18 = (s32[]{:T(128)}, bf16[64,192]{1,0:T(8,128)(2,1)S(1)}, bf16[2,512,128]{2,1,0:T(8,128)(2,1)}, bf16[512,192]{1,0:T(8,128)(2,1)}, pred[]{:T(512)}, /*ind...) while((s32[]{:T(128)}, bf16[64,192]{1,0:T(8,128)(2,1)S(1)}, ...), condition=%wide.region_7.8_spmd, body=%wide.region_0.7_spmd.sunk | while | flops 218644880 | bytes 9891711 | solution.py:89
  15.6 50.3 %all-reduce.2 = (f32[64]{0:T(128)S(1)}, f32[64]{0:T(128)S(1)}) all-reduce(f32[64]{0:T(128)S(1)} %get-tuple-element.393, f32[64]{0:T(128)S(1)} %get-tuple-element.394), channel_id=1, replica_groups=mesh['section'=32,'seq'=16] {'seq'}, use_global_device_ids=true, to_apply=%region_4.4 | all-reduce | flops 128 | bytes 1024 | tf_op jit(solution)/shard_map/while/body/eval_jaxpr/psum | solution.py:50
  66.0 41.8 %all-gather.4 = bf16[16,192,64]{1,2,0:T(8,128)(2,1)S(1)} all-gather(bf16[1,192,64]{1,2,0:T(8,128)(2,1)S(1)} %fusion.43), channel_id=1, replica_groups=mesh['section'=32,'seq'=16] {'seq'}, dimensions={0}, use_global_device_ids=true | all-gather | bytes 417792 | tf_op jit(solution)/shard_map/while/body/eval_jaxpr/all_gather | solution.py:56
  110.3 41.4 %all-gather.5 = bf16[64,1,2048]{2,0,1:T(8,128)(2,1)S(1)} all-gather(bf16[64,1,128]{2,0,1:T(8,128)(2,1)S(1)} %fusion.48), channel_id=2, replica_groups=mesh['section'=32,'seq'=16] {'seq'}, dimensions={2}, use_global_device_ids=true | all-gather | bytes 278528 | tf_op jit(solution)/shard_map/while/body/eval_jaxpr/all_gather | solution.py:75
  163.4 39.9 %all-reduce.2 = (f32[64]{0:T(128)S(1)}, f32[64]{0:T(128)S(1)}) all-reduce(f32[64]{0:T(128)S(1)} %get-tuple-element.393, f32[64]{0:T(128)S(1)} %get-tuple-element.394), channel_id=1, replica_groups=mesh['section'=32,'seq'=16] {'seq'}, use_global_device_ids=true, to_apply=%region_4.4 | all-reduce | flops 128 | bytes 1024 | tf_op jit(solution)/shard_map/while/body/eval_jaxpr/psum | solution.py:50
  203.4 43.6 %all-gather.4 = bf16[16,192,64]{1,2,0:T(8,128)(2,1)S(1)} all-gather(bf16[1,192,64]{1,2,0:T(8,128)(2,1)S(1)} %fusion.43), channel_id=1, replica_groups=mesh['section'=32,'seq'=16] {'seq'}, dimensions={0}, use_global_device_ids=true | all-gather | bytes 417792 | tf_op jit(solution)/shard_map/while/body/eval_jaxpr/all_gather | solution.py:56
  249.5 40.5 %all-gather.5 = bf16[64,1,2048]{2,0,1:T(8,128)(2,1)S(1)} all-gather(bf16[64,1,128]{2,0,1:T(8,128)(2,1)S(1)} %fusion.48), channel_id=2, replica_groups=mesh['section'=32,'seq'=16] {'seq'}, dimensions={2}, use_global_device_ids=true | all-gather | bytes 278528 | tf_op jit(solution)/shard_map/while/body/eval_jaxpr/all_gather | solution.py:75
  301.7 41.0 %all-reduce.2 = (f32[64]{0:T(128)S(1)}, f32[64]{0:T(128)S(1)}) all-reduce(f32[64]{0:T(128)S(1)} %get-tuple-element.393, f32[64]{0:T(128)S(1)} %get-tuple-element.394), channel_id=1, replica_groups=mesh['section'=32,'seq'=16] {'seq'}, use_global_device_ids=true, to_apply=%region_4.4 | all-reduce | flops 128 | bytes 1024 | tf_op jit(solution)/shard_map/while/body/eval_jaxpr/psum | solution.py:50
  342.8 42.7 %all-gather.4 = bf16[16,192,64]{1,2,0:T(8,128)(2,1)S(1)} all-gather(bf16[1,192,64]{1,2,0:T(8,128)(2,1)S(1)} %fusion.43), channel_id=1, replica_groups=mesh['section'=32,'seq'=16] {'seq'}, dimensions={0}, use_global_device_ids=true | all-gather | bytes 417792 | tf_op jit(solution)/shard_map/while/body/eval_jaxpr/all_gather | solution.py:56
  388.1 41.1 %all-gather.5 = bf16[64,1,2048]{2,0,1:T(8,128)(2,1)S(1)} all-gather(bf16[64,1,128]{2,0,1:T(8,128)(2,1)S(1)} %fusion.48), channel_id=2, replica_groups=mesh['section'=32,'seq'=16] {'seq'}, dimensions={2}, use_global_device_ids=true | all-gather | bytes 278528 | tf_op jit(solution)/shard_map/while/body/eval_jaxpr/all_gather | solution.py:75
  440.8 40.4 %all-reduce.2 = (f32[64]{0:T(128)S(1)}, f32[64]{0:T(128)S(1)}) all-reduce(f32[64]{0:T(128)S(1)} %get-tuple-element.393, f32[64]{0:T(128)S(1)} %get-tuple-element.394), channel_id=1, replica_groups=mesh['section'=32,'seq'=16] {'seq'}, use_global_device_ids=true, to_apply=%region_4.4 | all-reduce | flops 128 | bytes 1024 | tf_op jit(solution)/shard_map/while/body/eval_jaxpr/psum | solution.py:50
  481.3 42.8 %all-gather.4 = bf16[16,192,64]{1,2,0:T(8,128)(2,1)S(1)} all-gather(bf16[1,192,64]{1,2,0:T(8,128)(2,1)S(1)} %fusion.43), channel_id=1, replica_groups=mesh['section'=32,'seq'=16] {'seq'}, dimensions={0}, use_global_device_ids=true | all-gather | bytes 417792 | tf_op jit(solution)/shard_map/while/body/eval_jaxpr/all_gather | solution.py:56
  526.7 40.2 %all-gather.5 = bf16[64,1,2048]{2,0,1:T(8,128)(2,1)S(1)} all-gather(bf16[64,1,128]{2,0,1:T(8,128)(2,1)S(1)} %fusion.48), channel_id=2, replica_groups=mesh['section'=32,'seq'=16] {'seq'}, dimensions={2}, use_global_device_ids=true | all-gather | bytes 278528 | tf_op jit(solution)/shard_map/while/body/eval_jaxpr/all_gather | solution.py:75
  578.5 41.4 %all-reduce.2 = (f32[64]{0:T(128)S(1)}, f32[64]{0:T(128)S(1)}) all-reduce(f32[64]{0:T(128)S(1)} %get-tuple-element.393, f32[64]{0:T(128)S(1)} %get-tuple-element.394), channel_id=1, replica_groups=mesh['section'=32,'seq'=16] {'seq'}, use_global_device_ids=true, to_apply=%region_4.4 | all-reduce | flops 128 | bytes 1024 | tf_op jit(solution)/shard_map/while/body/eval_jaxpr/psum | solution.py:50
  620.0 41.7 %all-gather.4 = bf16[16,192,64]{1,2,0:T(8,128)(2,1)S(1)} all-gather(bf16[1,192,64]{1,2,0:T(8,128)(2,1)S(1)} %fusion.43), channel_id=1, replica_groups=mesh['section'=32,'seq'=16] {'seq'}, dimensions={0}, use_global_device_ids=true | all-gather | bytes 417792 | tf_op jit(solution)/shard_map/while/body/eval_jaxpr/all_gather | solution.py:56
  664.2 41.3 %all-gather.5 = bf16[64,1,2048]{2,0,1:T(8,128)(2,1)S(1)} all-gather(bf16[64,1,128]{2,0,1:T(8,128)(2,1)S(1)} %fusion.48), channel_id=2, replica_groups=mesh['section'=32,'seq'=16] {'seq'}, dimensions={2}, use_global_device_ids=true | all-gather | bytes 278528 | tf_op jit(solution)/shard_map/while/body/eval_jaxpr/all_gather | solution.py:75
  717.2 40.2 %all-reduce.2 = (f32[64]{0:T(128)S(1)}, f32[64]{0:T(128)S(1)}) all-reduce(f32[64]{0:T(128)S(1)} %get-tuple-element.393, f32[64]{0:T(128)S(1)} %get-tuple-element.394), channel_id=1, replica_groups=mesh['section'=32,'seq'=16] {'seq'}, use_global_device_ids=true, to_apply=%region_4.4 | all-reduce | flops 128 | bytes 1024 | tf_op jit(solution)/shard_map/while/body/eval_jaxpr/psum | solution.py:50
  757.5 43.4 %all-gather.4 = bf16[16,192,64]{1,2,0:T(8,128)(2,1)S(1)} all-gather(bf16[1,192,64]{1,2,0:T(8,128)(2,1)S(1)} %fusion.43), channel_id=1, replica_groups=mesh['section'=32,'seq'=16] {'seq'}, dimensions={0}, use_global_device_ids=true | all-gather | bytes 417792 | tf_op jit(solution)/shard_map/while/body/eval_jaxpr/all_gather | solution.py:56
  803.4 40.5 %all-gather.5 = bf16[64,1,2048]{2,0,1:T(8,128)(2,1)S(1)} all-gather(bf16[64,1,128]{2,0,1:T(8,128)(2,1)S(1)} %fusion.48), channel_id=2, replica_groups=mesh['section'=32,'seq'=16] {'seq'}, dimensions={2}, use_global_device_ids=true | all-gather | bytes 278528 | tf_op jit(solution)/shard_map/while/body/eval_jaxpr/all_gather | solution.py:75
  855.5 40.9 %all-reduce.2 = (f32[64]{0:T(128)S(1)}, f32[64]{0:T(128)S(1)}) all-reduce(f32[64]{0:T(128)S(1)} %get-tuple-element.393, f32[64]{0:T(128)S(1)} %get-tuple-element.394), channel_id=1, replica_groups=mesh['section'=32,'seq'=16] {'seq'}, use_global_device_ids=true, to_apply=%region_4.4 | all-reduce | flops 128 | bytes 1024 | tf_op jit(solution)/shard_map/while/body/eval_jaxpr/psum | solution.py:50
  896.5 42.3 %all-gather.4 = bf16[16,192,64]{1,2,0:T(8,128)(2,1)S(1)} all-gather(bf16[1,192,64]{1,2,0:T(8,128)(2,1)S(1)} %fusion.43), channel_id=1, replica_groups=mesh['section'=32,'seq'=16] {'seq'}, dimensions={0}, use_global_device_ids=true | all-gather | bytes 417792 | tf_op jit(solution)/shard_map/while/body/eval_jaxpr/all_gather | solution.py:56
  941.3 41.4 %all-gather.5 = bf16[64,1,2048]{2,0,1:T(8,128)(2,1)S(1)} all-gather(bf16[64,1,128]{2,0,1:T(8,128)(2,1)S(1)} %fusion.48), channel_id=2, replica_groups=mesh['section'=32,'seq'=16] {'seq'}, dimensions={2}, use_global_device_ids=true | all-gather | bytes 278528 | tf_op jit(solution)/shard_map/while/body/eval_jaxpr/all_gather | solution.py:75
  994.3 40.4 %all-reduce.2 = (f32[64]{0:T(128)S(1)}, f32[64]{0:T(128)S(1)}) all-reduce(f32[64]{0:T(128)S(1)} %get-tuple-element.393, f32[64]{0:T(128)S(1)} %get-tuple-element.394), channel_id=1, replica_groups=mesh['section'=32,'seq'=16] {'seq'}, use_global_device_ids=true, to_apply=%region_4.4 | all-reduce | flops 128 | bytes 1024 | tf_op jit(solution)/shard_map/while/body/eval_jaxpr/psum | solution.py:50
  1034.8 43.3 %all-gather.4 = bf16[16,192,64]{1,2,0:T(8,128)(2,1)S(1)} all-gather(bf16[1,192,64]{1,2,0:T(8,128)(2,1)S(1)} %fusion.43), channel_id=1, replica_groups=mesh['section'=32,'seq'=16] {'seq'}, dimensions={0}, use_global_device_ids=true | all-gather | bytes 417792 | tf_op jit(solution)/shard_map/while/body/eval_jaxpr/all_gather | solution.py:56
  1132.0 42.0 %all-reduce.2 = (f32[64]{0:T(128)S(1)}, f32[64]{0:T(128)S(1)}) all-reduce(f32[64]{0:T(128)S(1)} %get-tuple-element.393, f32[64]{0:T(128)S(1)} %get-tuple-element.394), channel_id=1, replica_groups=mesh['section'=32,'seq'=16] {'seq'}, use_global_device_ids=true, to_apply=%region_4.4 | all-reduce | flops 128 | bytes 1024 | tf_op jit(solution)/shard_map/while/body/eval_jaxpr/psum | solution.py:50
  1174.1 42.1 %all-gather.4 = bf16[16,192,64]{1,2,0:T(8,128)(2,1)S(1)} all-gather(bf16[1,192,64]{1,2,0:T(8,128)(2,1)S(1)} %fusion.43), channel_id=1, replica_groups=mesh['section'=32,'seq'=16] {'seq'}, dimensions={0}, use_global_device_ids=true | all-gather | bytes 417792 | tf_op jit(solution)/shard_map/while/body/eval_jaxpr/all_gather | solution.py:56
  1218.7 41.6 %all-gather.5 = bf16[64,1,2048]{2,0,1:T(8,128)(2,1)S(1)} all-gather(bf16[64,1,128]{2,0,1:T(8,128)(2,1)S(1)} %fusion.48), channel_id=2, replica_groups=mesh['section'=32,'seq'=16] {'seq'}, dimensions={2}, use_global_device_ids=true | all-gather | bytes 278528 | tf_op jit(solution)/shard_map/while/body/eval_jaxpr/all_gather | solution.py:75
  1311.8 43.6 %all-gather.4 = bf16[16,192,64]{1,2,0:T(8,128)(2,1)S(1)} all-gather(bf16[1,192,64]{1,2,0:T(8,128)(2,1)S(1)} %fusion.43), channel_id=1, replica_groups=mesh['section'=32,'seq'=16] {'seq'}, dimensions={0}, use_global_device_ids=true | all-gather | bytes 417792 | tf_op jit(solution)/shard_map/while/body/eval_jaxpr/all_gather | solution.py:56
  1358.0 40.7 %all-gather.5 = bf16[64,1,2048]{2,0,1:T(8,128)(2,1)S(1)} all-gather(bf16[64,1,128]{2,0,1:T(8,128)(2,1)S(1)} %fusion.48), channel_id=2, replica_groups=mesh['section'=32,'seq'=16] {'seq'}, dimensions={2}, use_global_device_ids=true | all-gather | bytes 278528 | tf_op jit(solution)/shard_map/while/body/eval_jaxpr/all_gather | solution.py:75
  1410.3 40.6 %all-reduce.2 = (f32[64]{0:T(128)S(1)}, f32[64]{0:T(128)S(1)}) all-reduce(f32[64]{0:T(128)S(1)} %get-tuple-element.393, f32[64]{0:T(128)S(1)} %get-tuple-element.394), channel_id=1, replica_groups=mesh['section'=32,'seq'=16] {'seq'}, use_global_device_ids=true, to_apply=%region_4.4 | all-reduce | flops 128 | bytes 1024 | tf_op jit(solution)/shard_map/while/body/eval_jaxpr/psum | solution.py:50
  1451.0 42.6 %all-gather.4 = bf16[16,192,64]{1,2,0:T(8,128)(2,1)S(1)} all-gather(bf16[1,192,64]{1,2,0:T(8,128)(2,1)S(1)} %fusion.43), channel_id=1, replica_groups=mesh['section'=32,'seq'=16] {'seq'}, dimensions={0}, use_global_device_ids=true | all-gather | bytes 417792 | tf_op jit(solution)/shard_map/while/body/eval_jaxpr/all_gather | solution.py:56
  1496.2 40.6 %all-gather.5 = bf16[64,1,2048]{2,0,1:T(8,128)(2,1)S(1)} all-gather(bf16[64,1,128]{2,0,1:T(8,128)(2,1)S(1)} %fusion.48), channel_id=2, replica_groups=mesh['section'=32,'seq'=16] {'seq'}, dimensions={2}, use_global_device_ids=true | all-gather | bytes 278528 | tf_op jit(solution)/shard_map/while/body/eval_jaxpr/all_gather | solution.py:75
  (262 shorter events, 242.0 us)
Async XLA Ops:
  6.6 3.1 copy-start.2
  6.6 4.4 copy-start.3
  6.6 5.9 copy-start.4
  9.7 3.8 copy-start.5
  108.6 1.0 copy-start
  109.6 51.6 %copy-start.1 = (bf16[2,512,128]{2,1,0:T(8,128)(2,1)}, bf16[2,512,128]{2,1,0:T(8,128)(2,1)S(1)}, u32[]{:S(2)}) copy-start(bf16[2,512,128]{2,1,0:T(8,128)(2,1)S(1)} %fusion.45) | copy-start | bytes 786436 | tf_op jit(solution)/shard_map/while
  153.9 7.3 collective-permute-start
  247.8 1.0 copy-start
  248.8 50.7 %copy-start.1 = (bf16[2,512,128]{2,1,0:T(8,128)(2,1)}, bf16[2,512,128]{2,1,0:T(8,128)(2,1)S(1)}, u32[]{:S(2)}) copy-start(bf16[2,512,128]{2,1,0:T(8,128)(2,1)S(1)} %fusion.45) | copy-start | bytes 786436 | tf_op jit(solution)/shard_map/while
  292.2 7.3 collective-permute-start
  386.4 1.0 copy-start
  387.4 51.3 %copy-start.1 = (bf16[2,512,128]{2,1,0:T(8,128)(2,1)}, bf16[2,512,128]{2,1,0:T(8,128)(2,1)S(1)}, u32[]{:S(2)}) copy-start(bf16[2,512,128]{2,1,0:T(8,128)(2,1)S(1)} %fusion.45) | copy-start | bytes 786436 | tf_op jit(solution)/shard_map/while
  431.3 7.3 collective-permute-start
  525.0 1.0 copy-start
  525.9 50.4 %copy-start.1 = (bf16[2,512,128]{2,1,0:T(8,128)(2,1)}, bf16[2,512,128]{2,1,0:T(8,128)(2,1)S(1)}, u32[]{:S(2)}) copy-start(bf16[2,512,128]{2,1,0:T(8,128)(2,1)S(1)} %fusion.45) | copy-start | bytes 786436 | tf_op jit(solution)/shard_map/while
  569.0 7.3 collective-permute-start
  662.5 1.0 copy-start
  663.5 51.5 %copy-start.1 = (bf16[2,512,128]{2,1,0:T(8,128)(2,1)}, bf16[2,512,128]{2,1,0:T(8,128)(2,1)S(1)}, u32[]{:S(2)}) copy-start(bf16[2,512,128]{2,1,0:T(8,128)(2,1)S(1)} %fusion.45) | copy-start | bytes 786436 | tf_op jit(solution)/shard_map/while
  707.7 7.3 collective-permute-start
  801.7 1.0 copy-start
  802.7 50.6 %copy-start.1 = (bf16[2,512,128]{2,1,0:T(8,128)(2,1)}, bf16[2,512,128]{2,1,0:T(8,128)(2,1)S(1)}, u32[]{:S(2)}) copy-start(bf16[2,512,128]{2,1,0:T(8,128)(2,1)S(1)} %fusion.45) | copy-start | bytes 786436 | tf_op jit(solution)/shard_map/while
  846.0 7.3 collective-permute-start
  940.6 51.6 %copy-start.1 = (bf16[2,512,128]{2,1,0:T(8,128)(2,1)}, bf16[2,512,128]{2,1,0:T(8,128)(2,1)S(1)}, u32[]{:S(2)}) copy-start(bf16[2,512,128]{2,1,0:T(8,128)(2,1)S(1)} %fusion.45) | copy-start | bytes 786436 | tf_op jit(solution)/shard_map/while
  984.9 7.3 collective-permute-start
  1079.9 49.9 %copy-start.1 = (bf16[2,512,128]{2,1,0:T(8,128)(2,1)}, bf16[2,512,128]{2,1,0:T(8,128)(2,1)S(1)}, u32[]{:S(2)}) copy-start(bf16[2,512,128]{2,1,0:T(8,128)(2,1)S(1)} %fusion.45) | copy-start | bytes 786436 | tf_op jit(solution)/shard_map/while
  1122.5 7.4 collective-permute-start
  1218.0 51.7 %copy-start.1 = (bf16[2,512,128]{2,1,0:T(8,128)(2,1)}, bf16[2,512,128]{2,1,0:T(8,128)(2,1)S(1)}, u32[]{:S(2)}) copy-start(bf16[2,512,128]{2,1,0:T(8,128)(2,1)S(1)} %fusion.45) | copy-start | bytes 786436 | tf_op jit(solution)/shard_map/while
  1262.4 7.3 collective-permute-start
  1357.3 50.9 %copy-start.1 = (bf16[2,512,128]{2,1,0:T(8,128)(2,1)}, bf16[2,512,128]{2,1,0:T(8,128)(2,1)S(1)}, u32[]{:S(2)}) copy-start(bf16[2,512,128]{2,1,0:T(8,128)(2,1)S(1)} %fusion.45) | copy-start | bytes 786436 | tf_op jit(solution)/shard_map/while
  1400.8 7.3 collective-permute-start
  1495.5 50.7 %copy-start.1 = (bf16[2,512,128]{2,1,0:T(8,128)(2,1)}, bf16[2,512,128]{2,1,0:T(8,128)(2,1)S(1)}, u32[]{:S(2)}) copy-start(bf16[2,512,128]{2,1,0:T(8,128)(2,1)S(1)} %fusion.45) | copy-start | bytes 786436 | tf_op jit(solution)/shard_map/while
  1538.9 7.3 collective-permute-start
  (5 other events, 4.8 us)
where the time goes:
time: 1550 us
  blocking collectives  1380 us (89%)
  waiting for transfers between devices  59.5 us (4%)
  local copies, waits for them, and re-layouts  34.6 us (2%)
  matrix products  34.1 us (2%)
  starting transfers between devices  21 us (1%)
    all_gather x11, blocking collectives, advance(): projected = add_rows(lax.all_gather(normed, 'seq', axis=1, tiled=True))  470 us
    psum x11, blocking collectives, advance(): lax.psum((jnp.sum(rows_f, axis=1), jnp.sum(rows_f * rows_f, axis=1)), 'seq')  457 us
    all_gather x11, blocking collectives, advance(): projection = add_heads(lax.all_gather(mixed, 'seq', axis=1, tiled=True))  449 us
    ppermute x11, waiting for transfers between devices, from_behind(): return lax.ppermute(array, axis, pairs)  59.5 us
  transfers between devices with their start and end apart: 11, of which 11 were waited for; matrix products, arithmetic and copies ran while one was open for 0% of the time, Pallas kernels for 0%

commit v1 on v0

v1 whole, which is shorter than its diff:
```python
import functools

import jax
import jax.numpy as jnp
from jax import lax
from jax.experimental import pallas as pl
from jax.experimental.pallas import tpu as pltpu
from jax.sharding import PartitionSpec as P

HEAD_DIM = 128
PATCHES = 8
CHAIN = 4
EPSILON = 1e-06
ROWS = 64
GROUP = PATCHES // 2
HALF = GROUP * ROWS
LANES = 128
REST = 64
SHARD = LANES + REST
PACK = HALF + HALF // 2
MODS = 16
F32 = jnp.float32
BF16 = jnp.bfloat16
VMEM = pl.BlockSpec(memory_space=pltpu.VMEM)
SMEM = pl.BlockSpec(memory_space=pltpu.SMEM)
ANY = pl.BlockSpec(memory_space=pl.ANY)


def params():
    return pltpu.CompilerParams(vmem_limit_bytes=20 * 1024 * 1024)


def low_lanes(rows):
    return lax.broadcasted_iota(jnp.int32, (rows, LANES), 1) < REST


def patch_at(order_ref, j):
    return pl.ds(pl.multiple_of(order_ref[j] * ROWS, ROWS), ROWS)


def pack_kernel(order_ref, lat_ref, mod_ref, own_ref, send_ref, rows_ref):
    rows_ref[:, :SHARD] = lat_ref[...].astype(F32).T
    low = low_lanes(ROWS)
    for group, out in ((0, own_ref), (1, send_ref)):
        rest = []
        for j in range(GROUP):
            at = patch_at(order_ref, group * GROUP + j)
            out[j * ROWS : (j + 1) * ROWS, :] = rows_ref[at, :LANES].astype(BF16)
            rest.append(rows_ref[at, LANES:])
        for j in range(2):
            both = jnp.where(low, rest[j], pltpu.roll(rest[j + 2], REST, 1))
            out[HALF + j * ROWS : HALF + (j + 1) * ROWS, :] = both.astype(BF16)
    mod = mod_ref[...]
    kinds = (1.0 + mod[1:2], mod[0:1], mod[2:3])
    lines = []
    for kind in kinds:
        first = kind[:, :LANES]
        last = jnp.concatenate([kind[:, LANES:], kind[:, LANES:]], axis=1)
        for value in (first, last):
            high = value.astype(BF16).astype(F32)
            lines += [high, value - high]
    lines.append(jnp.zeros((MODS - len(lines), LANES), F32))
    send_ref[PACK:, :] = jnp.concatenate(lines, axis=0).astype(BF16)


def spread_kernel(copies, x_ref, mods_ref, out_ref):
    for s in range(copies):
        out_ref[s, :PACK, :] = x_ref[...]
        out_ref[s, PACK:, :] = mods_ref[...]


def project_kernel(sources, flag_ref, x_ref, own_ref, peer_ref, q_ref, kv_ref, wm_ref, wr_ref, nm_ref, nr_ref, sems):
    def copies(w_ref):
        found = []
        for t in range(3):
            lanes = pl.ds(t * HEAD_DIM, HEAD_DIM)
            found.append(pltpu.make_async_copy(w_ref.at[t, :, :LANES, :], wm_ref.at[:, :, lanes], sems.at[2 * t]))
            found.append(pltpu.make_async_copy(w_ref.at[t, :, LANES:, :], wr_ref.at[:, :, lanes], sems.at[2 * t + 1]))
        return found

    @pl.when(flag_ref[0] == 1)
    def _():
        for copy in copies(own_ref):
            copy.start()

    @pl.when(flag_ref[0] == 0)
    def _():
        for copy in copies(peer_ref):
            copy.start()

    width = sources * SHARD
    low = low_lanes(ROWS)

    def line(s, k):
        at = PACK + 2 * k
        pair = x_ref[s, PACK:, :].astype(F32)
        return pair[2 * k : 2 * k + 1] + pair[2 * k + 1 : 2 * k + 2]

    scale_first = [line(s, 0) for s in range(sources)]
    shift_first = [line(s, 2) for s in range(sources)]
    scale_last = [jnp.where(low[:1], line(2 * p, 1), line(2 * p + 1, 1)) for p in range(sources // 2)]
    shift_last = [jnp.where(low[:1], line(2 * p, 3), line(2 * p + 1, 3)) for p in range(sources // 2)]
    for j in range(GROUP):
        mine = pl.ds(j * ROWS, ROWS)
        rest = pl.ds(HALF + (j % 2) * ROWS, ROWS)
        total = jnp.zeros((ROWS, LANES), F32)
        square = jnp.zeros((ROWS, LANES), F32)
        total_rest = jnp.zeros((ROWS, LANES), F32)
        square_rest = jnp.zeros((ROWS, LANES), F32)
        for s in range(sources):
            x = x_ref[s, mine, :].astype(F32)
            total = total + x
            square = square + x * x
            x = x_ref[s, rest, :].astype(F32)
            total_rest = total_rest + x
            square_rest = square_rest + x * x
        in_half = low if j < 2 else jnp.logical_not(low)
        total = total + jnp.where(in_half, total_rest, 0.0)
        square = square + jnp.where(in_half, square_rest, 0.0)
        mean = jnp.sum(total, axis=1, keepdims=True) / width
        var = jnp.sum(square, axis=1, keepdims=True) / width - mean * mean
        rstd = lax.rsqrt(var + EPSILON)
        for s in range(sources):
            x = x_ref[s, mine, :].astype(F32)
            normed = (x - mean) * rstd * scale_first[s] + shift_first[s]
            nm_ref[mine, s * LANES : (s + 1) * LANES] = normed.astype(BF16)
        for p in range(sources // 2):
            even = x_ref[2 * p, rest, :].astype(F32)
            odd = x_ref[2 * p + 1, rest, :].astype(F32)
            if j < 2:
                x = jnp.where(low, even, pltpu.roll(odd, REST, 1))
            else:
                x = jnp.where(low, pltpu.roll(even, REST, 1), odd)
            normed = (x - mean) * rstd * scale_last[p] + shift_last[p]
            nr_ref[mine, p * LANES : (p + 1) * LANES] = normed.astype(BF16)

    for copy in copies(own_ref):
        copy.wait()
    w_first = wm_ref[...].reshape(sources * LANES, 3 * HEAD_DIM)
    w_last = wr_ref[...].reshape(sources * REST, 3 * HEAD_DIM)
    qkv = jnp.dot(nm_ref[...], w_first, preferred_element_type=F32)
    qkv = qkv + jnp.dot(nr_ref[...], w_last, preferred_element_type=F32)
    qkv = qkv.astype(BF16)
    q_ref[...] = qkv[:, :HEAD_DIM]
    kv_ref[0] = qkv[:, HEAD_DIM : 2 * HEAD_DIM]
    kv_ref[1] = qkv[:, 2 * HEAD_DIM :]


def attend_kernel(copies, flag_ref, order_ref, q_ref, kv_ref, other_ref, own_ref, peer_ref, out_ref):
    mine = flag_ref[0] == 1
    core = flag_ref[1]

    def stale(part, j):
        at = patch_at(order_ref, j)
        return jnp.where(mine, own_ref[part, at, :], peer_ref[part, at, :])

    old, other = [], []
    for part in range(2):
        old.append([stale(part, core * GROUP + j) for j in range(GROUP)])
        kept = jnp.concatenate([stale(part, (1 - core) * GROUP + j) for j in range(GROUP)], axis=0)
        other.append(jnp.where(core == 1, other_ref[part], kept))
    for j in range(GROUP):
        at = slice(j * ROWS, (j + 1) * ROWS)
        keys, values = (
            jnp.concatenate([kv_ref[part, : (j + 1) * ROWS, :]] + old[part][j + 1 :] + [other[part]], axis=0)
            for part in range(2)
        )
        scores = lax.dot_general(q_ref[at, :], keys, (((1,), (1,)), ((), ())), preferred_element_type=F32)
        scores = scores * HEAD_DIM ** (-0.5)
        terms = jnp.exp(scores - jnp.max(scores, axis=1, keepdims=True))
        weights = (terms / jnp.sum(terms, axis=1, keepdims=True)).astype(BF16)
        mixed = jnp.dot(weights, values, preferred_element_type=F32).astype(BF16)
        for s in range(copies):
            out_ref[s, at, :] = mixed


def update_kernel(heads, last, flag_ref, mixed_ref, own_ref, peer_ref, x_ref, mods_ref, *refs):
    if last:
        next_ref, (new_ref, w_ref, held_ref, sem) = None, refs
    else:
        next_ref, new_ref, spread_ref, w_ref, held_ref, sem = refs

    @pl.when(flag_ref[0] == 1)
    def _():
        pltpu.make_async_copy(own_ref, w_ref, sem).start()

    @pl.when(flag_ref[0] == 0)
    def _():
        pltpu.make_async_copy(peer_ref, w_ref, sem).start()

    mixed = jnp.concatenate([mixed_ref[h] for h in range(heads)], axis=1)
    pltpu.make_async_copy(own_ref, w_ref, sem).wait()
    held_ref[:, :SHARD] = lax.dot_general(mixed, w_ref[...], (((1,), (1,)), ((), ())), preferred_element_type=F32)
    mods = mods_ref[...].astype(F32)
    gate_first = mods[8:9] + mods[9:10]
    gate_last = mods[10:11] + mods[11:12]
    first = x_ref[:HALF, :].astype(F32) + gate_first * held_ref[:, :LANES]
    rest = jnp.where(
        low_lanes(HALF // 2), held_ref[: HALF // 2, LANES:], pltpu.roll(held_ref[HALF // 2 :, LANES:], REST, 1)
    )
    rest = x_ref[HALF:, :].astype(F32) + gate_last * rest
    first, rest = first.astype(BF16), rest.astype(BF16)
    new_ref[:HALF, :] = first
    new_ref[HALF:, :] = rest
    if not last:
        for s in range(heads):
            spread_ref[s, :HALF, :] = first
            spread_ref[s, HALF:PACK, :] = rest
            spread_ref[s, PACK:, :] = next_ref[...]


def finish_kernel(flag_ref, order_ref, mine_ref, other_ref, kv_ref, kv_other_ref, out_ref, cache_ref, rows_ref):
    core = flag_ref[0]
    for whose, (x_ref, new_ref) in enumerate(((mine_ref, kv_ref), (other_ref, kv_other_ref))):
        group = core if whose == 0 else 1 - core
        for j in range(GROUP):
            at = patch_at(order_ref, group * GROUP + j)
            here = slice(j * ROWS, (j + 1) * ROWS)
            rest = x_ref[HALF + (j % 2) * ROWS : HALF + (j % 2 + 1) * ROWS, :].astype(F32)
            rows_ref[at, :LANES] = x_ref[here, :].astype(F32)
            rows_ref[at, LANES:] = rest if j < 2 else pltpu.roll(rest, REST, 1)
            for part in range(2):
                cache_ref[part, at, :] = new_ref[part, here, :]
    out_ref[...] = rows_ref[...].T[:SHARD, :].astype(BF16)


def body(latents, patch_order, timestep, mod_table, w_qkv, w_out, kv_cache):
    sections, seq = lax.axis_size("section"), lax.axis_size("seq")
    section = lax.axis_index("section")
    core = (section % 2).astype(jnp.int32)
    second = (section // 2) % 2
    swap_pairs = [(i, i ^ 1) for i in range(sections)]
    hop_pairs = [(i, i + 2) for i in range(sections) if i % CHAIN < 2]

    def swap(value):
        return lax.ppermute(value, "section", swap_pairs)

    def everyone(spread):
        return lax.all_to_all(spread, "seq", 0, 0)

    def shaped(*shape, dtype=BF16):
        return jax.ShapeDtypeStruct(shape, dtype)

    w_own = jnp.transpose(w_qkv[0], (1, 0, 2))
    o_own = jnp.transpose(w_out[0], (1, 0))
    cache_own = kv_cache[0]
    mod_now = lax.dynamic_index_in_dim(mod_table, timestep[0], 0, keepdims=False)[0]
    width = w_own.shape[1]

    own, send = pl.pallas_call(
        pack_kernel,
        out_shape=(shaped(PACK, LANES), shaped(PACK + MODS, LANES)),
        in_specs=[SMEM, VMEM, VMEM],
        out_specs=(VMEM, VMEM),
        scratch_shapes=[pltpu.VMEM((PATCHES * ROWS, 2 * LANES), F32)],
        compiler_params=params(),
        name="pack",
    )(patch_order, jnp.transpose(latents[0], (1, 0)), mod_now)
    got = swap(send)
    entering = jnp.where(core == 0, own, got[:PACK])
    mods_own, mods_peer = send[PACK:], got[PACK:]

    def run(entering):
        w_peer, o_peer, cache_peer = swap(w_own), swap(o_own), swap(cache_own)
        x = entering
        mods = [jnp.where(core == t, mods_own, mods_peer) for t in range(2)]
        spread = pl.pallas_call(
            functools.partial(spread_kernel, seq),
            out_shape=shaped(seq, PACK + MODS, LANES),
            in_specs=[VMEM, VMEM],
            out_specs=VMEM,
            compiler_params=params(),
            name="spread",
        )(x, mods[0])
        kept = []
        for t in range(2):
            flags = jnp.stack([(core == t).astype(jnp.int32), core])
            gathered = everyone(spread)
            q, kv = pl.pallas_call(
                functools.partial(project_kernel, seq),
                out_shape=(shaped(HALF, HEAD_DIM), shaped(2, HALF, HEAD_DIM)),
                in_specs=[SMEM, VMEM, ANY, ANY],
                out_specs=(VMEM, VMEM),
                scratch_shapes=[
                    pltpu.VMEM((seq, LANES, 3 * HEAD_DIM), BF16),
                    pltpu.VMEM((seq, REST, 3 * HEAD_DIM), BF16),
                    pltpu.VMEM((HALF, seq * LANES), BF16),
                    pltpu.VMEM((HALF, seq * REST), BF16),
                    pltpu.SemaphoreType.DMA((6,)),
                ],
                compiler_params=params(),
                name="project",
            )(
                flags,
                gathered,
                w_own.reshape(3, seq, width // seq, HEAD_DIM),
                w_peer.reshape(3, seq, width // seq, HEAD_DIM),
            )
            kv_other = swap(kv)
            mixed = pl.pallas_call(
                functools.partial(attend_kernel, seq),
                out_shape=shaped(seq, HALF, HEAD_DIM),
                in_specs=[SMEM, SMEM, VMEM, VMEM, VMEM, VMEM, VMEM],
                out_specs=VMEM,
                compiler_params=params(),
                name="attend",
            )(flags, patch_order, q, kv, kv_other, cache_own, cache_peer)
            heads = everyone(mixed)
            last = t == 1
            results = pl.pallas_call(
                functools.partial(update_kernel, seq, last),
                out_shape=(shaped(PACK, LANES),) + (() if last else (shaped(seq, PACK + MODS, LANES),)),
                in_specs=[SMEM, VMEM, ANY, ANY, VMEM, VMEM] + ([] if last else [VMEM]),
                out_specs=(VMEM,) if last else (VMEM, VMEM),
                scratch_shapes=[
                    pltpu.VMEM(o_own.shape, BF16),
                    pltpu.VMEM((HALF, 2 * LANES), F32),
                    pltpu.SemaphoreType.DMA,
                ],
                compiler_params=params(),
                name="update",
            )(flags, heads, o_own, o_peer, x, mods[t], *([] if last else [mods[1]]))
            x = results[0]
            spread = None if last else results[1]
            kept.append((x, kv, kv_other))
        (x0, kv0, other0), (x1, kv1, other1) = kept
        first = core == 0
        return (
            x1,
            jnp.where(first, x0, x1),
            jnp.where(first, x1, x0),
            jnp.where(first, kv0, kv1),
            jnp.where(first, other0, other1),
        )

    def rest(state):
        return state

    pair = shaped(2, HALF, HEAD_DIM)
    blank = [jnp.zeros(s.shape, s.dtype) for s in (shaped(PACK, LANES), shaped(PACK, LANES), pair, pair)]
    state = lax.cond(second == 0, lambda s: run(s[0]), rest, (entering, *blank))
    arrived = lax.ppermute(state[0], "section", hop_pairs)
    state = lax.cond(second == 1, lambda s: run(s[0]), rest, (arrived, *state[1:]))
    _, mine, theirs, kv, kv_other = state
    other = swap(theirs)
    out_t, cache = pl.pallas_call(
        finish_kernel,
        out_shape=(shaped(SHARD, PATCHES * ROWS), shaped(2, PATCHES * ROWS, HEAD_DIM)),
        in_specs=[SMEM, SMEM, VMEM, VMEM, VMEM, VMEM],
        out_specs=(VMEM, VMEM),
        scratch_shapes=[pltpu.VMEM((PATCHES * ROWS, 2 * LANES), F32)],
        compiler_params=params(),
        name="finish",
    )(core[None], patch_order, mine, other, kv, kv_other)
    return jnp.transpose(out_t, (1, 0))[None], cache[None]


def solution(mesh):
    return jax.shard_map(
        body,
        mesh=mesh,
        in_specs=(
            P("section", None, "seq"),
            P(),
            P(),
            P(None, "section", None, "seq"),
            P("section", None, None, "seq"),
            P("section", None, "seq"),
            P("section", None, None, "seq"),
        ),
        out_specs=(P("section", None, "seq"), P("section", None, None, "seq")),
        check_vma=False,
    )
```

time: 1550 us -> 359 us (0.23)
  the two profiles are of different devices: /device:TPU:32 before, /device:TPU:97 now
where the time goes in v1:
time: 359 us; the launch traced here: 358 us
  waiting for transfers between devices  278 us (77%)
  starting transfers between devices  45.9 us (13%)
  Pallas kernels  21 us (6%)
  local copies, waits for them, and re-layouts  7.97 us (2%)
  other arithmetic  3.75 us (1%)
    ppermute x1, waiting for transfers between devices, body(): arrived = lax.ppermute(state[0], 'section', hop_pairs)  175 us
    all_to_all x4, waiting for transfers between devices, everyone(): return lax.all_to_all(spread, 'seq', 0, 0)  94.6 us
    ppermute x7, starting transfers between devices, swap(): return lax.ppermute(value, 'section', swap_pairs)  27.2 us
    all_to_all x4, starting transfers between devices, everyone(): return lax.all_to_all(spread, 'seq', 0, 0)  17.4 us
    pallas_call x2, Pallas kernels, run(): pl.pallas_call(functools.partial(project_kernel, seq), out_shape=(shaped(...  8.58 us
    ppermute x7, waiting for transfers between devices, swap(): return lax.ppermute(value, 'section', swap_pairs)  8.35 us
  transfers between devices with their start and end apart: 12, of which 11 were waited for; matrix products, arithmetic and copies ran while one was open for 1% of the time, Pallas kernels for 1%

profile of v1, /device:TPU:97, one launch (start us, length us, event | category | flops | bytes accessed | tf_op | source)
XLA Modules:
  0.0 358.1 jit_solution(14970786404909110608)
XLA Ops:
  3.4 2.6 collective-permute-start.10
  7.6 1.4 conditional.2
  10.2 1.3 collective-permute-start.11
  11.5 174.9 %collective-permute-done.11 = bf16[384,128]{1,0:T(8,128)(2,1)S(1)} collective-permute-done((bf16[384,128]{1,0:T(8,128)(2,1)}, bf16[384,128]{1,0:T(8,128)(2,1)S(1)}, u32[]{:S(2)}, u32[]{:S(2)}) %collective-permute-start.11) | collective-permute-done | bytes 98336 | tf_op jit(solution)/shard_map/ppermute | solution.py:342
  186.4 165.2 %conditional.3 = ((bf16[384,128]{1,0:T(8,128)(2,1)}, bf16[384,128]{1,0:T(8,128)(2,1)}, bf16[2,256,128]{2,1,0:T(8,128)(2,1)}, bf16[2,256,128]{2,1,0:T(8,128)(2,1)})) conditional(s32[]{:T(128)} %convert_element_type.6, (bf16[384,128]{1,0:T(8,128)(2,1)}, bf16[384,128]{1,0:T(8,128)(2,1)}, bf16[2,256,128]{2,1,0:T(8,128)(2,1)}, ...), branch_computations={%region_2.3_spmd, %region_3.4_spmd} | conditional | flops 233480 | bytes 52839348 | solution.py:343
  186.4 1.4 spread.3
  187.8 4.9 %all-to-all-start.4 = ((bf16[16,400,128]{2,1,0:T(8,128)(2,1)}), bf16[16,400,128]{2,1,0:T(8,128)(2,1)}, u32[]{:S(2)}, u32[]{:S(2)}) async-start(bf16[16,400,128]{2,1,0:T(8,128)(2,1)} %spread.3), calls=%async_computation.4 | async-start | bytes 3276800 | tf_op jit(solution)/shard_map/cond/branch_1_fun/all_to_all | solution.py:239
  192.7 4.0 %collective-permute-start.5 = (bf16[3,3072,128]{2,1,0:T(8,128)(2,1)}, bf16[3,3072,128]{2,1,0:T(8,128)(2,1)S(1)}, u32[]{:S(2)}, u32[]{:S(2)}) collective-permute-start(bf16[3,3072,128]{2,1,0:T(8,128)(2,1)} %get-tuple-element.60), channel_id=1, source_target_pairs={{0,16},{16,0},{32,48},{48,32},{64,80},{80,64},{96,112},{112,96},{1... | collective-permute-start | bytes 7077896 | tf_op jit(solution)/shard_map/cond/branch_1_fun/ppermute | solution.py:236
  196.7 1.9 collective-permute-start.7
  198.7 2.3 collective-permute-done.5
  201.1 22.6 %all-to-all-done.4.x_ref = bf16[16,400,128]{2,1,0:T(8,128)(2,1)} async-done(((bf16[16,400,128]{2,1,0:T(8,128)(2,1)}), bf16[16,400,128]{2,1,0:T(8,128)(2,1)}, u32[]{:S(2)}, u32[]{:S(2)}) %all-to-all-start.4) | async-done | bytes 1638432 | tf_op jit(solution)/shard_map/cond/branch_1_fun/all_to_all | solution.py:239
  223.7 4.5 %project.6 = (bf16[256,128]{1,0:T(8,128)(2,1)S(1)}, bf16[2,256,128]{2,1,0:T(8,128)(2,1)S(1)}) custom-call(s32[2]{0:T(128)S(1)} %pad_add_fusion.2.flag_ref, bf16[16,400,128]{2,1,0:T(8,128)(2,1)} %all-to-all-done.4.x_ref, bf16[3,16,192,128]{3,2,1,0:T(8,128)(2,1)} %bitcast.42, bf16[3,16,192,128]{3,2,1,0:T(8,128)(2,1)S(1)} %bitcast.34), custom_call_target="tpu_custom_call" | custom-call | tf_op jit(solution)/shard_map/cond/branch_1_fun/project/pallas_call | solution.py:279
  228.2 6.4 %collective-permute-start.6 = (bf16[2,256,128]{2,1,0:T(8,128)(2,1)S(1)}, bf16[2,256,128]{2,1,0:T(8,128)(2,1)S(1)}, u32[]{:S(2)}, u32[]{:S(2)}) collective-permute-start(bf16[2,256,128]{2,1,0:T(8,128)(2,1)S(1)} %get-tuple-element.62.kv_ref), channel_id=1, source_target_pairs={{0,16},{16,0},{32,48},{48,32},{64,80},{80,64},{96,112},{112,96},{1... | collective-permute-start | bytes 393224 | tf_op jit(solution)/shard_map/cond/branch_1_fun/ppermute | solution.py:236
  235.6 2.0 attend.6
  239.3 4.3 %all-to-all-start.5 = ((bf16[16,256,128]{2,1,0:T(8,128)(2,1)}), bf16[16,256,128]{2,1,0:T(8,128)(2,1)}, u32[]{:S(2)}, u32[]{:S(2)}) async-start(bf16[16,256,128]{2,1,0:T(8,128)(2,1)} %copy-done.2), calls=%async_computation.5 | async-start | bytes 2097152 | tf_op jit(solution)/shard_map/cond/branch_1_fun/all_to_all | solution.py:239
  243.6 2.3 collective-permute-start.8
  245.9 2.1 collective-permute-done.8.peer_ref
  248.0 19.3 %all-to-all-done.5.mixed_ref = bf16[16,256,128]{2,1,0:T(8,128)(2,1)} async-done(((bf16[16,256,128]{2,1,0:T(8,128)(2,1)}), bf16[16,256,128]{2,1,0:T(8,128)(2,1)}, u32[]{:S(2)}, u32[]{:S(2)}) %all-to-all-start.5) | async-done | bytes 1048608 | tf_op jit(solution)/shard_map/cond/branch_1_fun/all_to_all | solution.py:239
  267.3 1.9 update.6
  269.3 1.2 copy-done.4
  271.1 4.4 %all-to-all-start.6 = ((bf16[16,400,128]{2,1,0:T(8,128)(2,1)}), bf16[16,400,128]{2,1,0:T(8,128)(2,1)}, u32[]{:S(2)}, u32[]{:S(2)}) async-start(bf16[16,400,128]{2,1,0:T(8,128)(2,1)} %copy-done.4), calls=%async_computation.6 | async-start | bytes 3276800 | tf_op jit(solution)/shard_map/cond/branch_1_fun/all_to_all | solution.py:239
  275.6 31.3 %all-to-all-done.6.x_ref = bf16[16,400,128]{2,1,0:T(8,128)(2,1)} async-done(((bf16[16,400,128]{2,1,0:T(8,128)(2,1)}), bf16[16,400,128]{2,1,0:T(8,128)(2,1)}, u32[]{:S(2)}, u32[]{:S(2)}) %all-to-all-start.6) | async-done | bytes 1638432 | tf_op jit(solution)/shard_map/cond/branch_1_fun/all_to_all | solution.py:239
  306.8 4.1 %project.7 = (bf16[256,128]{1,0:T(8,128)(2,1)S(1)}, bf16[2,256,128]{2,1,0:T(8,128)(2,1)S(1)}) custom-call(s32[2]{0:T(128)S(1)} %pad_add_fusion.3.flag_ref, bf16[16,400,128]{2,1,0:T(8,128)(2,1)} %all-to-all-done.6.x_ref, bf16[3,16,192,128]{3,2,1,0:T(8,128)(2,1)} %bitcast.43, bf16[3,16,192,128]{3,2,1,0:T(8,128)(2,1)S(1)} %bitcast.35), custom_call_target="tpu_custom_call" | custom-call | tf_op jit(solution)/shard_map/cond/branch_1_fun/project/pallas_call | solution.py:279
  311.0 6.6 %collective-permute-start.9 = (bf16[2,256,128]{2,1,0:T(8,128)(2,1)S(1)}, bf16[2,256,128]{2,1,0:T(8,128)(2,1)S(1)}, u32[]{:S(2)}, u32[]{:S(2)}) collective-permute-start(bf16[2,256,128]{2,1,0:T(8,128)(2,1)S(1)} %get-tuple-element.68.kv_ref), channel_id=1, source_target_pairs={{0,16},{16,0},{32,48},{48,32},{64,80},{80,64},{96,112},{112,96},{1... | collective-permute-start | bytes 393224 | tf_op jit(solution)/shard_map/cond/branch_1_fun/ppermute | solution.py:236
  318.5 3.0 attend.7
  322.2 3.8 %all-to-all-start.7 = ((bf16[16,256,128]{2,1,0:T(8,128)(2,1)}), bf16[16,256,128]{2,1,0:T(8,128)(2,1)S(1)}, u32[]{:S(2)}, u32[]{:S(2)}) async-start(bf16[16,256,128]{2,1,0:T(8,128)(2,1)} %attend.7), calls=%async_computation.7 | async-start | bytes 2097152 | tf_op jit(solution)/shard_map/cond/branch_1_fun/all_to_all | solution.py:239
  326.0 1.6 broadcast_select_fusion.7
  328.3 21.4 %all-to-all-done.7.mixed_ref = bf16[16,256,128]{2,1,0:T(8,128)(2,1)S(1)} async-done(((bf16[16,256,128]{2,1,0:T(8,128)(2,1)}), bf16[16,256,128]{2,1,0:T(8,128)(2,1)S(1)}, u32[]{:S(2)}, u32[]{:S(2)}) %all-to-all-start.7) | async-done | bytes 1048608 | tf_op jit(solution)/shard_map/cond/branch_1_fun/all_to_all | solution.py:239
  349.7 1.2 update.7
  351.6 3.4 collective-permute-start.12
  355.1 1.1 collective-permute-done.12.other_ref
  356.2 1.9 finish.1
  (54 shorter events, 12.6 us)
Async XLA Ops:
  0.6 0.9 copy-start
  1.6 0.9 copy-start.19
  3.4 3.5 collective-permute-start.10
  9.0 0.6 copy-start.27
  9.6 0.6 copy-start.28
  10.2 176.2 %collective-permute-start.11 = (bf16[384,128]{1,0:T(8,128)(2,1)}, bf16[384,128]{1,0:T(8,128)(2,1)S(1)}, u32[]{:S(2)}, u32[]{:S(2)}) collective-permute-start(bf16[384,128]{1,0:T(8,128)(2,1)} %get-tuple-element.90), channel_id=1, source_target_pairs={{0,32},{16,48},{64,96},{80,112},{128,160},{144,176},{192,224},{208... | collective-permute-start | bytes 294920 | tf_op jit(solution)/shard_map/ppermute | solution.py:342
  186.4 1.4 copy-start.26
  187.8 8.9 %copy-start.24 = (bf16[2,512,128]{2,1,0:T(8,128)(2,1)S(1)}, bf16[2,512,128]{2,1,0:T(8,128)(2,1)}, u32[]{:S(2)}) copy-start(bf16[2,512,128]{2,1,0:T(8,128)(2,1)} %get-tuple-element.63.own_ref) | copy-start | bytes 786436 | tf_op jit(solution)/shard_map/cond
  187.8 35.9 %all-to-all-start.4 = ((bf16[16,400,128]{2,1,0:T(8,128)(2,1)}), bf16[16,400,128]{2,1,0:T(8,128)(2,1)}, u32[]{:S(2)}, u32[]{:S(2)}) async-start(bf16[16,400,128]{2,1,0:T(8,128)(2,1)} %spread.3), calls=%async_computation.4 | async-start | bytes 3276800 | tf_op jit(solution)/shard_map/cond/branch_1_fun/all_to_all | solution.py:239
  192.7 8.4 %collective-permute-start.5 = (bf16[3,3072,128]{2,1,0:T(8,128)(2,1)}, bf16[3,3072,128]{2,1,0:T(8,128)(2,1)S(1)}, u32[]{:S(2)}, u32[]{:S(2)}) collective-permute-start(bf16[3,3072,128]{2,1,0:T(8,128)(2,1)} %get-tuple-element.60), channel_id=1, source_target_pairs={{0,16},{16,0},{32,48},{48,32},{64,80},{80,64},{96,112},{112,96},{1... | collective-permute-start | bytes 7077896 | tf_op jit(solution)/shard_map/cond/branch_1_fun/ppermute | solution.py:236
  196.7 37.9 %collective-permute-start.7 = (bf16[2,512,128]{2,1,0:T(8,128)(2,1)S(1)}, bf16[2,512,128]{2,1,0:T(8,128)(2,1)S(1)}, u32[]{:S(2)}, u32[]{:S(2)}) collective-permute-start(bf16[2,512,128]{2,1,0:T(8,128)(2,1)S(1)} %copy-done.24), channel_id=1, source_target_pairs={{0,16},{16,0},{32,48},{48,32},{64,80},{80,64},{96,112},{112,96},{1... | collective-permute-start | bytes 786440 | tf_op jit(solution)/shard_map/cond/branch_1_fun/ppermute | solution.py:236
  223.7 11.9 %copy-start.30 = (s32[8]{0:T(128)S(1)}, s32[8]{0:T(128)}, u32[]{:S(2)}) copy-start(s32[8]{0:T(128)} %get-tuple-element.56.order_ref) | copy-start | bytes 100 | tf_op jit(solution)/shard_map/cond
  228.2 7.4 %collective-permute-start.6 = (bf16[2,256,128]{2,1,0:T(8,128)(2,1)S(1)}, bf16[2,256,128]{2,1,0:T(8,128)(2,1)S(1)}, u32[]{:S(2)}, u32[]{:S(2)}) collective-permute-start(bf16[2,256,128]{2,1,0:T(8,128)(2,1)S(1)} %get-tuple-element.62.kv_ref), channel_id=1, source_target_pairs={{0,16},{16,0},{32,48},{48,32},{64,80},{80,64},{96,112},{112,96},{1... | collective-permute-start | bytes 393224 | tf_op jit(solution)/shard_map/cond/branch_1_fun/ppermute | solution.py:236
  234.6 4.7 %copy-start.7 = (bf16[2,512,128]{2,1,0:T(8,128)(2,1)}, bf16[2,512,128]{2,1,0:T(8,128)(2,1)S(1)}, u32[]{:S(2)}) copy-start(bf16[2,512,128]{2,1,0:T(8,128)(2,1)S(1)} %collective-permute-done.7.peer_ref) | copy-start | bytes 786436 | tf_op jit(solution)/shard_map/cond
  237.6 1.0 copy-start.2
  238.6 0.7 copy-start.9
  239.3 28.1 %all-to-all-start.5 = ((bf16[16,256,128]{2,1,0:T(8,128)(2,1)}), bf16[16,256,128]{2,1,0:T(8,128)(2,1)}, u32[]{:S(2)}, u32[]{:S(2)}) async-start(bf16[16,256,128]{2,1,0:T(8,128)(2,1)} %copy-done.2), calls=%async_computation.5 | async-start | bytes 2097152 | tf_op jit(solution)/shard_map/cond/branch_1_fun/all_to_all | solution.py:239
  243.6 4.4 %collective-permute-start.8 = (bf16[192,2048]{1,0:T(8,128)(2,1)}, bf16[192,2048]{1,0:T(8,128)(2,1)S(1)}, u32[]{:S(2)}, u32[]{:S(2)}) collective-permute-start(bf16[192,2048]{1,0:T(8,128)(2,1)} %get-tuple-element.64.own_ref), channel_id=1, source_target_pairs={{0,16},{16,0},{32,48},{48,32},{64,80},{80,64},{96,112},{112,96},{1... | collective-permute-start | bytes 2359304 | tf_op jit(solution)/shard_map/cond/branch_1_fun/ppermute | solution.py:236
  269.3 1.2 copy-start.4
  270.4 0.6 copy-start.15
  271.1 35.8 %all-to-all-start.6 = ((bf16[16,400,128]{2,1,0:T(8,128)(2,1)}), bf16[16,400,128]{2,1,0:T(8,128)(2,1)}, u32[]{:S(2)}, u32[]{:S(2)}) async-start(bf16[16,400,128]{2,1,0:T(8,128)(2,1)} %copy-done.4), calls=%async_computation.6 | async-start | bytes 3276800 | tf_op jit(solution)/shard_map/cond/branch_1_fun/all_to_all | solution.py:239
  306.8 11.7 %copy-start.8 = (bf16[2,512,128]{2,1,0:T(8,128)(2,1)S(1)}, bf16[2,512,128]{2,1,0:T(8,128)(2,1)}, u32[]{:S(2)}) copy-start(bf16[2,512,128]{2,1,0:T(8,128)(2,1)} %copy-done.7) | copy-start | bytes 786436 | tf_op jit(solution)/shard_map/cond
  306.8 11.7 %copy-start.25 = (bf16[2,512,128]{2,1,0:T(8,128)(2,1)S(1)}, bf16[2,512,128]{2,1,0:T(8,128)(2,1)}, u32[]{:S(2)}) copy-start(bf16[2,512,128]{2,1,0:T(8,128)(2,1)} %get-tuple-element.63.own_ref) | copy-start | bytes 786436 | tf_op jit(solution)/shard_map/cond
  311.0 7.5 %collective-permute-start.9 = (bf16[2,256,128]{2,1,0:T(8,128)(2,1)S(1)}, bf16[2,256,128]{2,1,0:T(8,128)(2,1)S(1)}, u32[]{:S(2)}, u32[]{:S(2)}) collective-permute-start(bf16[2,256,128]{2,1,0:T(8,128)(2,1)S(1)} %get-tuple-element.68.kv_ref), channel_id=1, source_target_pairs={{0,16},{16,0},{32,48},{48,32},{64,80},{80,64},{96,112},{112,96},{1... | collective-permute-start | bytes 393224 | tf_op jit(solution)/shard_map/cond/branch_1_fun/ppermute | solution.py:236
  321.6 0.7 copy-start.13
  322.2 5.4 %copy-start.10 = (bf16[2,256,128]{2,1,0:T(8,128)(2,1)S(1)}, bf16[2,256,128]{2,1,0:T(8,128)(2,1)}, u32[]{:S(2)}) copy-start(bf16[2,256,128]{2,1,0:T(8,128)(2,1)} %copy-done.9) | copy-start | bytes 393220 | tf_op jit(solution)/shard_map/cond
  322.2 27.5 %copy-start.16 = (bf16[384,128]{1,0:T(8,128)(2,1)S(1)}, bf16[384,128]{1,0:T(8,128)(2,1)}, u32[]{:S(2)}) copy-start(bf16[384,128]{1,0:T(8,128)(2,1)} %copy-done.15) | copy-start | bytes 294916 | tf_op jit(solution)/shard_map/cond
  322.2 27.5 %copy-start.21 = (bf16[192,2048]{1,0:T(8,128)(2,1)S(1)}, bf16[192,2048]{1,0:T(8,128)(2,1)}, u32[]{:S(2)}) copy-start(bf16[192,2048]{1,0:T(8,128)(2,1)} %get-tuple-element.64.own_ref) | copy-start | bytes 2359300 | tf_op jit(solution)/shard_map/cond
  322.2 27.4 %all-to-all-start.7 = ((bf16[16,256,128]{2,1,0:T(8,128)(2,1)}), bf16[16,256,128]{2,1,0:T(8,128)(2,1)S(1)}, u32[]{:S(2)}, u32[]{:S(2)}) async-start(bf16[16,256,128]{2,1,0:T(8,128)(2,1)} %attend.7), calls=%async_computation.7 | async-start | bytes 2097152 | tf_op jit(solution)/shard_map/cond/branch_1_fun/all_to_all | solution.py:239
  351.6 4.6 %collective-permute-start.12 = (bf16[384,128]{1,0:T(8,128)(2,1)}, bf16[384,128]{1,0:T(8,128)(2,1)S(1)}, u32[]{:S(2)}, u32[]{:S(2)}) collective-permute-start(bf16[384,128]{1,0:T(8,128)(2,1)} %get-tuple-element.92), channel_id=1, source_target_pairs={{0,16},{16,0},{32,48},{48,32},{64,80},{80,64},{96,112},{112,96},{1... | collective-permute-start | bytes 294920 | tf_op jit(solution)/shard_map/ppermute | solution.py:236

commit v2 on v0

v2 whole, which is shorter than its diff:
```python
import jax
import jax.numpy as jnp
from jax import lax
from jax.experimental import pallas as pl
from jax.experimental.pallas import tpu as pltpu
from jax.sharding import PartitionSpec as P

HEAD_DIM = 128
PATCHES = 8
CHAIN = 4
EPSILON = 1e-06
ROWS = 64
ALL = PATCHES * ROWS
SIDE = 4
SEQ = SIDE * SIDE
LANES = 128
REST = 64
SHARD = LANES + REST
WIDTH = SEQ * SHARD
PACK = ALL + ALL // 2
MODS = 16
GROUP = PATCHES // SIDE
PART = GROUP * ROWS
WIDE = SIDE * SHARD
HEADS = SIDE * HEAD_DIM
SCALE = HEAD_DIM ** (-0.5)
F32 = jnp.float32
BF16 = jnp.bfloat16
VMEM = pl.BlockSpec(memory_space=pltpu.VMEM)
SMEM = pl.BlockSpec(memory_space=pltpu.SMEM)
ANY = pl.BlockSpec(memory_space=pl.ANY)
ALONG_X = [[SIDE * i + j for i in range(SIDE)] for j in range(SIDE)]
ALONG_Z = [[SIDE * i + j for j in range(SIDE)] for i in range(SIDE)]
TRANSPOSED = (((1,), (1,)), ((), ()))


def shaped(*shape, dtype=BF16):
    return jax.ShapeDtypeStruct(shape, dtype)


def call(kernel, name, out_shape, in_specs, *args, scratch=()):
    many = isinstance(out_shape, tuple)
    return pl.pallas_call(
        kernel,
        out_shape=out_shape,
        in_specs=in_specs,
        out_specs=(VMEM,) * len(out_shape) if many else VMEM,
        scratch_shapes=list(scratch),
        compiler_params=pltpu.CompilerParams(vmem_limit_bytes=32 * 1024 * 1024),
        name=name,
    )(*args)


def low_lanes(rows):
    return lax.broadcasted_iota(jnp.int32, (rows, LANES), 1) < REST


def patch_at(order_ref, j, base=0):
    return pl.ds(pl.multiple_of(base + order_ref[j] * ROWS, ROWS), ROWS)


def tile(k):
    return slice(k * LANES, (k + 1) * LANES)


def pair_lanes(low, even, odd):
    return jnp.where(low, even, pltpu.roll(odd, REST, 1))


def softmax_mix(q, keys, values):
    scores = lax.dot_general(q, keys, TRANSPOSED, preferred_element_type=F32) * SCALE
    terms = jnp.exp(scores - jnp.max(scores, axis=1, keepdims=True))
    weights = (terms / jnp.sum(terms, axis=1, keepdims=True)).astype(BF16)
    return jnp.dot(weights, values, preferred_element_type=F32).astype(BF16)


def pack_kernel(order_ref, lat_ref, mod_ref, out_ref, rows_ref):
    rows_ref[:, :SHARD] = lat_ref[...].astype(F32).T
    low = low_lanes(ROWS)
    rest = []
    for j in range(PATCHES):
        at = patch_at(order_ref, j)
        out_ref[j * ROWS : (j + 1) * ROWS, :] = rows_ref[at, :LANES].astype(BF16)
        rest.append(rows_ref[at, LANES:])
    half = PATCHES // 2
    for j in range(half):
        both = pair_lanes(low, rest[j], rest[j + half])
        out_ref[ALL + j * ROWS : ALL + (j + 1) * ROWS, :] = both.astype(BF16)
    mod = mod_ref[...]
    lines = []
    for kind in (1.0 + mod[1:2], mod[0:1], mod[2:3]):
        last = jnp.concatenate([kind[:, LANES:], kind[:, LANES:]], axis=1)
        for value in (kind[:, :LANES], last):
            high = value.astype(BF16).astype(F32)
            lines += [high, value - high]
    lines.append(jnp.zeros((MODS - len(lines), LANES), F32))
    out_ref[PACK:, :] = jnp.concatenate(lines, axis=0).astype(BF16)


def repeat_kernel(in_ref, out_ref):
    for s in range(SIDE):
        out_ref[s] = in_ref[...]


def project_whole_kernel(x_ref, w_ref, q_ref, kv_ref, wm_ref, wr_ref, nm_ref, nr_ref, sems):
    copies = []
    for t in range(3):
        lanes = pl.ds(t * HEAD_DIM, HEAD_DIM)
        copies.append(pltpu.make_async_copy(w_ref.at[t, :, :LANES, :], wm_ref.at[:, :, lanes], sems.at[2 * t]))
        copies.append(pltpu.make_async_copy(w_ref.at[t, :, LANES:, :], wr_ref.at[:, :, lanes], sems.at[2 * t + 1]))
    for copy in copies:
        copy.start()
    low = low_lanes(ROWS)

    def line(s, k):
        rows = x_ref[s, PACK:, :].astype(F32)
        return rows[2 * k : 2 * k + 1] + rows[2 * k + 1 : 2 * k + 2]

    scale_first = [line(s, 0) for s in range(SEQ)]
    shift_first = [line(s, 2) for s in range(SEQ)]
    scale_last = [jnp.where(low[:1], line(2 * p, 1), line(2 * p + 1, 1)) for p in range(SEQ // 2)]
    shift_last = [jnp.where(low[:1], line(2 * p, 3), line(2 * p + 1, 3)) for p in range(SEQ // 2)]
    half = PATCHES // 2
    for j in range(PATCHES):
        mine = pl.ds(j * ROWS, ROWS)
        rest = pl.ds(ALL + (j % half) * ROWS, ROWS)
        total, square, total_rest, square_rest = (jnp.zeros((ROWS, LANES), F32) for _ in range(4))
        for s in range(SEQ):
            x = x_ref[s, mine, :].astype(F32)
            total = total + x
            square = square + x * x
            x = x_ref[s, rest, :].astype(F32)
            total_rest = total_rest + x
            square_rest = square_rest + x * x
        in_half = low if j < half else jnp.logical_not(low)
        total = total + jnp.where(in_half, total_rest, 0.0)
        square = square + jnp.where(in_half, square_rest, 0.0)
        mean = jnp.sum(total, axis=1, keepdims=True) / WIDTH
        var = jnp.sum(square, axis=1, keepdims=True) / WIDTH - mean * mean
        rstd = lax.rsqrt(var + EPSILON)
        for s in range(SEQ):
            x = x_ref[s, mine, :].astype(F32)
            nm_ref[mine, tile(s)] = ((x - mean) * rstd * scale_first[s] + shift_first[s]).astype(BF16)
        for p in range(SEQ // 2):
            even = x_ref[2 * p, rest, :].astype(F32)
            odd = x_ref[2 * p + 1, rest, :].astype(F32)
            if j < half:
                x = pair_lanes(low, even, odd)
            else:
                x = jnp.where(low, pltpu.roll(even, REST, 1), odd)
            nr_ref[mine, tile(p)] = ((x - mean) * rstd * scale_last[p] + shift_last[p]).astype(BF16)
    for copy in copies:
        copy.wait()
    qkv = jnp.dot(nm_ref[...], wm_ref[...].reshape(SEQ * LANES, 3 * HEAD_DIM), preferred_element_type=F32)
    qkv = qkv + jnp.dot(nr_ref[...], wr_ref[...].reshape(SEQ * REST, 3 * HEAD_DIM), preferred_element_type=F32)
    qkv = qkv.astype(BF16)
    q_ref[...] = qkv[:, :HEAD_DIM]
    kv_ref[0] = qkv[:, HEAD_DIM : 2 * HEAD_DIM]
    kv_ref[1] = qkv[:, 2 * HEAD_DIM :]


def attend_whole_kernel(order_ref, q_ref, kv_ref, stale_ref, out_ref):
    stale = [[stale_ref[part, patch_at(order_ref, j), :] for j in range(PATCHES)] for part in range(2)]
    for j in range(PATCHES):
        at = slice(j * ROWS, (j + 1) * ROWS)
        keys, values = (
            jnp.concatenate([kv_ref[part, : (j + 1) * ROWS, :]] + stale[part][j + 1 :], axis=0) for part in range(2)
        )
        mixed = softmax_mix(q_ref[at, :], keys, values)
        for s in range(SIDE):
            out_ref[s, at, :] = mixed


def update_whole_kernel(mixed_ref, w_ref, x_ref, out_ref, held_ref):
    mixed = jnp.concatenate([mixed_ref[h // SIDE, h % SIDE] for h in range(SEQ)], axis=1)
    held_ref[:, :SHARD] = lax.dot_general(mixed, w_ref[...], TRANSPOSED, preferred_element_type=F32)
    mods = x_ref[PACK:, :].astype(F32)
    gate_first = mods[8:9] + mods[9:10]
    gate_last = mods[10:11] + mods[11:12]
    half = ALL // 2
    for i in range(SIDE):
        at = slice(i * PART, (i + 1) * PART)
        out_ref[i, :, :LANES] = (x_ref[at, :].astype(F32) + gate_first * held_ref[at, :LANES]).astype(BF16)
        rest = x_ref[ALL + (i * PART) % half : ALL + (i * PART) % half + PART, :].astype(F32)
        if i >= SIDE // 2:
            rest = pltpu.roll(rest, REST, 1)
        rest = rest + gate_last * held_ref[at, LANES:]
        out_ref[i, :, LANES:] = jnp.where(low_lanes(PART), rest, 0.0).astype(BF16)


def join_kernel(in_ref, out_ref):
    low = low_lanes(PART)
    for i in range(SIDE):
        out_ref[:, tile(i)] = in_ref[i, :, :LANES]
    for m in range(SIDE // 2):
        even, odd = (in_ref[2 * m + k, :, LANES:].astype(F32) for k in range(2))
        out_ref[:, tile(SIDE + m)] = pair_lanes(low, even, odd).astype(BF16)


def part_kernel(in_ref, out_ref):
    low = low_lanes(PART)
    for i in range(SIDE):
        rest = in_ref[:, tile(SIDE + i // 2)].astype(F32)
        if i % 2:
            rest = pltpu.roll(rest, REST, 1)
        out_ref[i, :, :LANES] = in_ref[:, tile(i)]
        out_ref[i, :, LANES:] = jnp.where(low, rest, 0.0).astype(BF16)


def mods_kernel(gathered_ref, out_ref):
    low = low_lanes(1)
    rows = [gathered_ref[i, 2 * ALL :, :].astype(F32) for i in range(SIDE)]
    lines = []
    for k in range(3):
        for h in range(2):
            first, last = 4 * k + h, 4 * k + 2 + h
            parts = [rows[i][first : first + 1] for i in range(SIDE)]
            for m in range(SIDE // 2):
                even, odd = (rows[2 * m + e][last : last + 1] for e in range(2))
                parts.append(jnp.where(low, even, odd))
            lines.append(jnp.concatenate(parts, axis=1))
    lines.append(jnp.zeros((MODS - len(lines), WIDE), F32))
    out_ref[...] = jnp.concatenate(lines, axis=0).astype(BF16)


def spread_kernel(x_ref, mods_ref, out_ref):
    for s in range(SIDE):
        out_ref[s, :PART, :] = x_ref[...]
        out_ref[s, PART:, :] = mods_ref[...]


def project_kernel(x_ref, w_ref, q_ref, kv_ref, wm_ref, wr_ref, nm_ref, nr_ref, sems):
    copies = []
    for t in range(3):
        for h in range(SIDE):
            lanes = pl.ds((t * SIDE + h) * HEAD_DIM, HEAD_DIM)
            pairs = [(w_ref.at[h, t, :, :, :LANES, :], wm_ref.at[:, :, :, lanes])]
            pairs += [(w_ref.at[h, t, :, j, LANES:, :], wr_ref.at[j, :, :, lanes]) for j in range(SIDE)]
            copies += [pltpu.make_async_copy(a, b, sems.at[len(copies) + n]) for n, (a, b) in enumerate(pairs)]
    for copy in copies:
        copy.start()
    mods = [x_ref[j, PART:, :].astype(F32) for j in range(SIDE)]
    scale = [m[0:1] + m[1:2] for m in mods]
    shift = [m[2:3] + m[3:4] for m in mods]
    tiles = WIDE // LANES
    for g in range(GROUP):
        mine = pl.ds(g * ROWS, ROWS)
        total, square = (jnp.zeros((ROWS, LANES), F32) for _ in range(2))
        for j in range(SIDE):
            for k in range(tiles):
                x = x_ref[j, mine, tile(k)].astype(F32)
                total = total + x
                square = square + x * x
        mean = jnp.sum(total, axis=1, keepdims=True) / WIDTH
        var = jnp.sum(square, axis=1, keepdims=True) / WIDTH - mean * mean
        rstd = lax.rsqrt(var + EPSILON)
        for j in range(SIDE):
            for k in range(tiles):
                x = x_ref[j, mine, tile(k)].astype(F32)
                normed = ((x - mean) * rstd * scale[j][:, tile(k)] + shift[j][:, tile(k)]).astype(BF16)
                if k < SIDE:
                    nm_ref[mine, tile(k * SIDE + j)] = normed
                else:
                    nr_ref[mine, tile(j * (SIDE // 2) + k - SIDE)] = normed
    each = len(copies) // 3
    for t in range(3):
        for copy in copies[t * each : (t + 1) * each]:
            copy.wait()
        lanes = slice(t * HEADS, (t + 1) * HEADS)
        part = jnp.dot(nm_ref[...], wm_ref[:, :, :, lanes].reshape(SEQ * LANES, HEADS), preferred_element_type=F32)
        part = part + jnp.dot(nr_ref[...], wr_ref[:, :, :, lanes].reshape(SEQ * REST, HEADS), preferred_element_type=F32)
        part = part.astype(BF16)
        if t == 0:
            q_ref[...] = part
        else:
            for s in range(SIDE):
                kv_ref[s, :, (t - 1) * HEADS : t * HEADS] = part


def attend_kernel(row_ref, order_ref, q_ref, kv_ref, stale_ref, out_ref, own_ref):
    i = row_ref[0]
    for h in range(SIDE):
        new, old = [], []
        for part in range(2):
            lanes = tile(part * SIDE + h)
            new.append([kv_ref[n // GROUP, (n % GROUP) * ROWS : (n % GROUP + 1) * ROWS, lanes] for n in range(PATCHES)])
            old.append([stale_ref[h, patch_at(order_ref, n, part * ALL), :] for n in range(PATCHES)])
        for g in range(GROUP):
            at = slice(g * ROWS, (g + 1) * ROWS)
            keys, values = (
                jnp.concatenate(
                    [jnp.where(n <= GROUP * i + g, new[part][n], old[part][n]) for n in range(PATCHES)], axis=0
                )
                for part in range(2)
            )
            mixed = softmax_mix(q_ref[at, tile(h)], keys, values)
            for s in range(SIDE):
                out_ref[s, at, tile(h)] = mixed
    for part in range(2):
        lanes = pl.ds(pl.multiple_of(part * HEADS + i * HEAD_DIM, HEAD_DIM), HEAD_DIM)
        for n in range(SIDE):
            own_ref[part, n * PART : (n + 1) * PART, :] = kv_ref[n, :, lanes]


def update_kernel(mixed_ref, w_ref, x_ref, mods_ref, out_ref, held_ref, sems):
    copies = []
    for i in range(SIDE):
        first = held_ref.at[i * LANES : (i + 1) * LANES, :]
        last = held_ref.at[SIDE * LANES + i * REST : SIDE * LANES + (i + 1) * REST, :]
        copies.append(pltpu.make_async_copy(w_ref.at[i, :LANES, :], first, sems.at[2 * i]))
        copies.append(pltpu.make_async_copy(w_ref.at[i, LANES:, :], last, sems.at[2 * i + 1]))
    for copy in copies:
        copy.start()
    mixed = jnp.concatenate([mixed_ref[h % SIDE, :, tile(h // SIDE)] for h in range(SEQ)], axis=1)
    for copy in copies:
        copy.wait()
    made = lax.dot_general(mixed, held_ref[...], TRANSPOSED, preferred_element_type=F32)
    mods = mods_ref[...].astype(F32)
    out_ref[...] = (x_ref[...].astype(F32) + (mods[4:5] + mods[5:6]) * made).astype(BF16)


def finish_kernel(order_ref, x_ref, kv_ref, out_ref, cache_ref, rows_ref):
    for j in range(PATCHES):
        at = patch_at(order_ref, j)
        rows_ref[at, :] = x_ref[j // GROUP, (j % GROUP) * ROWS : (j % GROUP + 1) * ROWS, :].astype(F32)
        for part in range(2):
            cache_ref[part, at, :] = kv_ref[part, j * ROWS : (j + 1) * ROWS, :]
    out_ref[...] = rows_ref[...].T[:SHARD, :].astype(BF16)


def blank(*shapes):
    return pl.pallas_call(lambda *refs: None, out_shape=shapes, out_specs=(ANY,) * len(shapes), name="blank")()


def body(latents, patch_order, timestep, mod_table, w_qkv, w_out, kv_cache):
    sections = lax.axis_size("section")
    position = lax.axis_index("section") % CHAIN
    row = (lax.axis_index("seq") // SIDE).astype(jnp.int32)[None]
    w_own = jnp.transpose(w_qkv[0], (1, 0, 2))
    o_own = jnp.transpose(w_out[0], (1, 0))
    cache_own = kv_cache[0]
    mod_now = lax.dynamic_index_in_dim(mod_table, timestep[0], 0, keepdims=False)[0]

    def exchange(value, groups):
        return lax.all_to_all(value, "seq", 0, 0, axis_index_groups=groups)

    def gather(value, groups):
        return exchange(jnp.broadcast_to(value[None], (SIDE,) + value.shape), groups)

    packed = call(
        pack_kernel,
        "pack",
        shaped(PACK + MODS, LANES),
        [SMEM, VMEM, VMEM],
        patch_order,
        jnp.transpose(latents[0], (1, 0)),
        mod_now,
        scratch=[pltpu.VMEM((ALL, 2 * LANES), F32)],
    )
    rows_shape, kv_shape, x_shape = shaped(SIDE, PART, 2 * LANES), shaped(2, ALL, HEAD_DIM), shaped(PART, WIDE)

    def first_block(packed):
        gathered = gather(gather(packed, ALONG_Z), ALONG_X).reshape(SEQ, PACK + MODS, LANES)
        q, kv = call(
            project_whole_kernel,
            "project_whole",
            (shaped(ALL, HEAD_DIM), kv_shape),
            [VMEM, ANY],
            gathered,
            w_own.reshape(3, SEQ, SHARD, HEAD_DIM),
            scratch=[
                pltpu.VMEM((SEQ, LANES, 3 * HEAD_DIM), BF16),
                pltpu.VMEM((SEQ, REST, 3 * HEAD_DIM), BF16),
                pltpu.VMEM((ALL, SEQ * LANES), BF16),
                pltpu.VMEM((ALL, SEQ * REST), BF16),
                pltpu.SemaphoreType.DMA((6,)),
            ],
        )
        mixed = call(
            attend_whole_kernel,
            "attend_whole",
            shaped(SIDE, ALL, HEAD_DIM),
            [SMEM, VMEM, VMEM, VMEM],
            patch_order,
            q,
            kv,
            cache_own,
        )
        heads = gather(exchange(mixed, ALONG_Z), ALONG_X)
        rows = call(
            update_whole_kernel,
            "update_whole",
            rows_shape,
            [VMEM, VMEM, VMEM],
            heads,
            o_own,
            packed,
            scratch=[pltpu.VMEM((ALL, 2 * LANES), F32)],
        )
        x = call(join_kernel, "join", x_shape, [VMEM], exchange(rows, ALONG_X))
        return x, rows, kv

    def prepare(packed):
        w = gather(w_own, ALONG_X).reshape(SIDE, 3, SIDE, SIDE, SHARD, HEAD_DIM)
        o = gather(o_own, ALONG_X)
        small = jnp.concatenate([cache_own.reshape(2 * ALL, HEAD_DIM), packed[PACK:]], axis=0)
        small = gather(small, ALONG_X)
        mods = call(mods_kernel, "mods", shaped(MODS, WIDE), [VMEM], small)
        return w, o, small, mods

    def later_block(x, w, o, small, mods):
        spread = call(spread_kernel, "spread", shaped(SIDE, PART + MODS, WIDE), [VMEM, VMEM], x, mods)
        q, kv = call(
            project_kernel,
            "project",
            (shaped(PART, HEADS), shaped(SIDE, PART, 2 * HEADS)),
            [VMEM, ANY],
            exchange(spread, ALONG_Z),
            w,
            scratch=[
                pltpu.VMEM((SIDE, SIDE, LANES, 3 * HEADS), BF16),
                pltpu.VMEM((SIDE, SIDE, REST, 3 * HEADS), BF16),
                pltpu.VMEM((PART, SEQ * LANES), BF16),
                pltpu.VMEM((PART, SEQ * REST), BF16),
                pltpu.SemaphoreType.DMA((60,)),
            ],
        )
        mixed, kv_own = call(
            attend_kernel,
            "attend",
            (shaped(SIDE, PART, HEADS), kv_shape),
            [SMEM, SMEM, VMEM, VMEM, VMEM],
            row,
            patch_order,
            q,
            exchange(kv, ALONG_X),
            small,
        )
        new = call(
            update_kernel,
            "update",
            x_shape,
            [VMEM, ANY, VMEM, VMEM],
            exchange(mixed, ALONG_Z),
            o,
            x,
            mods,
            scratch=[pltpu.VMEM((WIDE, SEQ * HEAD_DIM), BF16), pltpu.SemaphoreType.DMA((2 * SIDE,))],
        )
        return new, kv_own

    def nothing_yet(packed):
        return tuple(jnp.zeros(s.shape, s.dtype) for s in (x_shape, rows_shape, kv_shape))

    def no_weights(packed):
        return blank(
            shaped(SIDE, 3, SIDE, SIDE, SHARD, HEAD_DIM),
            shaped(SIDE, SHARD, SEQ * HEAD_DIM),
            shaped(SIDE, 2 * ALL + MODS, LANES),
            shaped(MODS, WIDE),
        )

    x, rows, kv = lax.cond(position == 0, first_block, nothing_yet, packed)
    weights = lax.cond(position > 0, prepare, no_weights, packed)
    (x, weights) = lax.optimization_barrier((x, weights))
    for p in range(1, CHAIN):
        pairs = [(s, s + 1) for s in range(sections) if s % CHAIN == p - 1]
        arrived = lax.ppermute(x, "section", pairs)
        x, kv = lax.cond(
            position == p,
            lambda arrived, x, kv, *weights: later_block(arrived, *weights),
            lambda arrived, x, kv, *weights: (x, kv),
            arrived,
            x,
            kv,
            *weights,
        )
    rows = lax.cond(
        position > 0,
        lambda x, rows: exchange(call(part_kernel, "part", rows_shape, [VMEM], x), ALONG_X),
        lambda x, rows: rows,
        x,
        rows,
    )
    out_t, cache = call(
        finish_kernel,
        "finish",
        (shaped(SHARD, ALL), kv_shape),
        [SMEM, VMEM, VMEM],
        patch_order,
        rows,
        kv,
        scratch=[pltpu.VMEM((ALL, 2 * LANES), F32)],
    )
    return jnp.transpose(out_t, (1, 0))[None], cache[None]


def solution(mesh):
    return jax.shard_map(
        body,
        mesh=mesh,
        in_specs=(
            P("section", None, "seq"),
            P(),
            P(),
            P(None, "section", None, "seq"),
            P("section", None, None, "seq"),
            P("section", None, "seq"),
            P("section", None, None, "seq"),
        ),
        out_specs=(P("section", None, "seq"), P("section", None, None, "seq")),
        check_vma=False,
    )
```

time: 1550 us -> 336 us (0.22)
  the two profiles are of different devices: /device:TPU:32 before, /device:TPU:65 now
where the time goes in v2:
time: 336 us; the launch traced here: 335 us
  waiting for transfers between devices  191 us (57%)
  blocking collectives  106 us (32%)
  Pallas kernels  17.5 us (5%)
  local copies, waits for them, and re-layouts  9.18 us (3%)
  starting transfers between devices  8.46 us (3%)
    all_to_all x6, blocking collectives, exchange(): return lax.all_to_all(value, 'seq', 0, 0, axis_index_groups=groups)  106 us
    all_to_all x1, waiting for transfers between devices, exchange(): return lax.all_to_all(value, 'seq', 0, 0, axis_index_groups=groups)  100 us
    ppermute x3, waiting for transfers between devices, body(): arrived = lax.ppermute(x, 'section', pairs)  90.6 us
    pallas_call x8, Pallas kernels, call(): pl.pallas_call(kernel, out_shape=out_shape, in_specs=in_specs, out_specs=...  17.5 us
  transfers between devices with their start and end apart: 4, of which 2 were waited for; matrix products, arithmetic and copies ran while one was open for 0% of the time, Pallas kernels for 1%

profile of v2, /device:TPU:65, one launch (start us, length us, event | category | flops | bytes accessed | tf_op | source)
XLA Modules:
  0.0 335.0 jit_solution(14200402519268655978)
XLA Ops:
  1.3 0.2 copy-done
  1.6 0.9 copy-done.1
  2.5 0.9 pack.1
  3.4 171.5 %conditional.7 = ((bf16[4,3,4,4,192,128]{5,4,3,2,1,0:T(8,128)(2,1)}, bf16[4,192,2048]{2,1,0:T(8,128)(2,1)S(1)}, bf16[4,1040,128]{2,1,0:T(8,128)(2,1)}, bf16[16,768]{1,0:T(8,128)(2,1)})) conditional(s32[]{:T(128)} %convert_element_type.16, () %tuple.60, (bf16[3,3072,128]{2,1,0:T(8,128)(2,1)}, bf16[192,2048]{1,0:T(8,128)(2,1)}, ...), branch_computations={%region_2.3_spmd, %region_3.4_spmd} | conditional | flops 532480 | bytes 66916480 | solution.py:464
  3.5 1.0 pad_maximum_fusion
  4.7 18.2 %all_to_all.77.gathered_ref = bf16[4,1040,128]{2,1,0:T(8,128)(2,1)} all-to-all(bf16[4,1040,128]{2,1,0:T(8,128)(2,1)S(1)} %broadcast_in_dim.26), channel_id=1, replica_groups={{0,4,8,12},{1,5,9,13},{2,6,10,14},{3,7,11,15},{16,20,24,28},{17,21,25,2..., dimensions={0} | all-to-all | bytes 2129920 | tf_op jit(solution)/shard_map/cond/branch_1_fun/all_to_all | solution.py:345
  22.9 0.4 broadcast_in_dim.25
  23.3 38.3 %all_to_all.78 = bf16[4,192,2048]{2,1,0:T(8,128)(2,1)S(1)} all-to-all(bf16[4,192,2048]{2,1,0:T(8,128)(2,1)S(1)} %broadcast_in_dim.25), channel_id=1, replica_groups={{0,4,8,12},{1,5,9,13},{2,6,10,14},{3,7,11,15},{16,20,24,28},{17,21,25,2..., dimensions={0} | all-to-all | bytes 6291456 | tf_op jit(solution)/shard_map/cond/branch_1_fun/all_to_all | solution.py:345
  61.6 5.3 %broadcast_in_dim.12 = bf16[4,3,3072,128]{3,2,1,0:T(8,128)(2,1)} broadcast(bf16[3,3072,128]{2,1,0:T(8,128)(2,1)S(1)} %copy-done.5), dimensions={1,2,3} | broadcast | bytes 11796480 | tf_op jit(solution)/shard_map/cond/branch_1_fun/broadcast_in_dim | solution.py:348
  66.9 5.8 %all-to-all-start.15 = ((bf16[4,3,3072,128]{3,2,1,0:T(8,128)(2,1)}), bf16[4,3,3072,128]{3,2,1,0:T(8,128)(2,1)}, u32[]{:S(2)}, u32[]{:S(2)}) async-start(bf16[4,3,3072,128]{3,2,1,0:T(8,128)(2,1)} %broadcast_in_dim.12), calls=%async_computation.15 | async-start | bytes 18874368 | tf_op jit(solution)/shard_map/cond/branch_1_fun/all_to_all | solution.py:345
  72.7 1.8 mods.1
  74.6 100.4 %all-to-all-done.15 = bf16[4,3,3072,128]{3,2,1,0:T(8,128)(2,1)} async-done(((bf16[4,3,3072,128]{3,2,1,0:T(8,128)(2,1)}), bf16[4,3,3072,128]{3,2,1,0:T(8,128)(2,1)}, u32[]{:S(2)}, u32[]{:S(2)}) %all-to-all-start.15) | async-done | bytes 9437216 | tf_op jit(solution)/shard_map/cond/branch_1_fun/all_to_all | solution.py:345
  175.0 2.2 conditional.6
  175.0 0.8 broadcast.15
  175.7 0.7 broadcast.16
  176.5 0.7 broadcast.14
  177.2 0.7 collective-permute-start
  178.1 0.7 collective-permute-start.1
  178.8 1.3 collective-permute-start.2
  180.1 90.6 %collective-permute-done.2 = bf16[128,768]{1,0:T(8,128)(2,1)S(1)} collective-permute-done((bf16[128,768]{1,0:T(8,128)(2,1)}, bf16[128,768]{1,0:T(8,128)(2,1)S(1)}, u32[]{:S(2)}, u32[]{:S(2)}) %collective-permute-start.2) | collective-permute-done | bytes 196640 | tf_op jit(solution)/shard_map/ppermute | solution.py:468
  270.7 52.8 %conditional.10 = ((bf16[2,512,128]{2,1,0:T(8,128)(2,1)}, bf16[128,768]{1,0:T(8,128)(2,1)})) conditional(s32[]{:T(128)} %convert_element_type.18, (bf16[2,512,128]{2,1,0:T(8,128)(2,1)}, bf16[128,768]{1,0:T(8,128)(2,1)}) %tuple.66, (bf16[128,768]{1,0:T(8,128)(2,1)S(1)}, bf16[16,768]{1,0:T(8,128)(2,1)}, bf16[4,3,4,4,192,128]{5,4,3,2,1,0:T(8,128)(2,1)}, ...), branch_computations={%region_8.9_spmd, %region_9.10_spmd} | conditional | bytes 10846344 | solution.py:469
  270.7 0.8 spread.5
  271.5 15.8 %all_to_all.85.x_ref = bf16[4,144,768]{2,1,0:T(8,128)(2,1)S(1)} all-to-all(bf16[4,144,768]{2,1,0:T(8,128)(2,1)S(1)} %spread.5), channel_id=1, replica_groups={{0,1,2,3},{4,5,6,7},{8,9,10,11},{12,13,14,15},{16,17,18,19},{20,21,22,2..., dimensions={0} | all-to-all | bytes 1769472 | tf_op jit(solution)/shard_map/cond/branch_1_fun/all_to_all | solution.py:345
  287.3 4.9 %project.5 = (bf16[128,512]{1,0:T(8,128)(2,1)S(1)}, bf16[4,128,1024]{2,1,0:T(8,128)(2,1)S(1)}) custom-call(bf16[4,144,768]{2,1,0:T(8,128)(2,1)S(1)} %all_to_all.85.x_ref, bf16[4,3,4,4,192,128]{5,4,3,2,1,0:T(8,128)(2,1)} %get-tuple-element.119.w_ref), custom_call_target="tpu_custom_call" | custom-call | tf_op jit(solution)/shard_map/cond/branch_1_fun/project/pallas_call | solution.py:43
  292.2 12.3 %all_to_all.86.kv_ref = bf16[4,128,1024]{2,1,0:T(8,128)(2,1)S(1)} all-to-all(bf16[4,128,1024]{2,1,0:T(8,128)(2,1)S(1)} %get-tuple-element.121), channel_id=1, replica_groups={{0,4,8,12},{1,5,9,13},{2,6,10,14},{3,7,11,15},{16,20,24,28},{17,21,25,2..., dimensions={0} | all-to-all | bytes 2097152 | tf_op jit(solution)/shard_map/cond/branch_1_fun/all_to_all | solution.py:345
  304.5 4.0 %attend.5 = (bf16[4,128,512]{2,1,0:T(8,128)(2,1)S(1)}, bf16[2,512,128]{2,1,0:T(8,128)(2,1)}) custom-call(s32[1]{0:T(128)} %get-tuple-element.115.row_ref, s32[8]{0:T(128)S(1)} %get-tuple-element.116.order_ref, bf16[128,512]{1,0:T(8,128)(2,1)S(1)} %get-tuple-element.120.q_ref, bf16[4,128,1024]{2,1,0:T(8,128)(2,1)S(1)} %all_to_all.86.kv_ref, ...), custom_call_target="tpu_custom_call" | custom-call | tf_op jit(solution)/shard_map/cond/branch_1_fun/attend/pallas_call | solution.py:43
  308.5 12.8 %all_to_all.87.mixed_ref = bf16[4,128,512]{2,1,0:T(8,128)(2,1)S(1)} all-to-all(bf16[4,128,512]{2,1,0:T(8,128)(2,1)S(1)} %get-tuple-element.124), channel_id=1, replica_groups={{0,1,2,3},{4,5,6,7},{8,9,10,11},{12,13,14,15},{16,17,18,19},{20,21,22,2..., dimensions={0} | all-to-all | bytes 1048576 | tf_op jit(solution)/shard_map/cond/branch_1_fun/all_to_all | solution.py:345
  321.3 2.2 update.5
  323.5 9.6 %conditional.11 = (bf16[4,128,256]{2,1,0:T(8,128)(2,1)}) conditional(s32[]{:T(128)} %convert_element_type.16, bf16[4,128,256]{2,1,0:T(8,128)(2,1)} %get-tuple-element.147, bf16[128,768]{1,0:T(8,128)(2,1)} %get-tuple-element.162), branch_computations={%region_10.11_spmd, %region_11.12_spmd} | conditional | bytes 524296 | solution.py:478
  323.5 1.0 part.1
  324.5 8.6 %all_to_all.88 = bf16[4,128,256]{2,1,0:T(8,128)(2,1)} all-to-all(bf16[4,128,256]{2,1,0:T(8,128)(2,1)S(1)} %part.1), channel_id=1, replica_groups={{0,4,8,12},{1,5,9,13},{2,6,10,14},{3,7,11,15},{16,20,24,28},{17,21,25,2..., dimensions={0} | all-to-all | bytes 524288 | tf_op jit(solution)/shard_map/cond/branch_1_fun/all_to_all | solution.py:345
  333.1 1.9 finish.1
  (24 shorter events, 0.4 us)
Async XLA Ops:
  0.6 0.9 copy-start
  1.6 0.9 copy-start.1
  3.4 171.6 %copy-start.19 = (s32[8]{0:T(128)S(1)}, s32[8]{0:T(128)}, u32[]{:S(2)}) copy-start(s32[8]{0:T(128)} %order_ref.3) | copy-start | bytes 100
  3.4 19.4 %copy-start.7 = (bf16[192,2048]{1,0:T(8,128)(2,1)S(1)}, bf16[192,2048]{1,0:T(8,128)(2,1)}, u32[]{:S(2)}) copy-start(bf16[192,2048]{1,0:T(8,128)(2,1)} %get-tuple-element.90) | copy-start | bytes 2359300 | tf_op jit(solution)/shard_map/cond
  23.3 38.3 %copy-start.5 = (bf16[3,3072,128]{2,1,0:T(8,128)(2,1)S(1)}, bf16[3,3072,128]{2,1,0:T(8,128)(2,1)}, u32[]{:S(2)}) copy-start(bf16[3,3072,128]{2,1,0:T(8,128)(2,1)} %get-tuple-element.89) | copy-start | bytes 7077892 | tf_op jit(solution)/shard_map/cond
  66.9 108.1 %all-to-all-start.15 = ((bf16[4,3,3072,128]{3,2,1,0:T(8,128)(2,1)}), bf16[4,3,3072,128]{3,2,1,0:T(8,128)(2,1)}, u32[]{:S(2)}, u32[]{:S(2)}) async-start(bf16[4,3,3072,128]{3,2,1,0:T(8,128)(2,1)} %broadcast_in_dim.12), calls=%async_computation.15 | async-start | bytes 18874368 | tf_op jit(solution)/shard_map/cond/branch_1_fun/all_to_all | solution.py:345
  177.2 0.7 collective-permute-start
  178.1 0.7 collective-permute-start.1
  178.8 91.9 %collective-permute-start.2 = (bf16[128,768]{1,0:T(8,128)(2,1)}, bf16[128,768]{1,0:T(8,128)(2,1)S(1)}, u32[]{:S(2)}, u32[]{:S(2)}) collective-permute-start(bf16[128,768]{1,0:T(8,128)(2,1)} %get-tuple-element.161), channel_id=1, source_target_pairs={{32,48},{96,112},{160,176},{224,240},{288,304},{352,368},{416,432}... | collective-permute-start | bytes 589832 | tf_op jit(solution)/shard_map/ppermute | solution.py:468
  270.7 16.6 %copy-start.15 = (bf16[128,768]{1,0:T(8,128)(2,1)}, bf16[128,768]{1,0:T(8,128)(2,1)S(1)}, u32[]{:S(2)}) copy-start(bf16[128,768]{1,0:T(8,128)(2,1)S(1)} %get-tuple-element.117.x_ref) | copy-start | bytes 589828 | tf_op jit(solution)/shard_map/cond
  287.3 17.2 %copy-start.4 = (bf16[4,1040,128]{2,1,0:T(8,128)(2,1)S(1)}, bf16[4,1040,128]{2,1,0:T(8,128)(2,1)}, u32[]{:S(2)}) copy-start(bf16[4,1040,128]{2,1,0:T(8,128)(2,1)} %get-tuple-element.122.stale_ref) | copy-start | bytes 3194884 | tf_op jit(solution)/shard_map/cond
  292.2 29.1 %copy-start.12 = (bf16[16,768]{1,0:T(8,128)(2,1)S(1)}, bf16[16,768]{1,0:T(8,128)(2,1)}, u32[]{:S(2)}) copy-start(bf16[16,768]{1,0:T(8,128)(2,1)} %get-tuple-element.118.mods_ref) | copy-start | bytes 73732 | tf_op jit(solution)/shard_map/cond
  292.2 29.1 %copy-start.16 = (bf16[128,768]{1,0:T(8,128)(2,1)S(1)}, bf16[128,768]{1,0:T(8,128)(2,1)}, u32[]{:S(2)}) copy-start(bf16[128,768]{1,0:T(8,128)(2,1)} %copy-done.15) | copy-start | bytes 589828 | tf_op jit(solution)/shard_map/cond

commit v3 on v2

v3 whole, which is shorter than its diff:
```python
import functools

import jax
import jax.numpy as jnp
from jax import lax
from jax.experimental import pallas as pl
from jax.experimental.pallas import tpu as pltpu
from jax.sharding import PartitionSpec as P

HEAD_DIM = 128
PATCHES = 8
CHAIN = 4
EPSILON = 1e-06
ROWS = 64
ALL = PATCHES * ROWS
SIDE = 4
SEQ = SIDE * SIDE
LANES = 128
REST = 64
SHARD = LANES + REST
WIDTH = SEQ * SHARD
HALF = ALL // 2
QUARTER = HALF // 2
PACK = HALF + QUARTER
MODS = 16
CACHE = PACK + MODS
GROUP = PATCHES // SIDE
PART = GROUP * ROWS
WIDE = SIDE * SHARD
HEADS = SIDE * HEAD_DIM
SCALE = HEAD_DIM ** (-0.5)
F32 = jnp.float32
BF16 = jnp.bfloat16
VMEM = pl.BlockSpec(memory_space=pltpu.VMEM)
SMEM = pl.BlockSpec(memory_space=pltpu.SMEM)
ANY = pl.BlockSpec(memory_space=pl.ANY)
ALONG_X = [[SIDE * i + j for i in range(SIDE)] for j in range(SIDE)]
ALONG_Z = [[SIDE * i + j for j in range(SIDE)] for i in range(SIDE)]
TRANSPOSED = (((1,), (1,)), ((), ()))


def shaped(*shape, dtype=BF16):
    return jax.ShapeDtypeStruct(shape, dtype)


def call(kernel, name, out_shape, in_specs, *args, scratch=(), mib=12):
    many = isinstance(out_shape, tuple)
    return pl.pallas_call(
        kernel,
        out_shape=out_shape,
        in_specs=in_specs,
        out_specs=(VMEM,) * len(out_shape) if many else VMEM,
        scratch_shapes=list(scratch),
        compiler_params=pltpu.CompilerParams(vmem_limit_bytes=mib * 1024 * 1024),
        name=name,
    )(*args)


def low_lanes(rows):
    return lax.broadcasted_iota(jnp.int32, (rows, LANES), 1) < REST


def patch_at(order_ref, j, base=0):
    return pl.ds(pl.multiple_of(base + order_ref[j] * ROWS, ROWS), ROWS)


def tile(k):
    return slice(k * LANES, (k + 1) * LANES)


def pair_lanes(low, even, odd):
    return jnp.where(low, even, pltpu.roll(odd, REST, 1))


def softmax_mix(queries, keys, values):
    scores = [
        lax.dot_general(q, k, TRANSPOSED, preferred_element_type=F32) * SCALE for q, k in zip(queries, keys, strict=True)
    ]
    tops = [jnp.max(x, axis=1, keepdims=True) for x in scores]
    terms = [jnp.exp(x - top) for x, top in zip(scores, tops, strict=True)]
    sums = [jnp.sum(x, axis=1, keepdims=True) for x in terms]
    weights = [(x * (1.0 / total)).astype(BF16) for x, total in zip(terms, sums, strict=True)]
    return [jnp.dot(w, v, preferred_element_type=F32).astype(BF16) for w, v in zip(weights, values, strict=True)]


def pack_kernel(order_ref, lat_ref, mod_ref, cache_ref, own_ref, send_ref, rows_ref):
    rows_ref[:, :SHARD] = lat_ref[...].astype(F32).T
    low = low_lanes(ROWS)
    for core, out_ref in ((0, own_ref), (1, send_ref)):
        rest = []
        for j in range(SIDE):
            at = patch_at(order_ref, core * SIDE + j)
            out_ref[j * ROWS : (j + 1) * ROWS, :] = rows_ref[at, :LANES].astype(BF16)
            rest.append(rows_ref[at, LANES:])
        for j in range(2):
            both = pair_lanes(low, rest[j], rest[j + 2])
            out_ref[HALF + j * ROWS : HALF + (j + 1) * ROWS, :] = both.astype(BF16)
    mod = mod_ref[...]
    lines = []
    for kind in (1.0 + mod[1:2], mod[0:1], mod[2:3]):
        last = jnp.concatenate([kind[:, LANES:], kind[:, LANES:]], axis=1)
        for value in (kind[:, :LANES], last):
            high = value.astype(BF16).astype(F32)
            lines += [high, value - high]
    lines.append(jnp.zeros((MODS - len(lines), LANES), F32))
    send_ref[PACK : PACK + MODS, :] = jnp.concatenate(lines, axis=0).astype(BF16)
    for part in range(2):
        send_ref[CACHE + part * ALL : CACHE + (part + 1) * ALL, :] = cache_ref[part]


def mods_of(flag_ref, t, send_ref, got_ref):
    return jnp.where(flag_ref[t] == 1, send_ref[PACK:CACHE, :], got_ref[PACK:CACHE, :])


def start_kernel(flag_ref, own_ref, send_ref, got_ref, x_ref, out_ref):
    x = jnp.where(flag_ref[2] == 0, own_ref[...], got_ref[:PACK, :])
    mods = mods_of(flag_ref, 0, send_ref, got_ref)
    x_ref[...] = x
    for s in range(SIDE):
        out_ref[s, :PACK, :] = x
        out_ref[s, PACK:, :] = mods


def place(flag_ref, s):
    return jnp.where(flag_ref[2] == 0, s, (s % SIDE) * SIDE + s // SIDE)


def project_half_kernel(t_now, flag_ref, x_ref, own_ref, peer_ref, q_ref, kv_ref, wm_ref, wr_ref, nm_ref, nr_ref, sems):
    def copies(w_ref):
        found = []
        for t in range(3):
            lanes = pl.ds(t * HEAD_DIM, HEAD_DIM)
            found.append(pltpu.make_async_copy(w_ref.at[t, :, :LANES, :], wm_ref.at[:, :, lanes], sems.at[2 * t]))
            found.append(pltpu.make_async_copy(w_ref.at[t, :, LANES:, :], wr_ref.at[:, :, lanes], sems.at[2 * t + 1]))
        return found

    @pl.when(flag_ref[t_now] == 1)
    def _():
        for copy in copies(own_ref):
            copy.start()

    @pl.when(flag_ref[t_now] == 0)
    def _():
        for copy in copies(peer_ref):
            copy.start()

    low = low_lanes(ROWS)
    at = [place(flag_ref, s) for s in range(SEQ)]

    def line(s, k):
        pair = x_ref[at[s], PACK:, :].astype(F32)
        return pair[2 * k : 2 * k + 1] + pair[2 * k + 1 : 2 * k + 2]

    scale_first = [line(s, 0) for s in range(SEQ)]
    shift_first = [line(s, 2) for s in range(SEQ)]
    scale_last = [jnp.where(low[:1], line(2 * p, 1), line(2 * p + 1, 1)) for p in range(SEQ // 2)]
    shift_last = [jnp.where(low[:1], line(2 * p, 3), line(2 * p + 1, 3)) for p in range(SEQ // 2)]
    for j in range(SIDE):
        mine = pl.ds(j * ROWS, ROWS)
        rest = pl.ds(HALF + (j % 2) * ROWS, ROWS)
        total = jnp.zeros((ROWS, LANES), F32)
        square = jnp.zeros((ROWS, LANES), F32)
        total_rest = jnp.zeros((ROWS, LANES), F32)
        square_rest = jnp.zeros((ROWS, LANES), F32)
        for s in range(SEQ):
            x = x_ref[at[s], mine, :].astype(F32)
            total = total + x
            square = square + x * x
            x = x_ref[at[s], rest, :].astype(F32)
            total_rest = total_rest + x
            square_rest = square_rest + x * x
        in_half = low if j < 2 else jnp.logical_not(low)
        total = total + jnp.where(in_half, total_rest, 0.0)
        square = square + jnp.where(in_half, square_rest, 0.0)
        mean = jnp.sum(total, axis=1, keepdims=True) / WIDTH
        var = jnp.sum(square, axis=1, keepdims=True) / WIDTH - mean * mean
        rstd = lax.rsqrt(var + EPSILON)
        for s in range(SEQ):
            x = x_ref[at[s], mine, :].astype(F32)
            normed = (x - mean) * rstd * scale_first[s] + shift_first[s]
            nm_ref[mine, tile(s)] = normed.astype(BF16)
        for p in range(SEQ // 2):
            even = x_ref[at[2 * p], rest, :].astype(F32)
            odd = x_ref[at[2 * p + 1], rest, :].astype(F32)
            if j < 2:
                x = pair_lanes(low, even, odd)
            else:
                x = jnp.where(low, pltpu.roll(even, REST, 1), odd)
            normed = (x - mean) * rstd * scale_last[p] + shift_last[p]
            nr_ref[mine, tile(p)] = normed.astype(BF16)

    for copy in copies(own_ref):
        copy.wait()
    w_first = wm_ref[...].reshape(SEQ * LANES, 3 * HEAD_DIM)
    w_last = wr_ref[...].reshape(SEQ * REST, 3 * HEAD_DIM)
    qkv = jnp.dot(nm_ref[...], w_first, preferred_element_type=F32)
    qkv = qkv + jnp.dot(nr_ref[...], w_last, preferred_element_type=F32)
    qkv = qkv.astype(BF16)
    q_ref[...] = qkv[:, :HEAD_DIM]
    kv_ref[0] = qkv[:, HEAD_DIM : 2 * HEAD_DIM]
    kv_ref[1] = qkv[:, 2 * HEAD_DIM :]


def attend_half_kernel(t, flag_ref, order_ref, q_ref, kv_ref, other_ref, own_ref, got_ref, out_ref):
    mine = flag_ref[t] == 1
    core = flag_ref[2]

    def stale(part, j):
        peer = got_ref[patch_at(order_ref, j, CACHE + part * ALL), :]
        return jnp.where(mine, own_ref[part, patch_at(order_ref, j), :], peer)

    old, other = [], []
    for part in range(2):
        old.append([stale(part, core * SIDE + j) for j in range(SIDE)])
        kept = jnp.concatenate([stale(part, (1 - core) * SIDE + j) for j in range(SIDE)], axis=0)
        other.append(jnp.where(core == 1, other_ref[part], kept))
    queries, keys, values = [], [], []
    for j in range(SIDE):
        queries.append(q_ref[j * ROWS : (j + 1) * ROWS, :])
        for part, found in ((0, keys), (1, values)):
            parts = [kv_ref[part, : (j + 1) * ROWS, :]] + old[part][j + 1 :] + [other[part]]
            found.append(jnp.concatenate(parts, axis=0))
    for j, mixed in enumerate(softmax_mix(queries, keys, values)):
        for s in range(SIDE):
            out_ref[s, j * ROWS : (j + 1) * ROWS, :] = mixed


def update_half_kernel(t, flag_ref, mixed_ref, own_ref, peer_ref, x_ref, send_ref, got_ref, rows_ref, *refs):
    last = t == 1
    if last:
        w_ref, held_ref, sem = refs
    else:
        new_ref, spread_ref, w_ref, held_ref, sem = refs

    @pl.when(flag_ref[t] == 1)
    def _():
        pltpu.make_async_copy(own_ref, w_ref, sem).start()

    @pl.when(flag_ref[t] == 0)
    def _():
        pltpu.make_async_copy(peer_ref, w_ref, sem).start()

    mixed = jnp.concatenate([mixed_ref[place(flag_ref, h)] for h in range(SEQ)], axis=1)
    pltpu.make_async_copy(own_ref, w_ref, sem).wait()
    held_ref[:, :SHARD] = lax.dot_general(mixed, w_ref[...], TRANSPOSED, preferred_element_type=F32)
    mods = mods_of(flag_ref, t, send_ref, got_ref).astype(F32)
    gate_first = mods[8:9] + mods[9:10]
    gate_last = mods[10:11] + mods[11:12]
    first = (x_ref[:HALF, :].astype(F32) + gate_first * held_ref[:, :LANES]).astype(BF16)
    made = pair_lanes(low_lanes(QUARTER), held_ref[:QUARTER, LANES:], held_ref[QUARTER:, LANES:])
    rest = x_ref[HALF:, :].astype(F32) + gate_last * made
    other = pltpu.roll(rest, REST, 1).astype(BF16)
    rest = rest.astype(BF16)
    for n in range(SIDE):
        at = slice((n % 2) * ROWS, (n % 2 + 1) * ROWS)
        rows_ref[n, :, :LANES] = first[n * ROWS : (n + 1) * ROWS]
        rows_ref[n, :, LANES:] = rest[at] if n < 2 else other[at]
    if not last:
        mods = mods_of(flag_ref, 1, send_ref, got_ref)
        new_ref[:HALF, :] = first
        new_ref[HALF:, :] = rest
        for s in range(SIDE):
            spread_ref[s, :HALF, :] = first
            spread_ref[s, HALF:PACK, :] = rest
            spread_ref[s, PACK:, :] = mods


def join_kernel(in_ref, out_ref):
    low = low_lanes(ROWS)
    for i in range(SIDE):
        out_ref[:, tile(i)] = in_ref[i, :, :LANES]
    for m in range(SIDE // 2):
        even, odd = (in_ref[2 * m + k, :, LANES:].astype(F32) for k in range(2))
        out_ref[:, tile(SIDE + m)] = pair_lanes(low, even, odd).astype(BF16)


def mods_kernel(gathered_ref, out_ref):
    low = low_lanes(1)
    rows = [gathered_ref[i, :MODS, :].astype(F32) for i in range(SIDE)]
    lines = []
    for k in range(3):
        for h in range(2):
            first, last = 4 * k + h, 4 * k + 2 + h
            parts = [rows[i][first : first + 1] for i in range(SIDE)]
            for m in range(SIDE // 2):
                even, odd = (rows[2 * m + e][last : last + 1] for e in range(2))
                parts.append(jnp.where(low, even, odd))
            lines.append(jnp.concatenate(parts, axis=1))
    lines.append(jnp.zeros((MODS - len(lines), WIDE), F32))
    out_ref[...] = jnp.concatenate(lines, axis=0).astype(BF16)


def spread_kernel(low_ref, high_ref, x_ref, out_ref):
    x_ref[:ROWS, :] = low_ref[...]
    x_ref[ROWS:, :] = high_ref[...]
    for s in range(SIDE):
        out_ref[s, :ROWS, :] = low_ref[...]
        out_ref[s, ROWS:, :] = high_ref[...]


def project_kernel(row_ref, x_ref, mods_ref, w_ref, below_ref, above_ref, *refs):
    across_low_ref, across_high_ref, q_ref, kv_ref, wm_ref, wr_ref, nm_ref, nr_ref, sems = refs
    i = row_ref[0]
    half = SIDE // 2
    sources = (
        (w_ref, 0, SIDE, i),
        (below_ref, 0, SIDE, lax.rem(i + 3, SIDE)),
        (above_ref, 0, SIDE, lax.rem(i + 1, SIDE)),
        (across_low_ref, 0, half, lax.rem(i + 2, SIDE)),
        (across_high_ref, half, SIDE, lax.rem(i + 2, SIDE)),
    )
    copies = []
    for t in range(3):
        for source, first, last, h in sources:
            lanes = pl.ds(pl.multiple_of((t * SIDE + h) * HEAD_DIM, HEAD_DIM), HEAD_DIM)
            pairs = [(source.at[t, :, :, :LANES, :], wm_ref.at[first:last, :, :, lanes])]
            pairs += [(source.at[t, :, j, LANES:, :], wr_ref.at[j, first:last, :, lanes]) for j in range(SIDE)]
            copies += [pltpu.make_async_copy(a, b, sems.at[len(copies) + n]) for n, (a, b) in enumerate(pairs)]
    for copy in copies:
        copy.start()
    mods = [mods_ref[j].astype(F32) for j in range(SIDE)]
    scale = [m[0:1] + m[1:2] for m in mods]
    shift = [m[2:3] + m[3:4] for m in mods]
    tiles = WIDE // LANES
    for g in range(GROUP):
        mine = pl.ds(g * ROWS, ROWS)
        total, square = (jnp.zeros((ROWS, LANES), F32) for _ in range(2))
        for j in range(SIDE):
            for k in range(tiles):
                x = x_ref[j, mine, tile(k)].astype(F32)
                total = total + x
                square = square + x * x
        mean = jnp.sum(total, axis=1, keepdims=True) / WIDTH
        var = jnp.sum(square, axis=1, keepdims=True) / WIDTH - mean * mean
        rstd = lax.rsqrt(var + EPSILON)
        for j in range(SIDE):
            for k in range(tiles):
                x = x_ref[j, mine, tile(k)].astype(F32)
                normed = ((x - mean) * rstd * scale[j][:, tile(k)] + shift[j][:, tile(k)]).astype(BF16)
                if k < SIDE:
                    nm_ref[mine, tile(k * SIDE + j)] = normed
                else:
                    nr_ref[mine, tile(j * (SIDE // 2) + k - SIDE)] = normed
    each = len(copies) // 3
    for t in range(3):
        for copy in copies[t * each : (t + 1) * each]:
            copy.wait()
        lanes = slice(t * HEADS, (t + 1) * HEADS)
        part = jnp.dot(nm_ref[...], wm_ref[:, :, :, lanes].reshape(SEQ * LANES, HEADS), preferred_element_type=F32)
        part = part + jnp.dot(nr_ref[...], wr_ref[:, :, :, lanes].reshape(SEQ * REST, HEADS), preferred_element_type=F32)
        part = part.astype(BF16)
        if t == 0:
            q_ref[...] = part
        else:
            for s in range(SIDE):
                kv_ref[s, :, (t - 1) * HEADS : t * HEADS] = part


def attend_kernel(row_ref, order_ref, q_ref, kv_ref, stale_ref, out_ref, low_ref, high_ref):
    i = row_ref[0]
    for pair in range(SIDE // 2):
        where, queries, keys, values = [], [], [], []
        for h in (2 * pair, 2 * pair + 1):
            new, old = [], []
            for part in range(2):
                lanes = tile(part * SIDE + h)
                halves = [slice(g * ROWS, (g + 1) * ROWS) for g in range(GROUP)]
                new.append([kv_ref[n % SIDE, halves[n // SIDE], lanes] for n in range(PATCHES)])
                old.append([stale_ref[h, patch_at(order_ref, n, MODS + part * ALL), :] for n in range(PATCHES)])
            for g in range(GROUP):
                where.append((halves[g], tile(h)))
                queries.append(q_ref[halves[g], tile(h)])
                for part, found in ((0, keys), (1, values)):
                    rows = [jnp.where(n <= i + SIDE * g, new[part][n], old[part][n]) for n in range(PATCHES)]
                    found.append(jnp.concatenate(rows, axis=0))
        for (rows, lanes), mixed in zip(where, softmax_mix(queries, keys, values), strict=True):
            for s in range(SIDE):
                out_ref[s, rows, lanes] = mixed
    for part in range(2):
        lanes = pl.ds(pl.multiple_of(part * HEADS + i * HEAD_DIM, HEAD_DIM), HEAD_DIM)
        for n in range(SIDE):
            low_ref[part, n * ROWS : (n + 1) * ROWS, :] = kv_ref[n, :ROWS, lanes]
            high_ref[part, n * ROWS : (n + 1) * ROWS, :] = kv_ref[n, ROWS:, lanes]


def update_kernel(row_ref, mixed_ref, w_ref, below_ref, above_ref, *refs):
    across_low_ref, across_high_ref, x_ref, mods_ref, out_ref, part_ref, held_ref, sems = refs
    i = row_ref[0]
    width = SEQ * HEAD_DIM
    sources = (
        (w_ref, 0, width, i),
        (below_ref, 0, width, lax.rem(i + 3, SIDE)),
        (above_ref, 0, width, lax.rem(i + 1, SIDE)),
        (across_low_ref, 0, width // 2, lax.rem(i + 2, SIDE)),
        (across_high_ref, width // 2, width, lax.rem(i + 2, SIDE)),
    )
    copies = []
    for source, begin, end, h in sources:
        first = pl.ds(pl.multiple_of(h * LANES, LANES), LANES)
        last = pl.ds(pl.multiple_of(SIDE * LANES + h * REST, REST), REST)
        for taken, rows in ((slice(0, LANES), first), (slice(LANES, SHARD), last)):
            held = held_ref.at[rows, begin:end]
            copies.append(pltpu.make_async_copy(source.at[taken, :], held, sems.at[len(copies)]))
    for copy in copies:
        copy.start()
    mixed = jnp.concatenate([mixed_ref[h % SIDE, :, tile(h // SIDE)] for h in range(SEQ)], axis=1)
    for copy in copies:
        copy.wait()
    made = lax.dot_general(mixed, held_ref[...], TRANSPOSED, preferred_element_type=F32)
    mods = mods_ref[...].astype(F32)
    new = x_ref[...].astype(F32) + (mods[4:5] + mods[5:6]) * made
    out_ref[...] = new.astype(BF16)
    for n in range(SIDE):
        rest = new[:, tile(SIDE + n // 2)]
        part_ref[n, :, :LANES] = new[:, tile(n)].astype(BF16)
        part_ref[n, :, LANES:] = (rest if n % 2 == 0 else pltpu.roll(rest, REST, 1)).astype(BF16)


def finish_kernel(order_ref, low_ref, high_ref, kv_low_ref, kv_high_ref, out_ref, cache_ref, rows_ref):
    for half, (x_ref, kv_ref) in enumerate(((low_ref, kv_low_ref), (high_ref, kv_high_ref))):
        for n in range(SIDE):
            at = patch_at(order_ref, half * SIDE + n)
            rows_ref[at, :] = x_ref[n].astype(F32)
            for part in range(2):
                cache_ref[part, at, :] = kv_ref[part, n * ROWS : (n + 1) * ROWS, :]
    out_ref[...] = rows_ref[...].T[:SHARD, :].astype(BF16)


def blank(*shapes):
    return pl.pallas_call(lambda *refs: None, out_shape=shapes, out_specs=(ANY,) * len(shapes), name="blank")()


def body(latents, patch_order, timestep, mod_table, w_qkv, w_out, kv_cache):
    sections = lax.axis_size("section")
    section = lax.axis_index("section")
    position = section % CHAIN
    core = (section % 2).astype(jnp.int32)
    row = (lax.axis_index("seq") // SIDE).astype(jnp.int32)[None]
    w_own = jnp.transpose(w_qkv[0], (1, 0, 2))
    o_own = jnp.transpose(w_out[0], (1, 0))
    cache_own = kv_cache[0]
    mod_now = lax.dynamic_index_in_dim(mod_table, timestep[0], 0, keepdims=False)[0]

    def swap(value):
        return lax.ppermute(value, "section", [(s, s ^ 1) for s in range(sections)])

    def exchange(value, groups):
        return lax.all_to_all(value, "seq", 0, 0, axis_index_groups=groups)

    def shift(value, by):
        pairs = [(s, (s + SIDE * by) % SEQ) for s in range(SEQ)]
        return lax.ppermute(value, "seq", pairs)

    def by_core(value, even, odd):
        groups = [[s * SEQ + d for d in g] for s in range(sections) for g in (odd if s % 2 else even)]
        return lax.all_to_all(value, ("section", "seq"), 0, 0, axis_index_groups=groups)

    def gather_mixed(spread):
        near = by_core(spread, ALONG_Z, ALONG_X)
        far = by_core(jnp.broadcast_to(near[None], (SIDE,) + near.shape), ALONG_X, ALONG_Z)
        return far.reshape((SEQ,) + near.shape[1:])

    def gather(value, groups):
        return exchange(jnp.broadcast_to(value[None], (SIDE,) + value.shape), groups)

    rows_shape, kv_shape = shaped(SIDE, ROWS, 2 * LANES), shaped(2, HALF, HEAD_DIM)
    patch_shape, x_shape, parts_shape = shaped(ROWS, WIDE), shaped(PART, WIDE), shaped(SIDE, PART, 2 * LANES)

    flags = jnp.stack([core == 0, core == 1, core]).astype(jnp.int32)
    flags, mod_now = lax.optimization_barrier((flags, mod_now))
    own, send = call(
        pack_kernel,
        "pack",
        (shaped(PACK, LANES), shaped(CACHE + 2 * ALL, LANES)),
        [SMEM, VMEM, VMEM, VMEM],
        patch_order,
        jnp.transpose(latents[0], (1, 0)),
        mod_now,
        cache_own,
        scratch=[pltpu.VMEM((ALL, 2 * LANES), F32)],
    )
    own, send, w_own, o_own = lax.optimization_barrier((own, send, w_own, o_own))
    got, w_peer, o_peer = swap(send), swap(w_own), swap(o_own)
    got, w_peer, o_peer = lax.optimization_barrier((got, w_peer, o_peer))

    def first_blocks(own, send, got, w_peer, o_peer):
        spread_shape = shaped(SIDE, PACK + MODS, LANES)
        x, spread = call(
            start_kernel, "start", (shaped(PACK, LANES), spread_shape), [SMEM, VMEM, VMEM, VMEM], flags, own, send, got
        )
        kept = []
        for t in range(2):
            q, kv = call(
                functools.partial(project_half_kernel, t),
                "project_half",
                (shaped(HALF, HEAD_DIM), kv_shape),
                [SMEM, VMEM, ANY, ANY],
                flags,
                gather_mixed(spread),
                w_own.reshape(3, SEQ, SHARD, HEAD_DIM),
                w_peer.reshape(3, SEQ, SHARD, HEAD_DIM),
                scratch=[
                    pltpu.VMEM((SEQ, LANES, 3 * HEAD_DIM), BF16),
                    pltpu.VMEM((SEQ, REST, 3 * HEAD_DIM), BF16),
                    pltpu.VMEM((HALF, SEQ * LANES), BF16),
                    pltpu.VMEM((HALF, SEQ * REST), BF16),
                    pltpu.SemaphoreType.DMA((6,)),
                ],
            )
            kv_other = swap(kv)
            mixed = call(
                functools.partial(attend_half_kernel, t),
                "attend_half",
                shaped(SIDE, HALF, HEAD_DIM),
                [SMEM, SMEM, VMEM, VMEM, VMEM, VMEM, VMEM],
                flags,
                patch_order,
                q,
                kv,
                kv_other,
                cache_own,
                got,
            )
            heads = gather_mixed(mixed)
            last = t == 1
            results = call(
                functools.partial(update_half_kernel, t),
                "update_half",
                (rows_shape,) + (() if last else (shaped(PACK, LANES), spread_shape)),
                [SMEM, VMEM, ANY, ANY, VMEM, VMEM, VMEM],
                flags,
                heads,
                o_own,
                o_peer,
                x,
                send,
                got,
                scratch=[
                    pltpu.VMEM(o_own.shape, BF16),
                    pltpu.VMEM((HALF, 2 * LANES), F32),
                    pltpu.SemaphoreType.DMA,
                ],
            )
            if not last:
                x, spread = results[1:]
            kept.append((results[0], kv, kv_other))
        patch = call(join_kernel, "join", patch_shape, [VMEM], exchange(kept[1][0], ALONG_X))
        return patch, kept

    half_width = SEQ * HEAD_DIM // 2

    def prepare(small):
        w = w_own.reshape(3, SIDE, SIDE, SHARD, HEAD_DIM)
        w_near = shift(w, 1), shift(w, -1)
        small = gather(small, ALONG_X)
        mods = call(mods_kernel, "mods", shaped(MODS, WIDE), [VMEM], small)
        others = gather(mods, ALONG_Z), small, mods
        w_near, o, others = lax.optimization_barrier((w_near, o_own, others))
        w_far = shift(w_near[0][:, : SIDE // 2], 1), shift(w_near[1][:, SIDE // 2 :], -1)
        o_near = shift(o, 1), shift(o, -1)
        w_far, o_near = lax.optimization_barrier((w_far, o_near))
        o_far = shift(o_near[0][:, :half_width], 1), shift(o_near[1][:, half_width:], -1)
        mods_all, small, mods = others
        return w_near + w_far, o_near + o_far, small, mods, mods_all

    def no_weights(small):
        side, half = (shaped(3, n, SIDE, SHARD, HEAD_DIM) for n in (SIDE, SIDE // 2))
        whole, part = (shaped(SHARD, n) for n in (2 * half_width, half_width))
        shapes = (side, side, half, half, whole, whole, part, part)
        shapes += (shaped(SIDE, *small.shape), shaped(MODS, WIDE), shaped(SIDE, MODS, WIDE))
        made = blank(*shapes)
        return tuple(made[:4]), tuple(made[4:8]), *made[8:]

    def later_block(x, spread, w_others, o_others, small, mods, mods_all):
        q, kv = call(
            project_kernel,
            "project",
            (shaped(PART, HEADS), shaped(SIDE, PART, 2 * HEADS)),
            [SMEM, VMEM, VMEM] + [ANY] * 5,
            row,
            exchange(spread, ALONG_Z),
            mods_all,
            w_own.reshape(3, SIDE, SIDE, SHARD, HEAD_DIM),
            *w_others,
            scratch=[
                pltpu.VMEM((SIDE, SIDE, LANES, 3 * HEADS), BF16),
                pltpu.VMEM((SIDE, SIDE, REST, 3 * HEADS), BF16),
                pltpu.VMEM((PART, SEQ * LANES), BF16),
                pltpu.VMEM((PART, SEQ * REST), BF16),
                pltpu.SemaphoreType.DMA((75,)),
            ],
            mib=20,
        )
        mixed, kv_low, kv_high = call(
            attend_kernel,
            "attend",
            (shaped(SIDE, PART, HEADS), kv_shape, kv_shape),
            [SMEM, SMEM, VMEM, VMEM, VMEM],
            row,
            patch_order,
            q,
            exchange(kv, ALONG_X),
            small,
        )
        new, parts = call(
            update_kernel,
            "update",
            (x_shape, parts_shape),
            [SMEM, VMEM] + [ANY] * 5 + [VMEM, VMEM],
            row,
            exchange(mixed, ALONG_Z),
            o_own,
            *o_others,
            x,
            mods,
            scratch=[pltpu.VMEM((WIDE, SEQ * HEAD_DIM), BF16), pltpu.SemaphoreType.DMA((10,))],
        )
        return new, parts, kv_low, kv_high

    def second_block(low, high, weights):
        spread_shape = shaped(SIDE, PART, WIDE)
        x, spread = call(spread_kernel, "spread", (x_shape, spread_shape), [VMEM, VMEM], low, high)
        return later_block(x, spread, *weights)

    def third_block(x, weights):
        return later_block(x, jnp.broadcast_to(x[None], (SIDE,) + x.shape), *weights)

    early = position < 2
    one = (rows_shape, kv_shape, kv_shape)

    def not_here(*_):
        patch, *both = blank(patch_shape, *one, *one)
        return patch, [tuple(both[:3]), tuple(both[3:])]

    patch, kept = lax.cond(early, first_blocks, not_here, own, send, got, w_peer, o_peer)
    weights = lax.cond(early, no_weights, prepare, send[PACK:])
    patch, weights = lax.optimization_barrier((patch, weights))
    low = lax.ppermute(patch, "section", [(s, s + 2) for s in range(sections) if s % CHAIN == 0])
    high = lax.ppermute(patch, "section", [(s, s + 1) for s in range(sections) if s % CHAIN == 1])
    state = blank(x_shape, parts_shape, kv_shape, kv_shape)
    state = lax.cond(
        position == 2,
        lambda low, high, state, weights: second_block(low, high, weights),
        lambda low, high, state, weights: tuple(state),
        low,
        high,
        tuple(state),
        weights,
    )
    arrived = lax.ppermute(state[0], "section", [(s, s + 1) for s in range(sections) if s % CHAIN == 2])
    state = lax.cond(
        position == 3,
        lambda x, state, weights: third_block(x, weights)[1:],
        lambda x, state, weights: tuple(state),
        arrived,
        tuple(state[1:]),
        weights,
    )

    def finish_early(state, kept):
        (rows0, kv0, other0), (rows1, kv1, other1) = kept
        first = core == 0
        mine, theirs = jnp.where(first, rows0, rows1), jnp.where(first, rows1, rows0)
        other = swap(theirs)
        rows = jnp.where(first, mine, other), jnp.where(first, other, mine)
        return rows + (jnp.where(first, kv0, other1), jnp.where(first, other0, kv1))

    def finish_late(state, kept):
        parts, kv_low, kv_high = state
        rows = exchange(parts, ALONG_X)
        return rows[:, :ROWS], rows[:, ROWS:], kv_low, kv_high

    rows_low, rows_high, kv_low, kv_high = lax.cond(early, finish_early, finish_late, state, kept)
    out_t, cache = call(
        finish_kernel,
        "finish",
        (shaped(SHARD, ALL), shaped(2, ALL, HEAD_DIM)),
        [SMEM, VMEM, VMEM, VMEM, VMEM],
        patch_order,
        rows_low,
        rows_high,
        kv_low,
        kv_high,
        scratch=[pltpu.VMEM((ALL, 2 * LANES), F32)],
    )
    return jnp.transpose(out_t, (1, 0))[None], cache[None]


def solution(mesh):
    return jax.shard_map(
        body,
        mesh=mesh,
        in_specs=(
            P("section", None, "seq"),
            P(),
            P(),
            P(None, "section", None, "seq"),
            P("section", None, None, "seq"),
            P("section", None, "seq"),
            P("section", None, None, "seq"),
        ),
        out_specs=(P("section", None, "seq"), P("section", None, None, "seq")),
        check_vma=False,
    )
```

time: 336 us -> 290 us (0.86)
  waiting for transfers between devices: 191 us -> 104 us
  starting transfers between devices: 8.46 us -> 40.7 us
  blocking collectives: 106 us -> 126 us
  local copies, waits for them, and re-layouts: 9.18 us -> 3.25 us
  Pallas kernels: 17.5 us -> 12.9 us
    all_to_all x1 -> x0, waiting for transfers between devices: 100 us -> none  [exchange(): return lax.all_to_all(value, 'seq', 0, 0, axis_index_groups=groups)]
    ppermute x3 -> x14, starting transfers between devices: 2.63 us -> 40.7 us  [the longest x8 26.4 us: shift(): return lax.ppermute(value, 'seq', pairs)]
    all_to_all x6, blocking collectives: 106 us -> 126 us  [exchange(): return lax.all_to_all(value, 'seq', 0, 0, axis_index_groups=groups)]
    ppermute x3 -> x14, waiting for transfers between devices: 90.6 us -> 104 us  [the longest x1 64.3 us: body(): lax.ppermute(state[0], 'section', [(s, s + 1) for s in range(sections) if...]
    all_to_all x1 -> x0, starting transfers between devices: 5.83 us -> none  [exchange(): return lax.all_to_all(value, 'seq', 0, 0, axis_index_groups=groups)]
    broadcast_in_dim x3 -> x2, local copies, waits for them, and re-layouts: 5.79 us -> 0.15 us  [gather(): jnp.broadcast_to(value[None], (SIDE,) + value.shape)]
    pallas_call x8 -> x6, Pallas kernels: 17.5 us -> 12.9 us  [call(): pl.pallas_call(kernel, out_shape=out_shape, in_specs=in_specs, out_specs=...]
  transfers between devices with their start and end apart: 4 -> 14, of which waited for: 2 -> 6; matrix products, arithmetic and copies ran while one was open for 0% -> 0% of each run, Pallas kernels for 1% -> 0%
where the time goes in v3:
time: 290 us; the launch traced here: 289 us
  blocking collectives  126 us (43%)
  waiting for transfers between devices  104 us (36%)
  starting transfers between devices  40.7 us (14%)
  Pallas kernels  12.9 us (4%)
  local copies, waits for them, and re-layouts  3.25 us (1%)
    all_to_all x6, blocking collectives, exchange(): return lax.all_to_all(value, 'seq', 0, 0, axis_index_groups=groups)  126 us
    ppermute x1, waiting for transfers between devices, body(): lax.ppermute(state[0], 'section', [(s, s + 1) for s in range(sections) if...  64.3 us
    ppermute x8, waiting for transfers between devices, shift(): return lax.ppermute(value, 'seq', pairs)  37.6 us
    ppermute x8, starting transfers between devices, shift(): return lax.ppermute(value, 'seq', pairs)  26.4 us
    pallas_call x6, Pallas kernels, call(): pl.pallas_call(kernel, out_shape=out_shape, in_specs=in_specs, out_specs=...  12.9 us
    ppermute x3, starting transfers between devices, swap(): return lax.ppermute(value, 'section', [(s, s ^ 1) for s in range(sections)])  11.7 us
  transfers between devices with their start and end apart: 14, of which 6 were waited for; matrix products, arithmetic and copies ran while one was open for 0% of the time, Pallas kernels for 0%

profile of v3, /device:TPU:65, one launch (start us, length us, event | category | flops | bytes accessed | tf_op | source)
XLA Modules:
  0.0 288.9 jit_solution(17881528160141569256)
XLA Ops:
  1.7 0.9 copy-done.1
  2.6 1.8 pack.1
  4.4 2.6 collective-permute-start.12
  7.0 144.7 %conditional.6 = ((bf16[3,4,4,192,128]{4,3,2,1,0:T(8,128)(2,1)}, bf16[3,4,4,192,128]{4,3,2,1,0:T(8,128)(2,1)}, bf16[3,2,4,192,128]{4,3,2,1,0:T(8,128)(2,1)}, bf1...) conditional(s32[]{:T(128)} %convert_element_type.6, ...), branch_computations={%region_2.3_spmd, %region_3.4_spmd} | conditional | bytes 86102648 | solution.py:636
  7.1 3.3 %collective-permute-start.2 = (bf16[3,4,4,192,128]{4,3,2,1,0:T(8,128)(2,1)}, bf16[3,4,4,192,128]{4,3,2,1,0:T(8,128)(2,1)S(1)}, u32[]{:S(2)}, u32[]{:S(2)}) collective-permute-start(bf16[3,4,4,192,128]{4,3,2,1,0:T(8,128)(2,1)} %bitcast.45), channel_id=1, source_target_pairs={{0,4},{1,5},{2,6},{3,7},{4,8},{5,9},{6,10},{7,11},{8,12},{9,13},{1... | collective-permute-start | bytes 7077896 | tf_op jit(solution)/shard_map/cond/branch_0_fun/ppermute | solution.py:452
  10.3 3.4 %collective-permute-start.3 = (bf16[3,4,4,192,128]{4,3,2,1,0:T(8,128)(2,1)}, bf16[3,4,4,192,128]{4,3,2,1,0:T(8,128)(2,1)S(1)}, u32[]{:S(2)}, u32[]{:S(2)}) collective-permute-start(bf16[3,4,4,192,128]{4,3,2,1,0:T(8,128)(2,1)} %bitcast.46), channel_id=1, source_target_pairs={{0,12},{1,13},{2,14},{3,15},{4,0},{5,1},{6,2},{7,3},{8,4},{9,5},{1... | collective-permute-start | bytes 7077896 | tf_op jit(solution)/shard_map/cond/branch_0_fun/ppermute | solution.py:452
  13.9 62.4 %all_to_all.81.gathered_ref = bf16[4,1040,128]{2,1,0:T(8,128)(2,1)S(1)} all-to-all(bf16[4,1040,128]{2,1,0:T(8,128)(2,1)S(1)} %broadcast_in_dim.13), channel_id=1, replica_groups={{0,4,8,12},{1,5,9,13},{2,6,10,14},{3,7,11,15},{16,20,24,28},{17,21,25,2..., dimensions={0} | all-to-all | bytes 2129920 | tf_op jit(solution)/shard_map/cond/branch_0_fun/all_to_all | solution.py:448
  76.3 16.1 %all_to_all.82 = bf16[4,16,768]{2,1,0:T(8,128)(2,1)} all-to-all(bf16[4,16,768]{2,1,0:T(8,128)(2,1)S(1)} %broadcast_in_dim.15), channel_id=1, replica_groups={{0,1,2,3},{4,5,6,7},{8,9,10,11},{12,13,14,15},{16,17,18,19},{20,21,22,2..., dimensions={0} | all-to-all | bytes 196608 | tf_op jit(solution)/shard_map/cond/branch_0_fun/all_to_all | solution.py:448
  92.6 4.0 %collective-permute-start.4 = (bf16[3,2,4,192,128]{4,3,2,1,0:T(8,128)(2,1)S(1)}, bf16[3,2,4,192,128]{4,3,2,1,0:T(8,128)(2,1)S(1)}, u32[]{:S(2)}, u32[]{:S(2)}) collective-permute-start(bf16[3,2,4,192,128]{4,3,2,1,0:T(8,128)(2,1)S(1)} %slice.16), channel_id=1, source_target_pairs={{0,4},{1,5},{2,6},{3,7},{4,8},{5,9},{6,10},{7,11},{8,12},{9,13},{1... | collective-permute-start | bytes 3538952 | tf_op jit(solution)/shard_map/cond/branch_0_fun/ppermute | solution.py:452
  96.6 2.8 collective-permute-start.5
  99.5 2.5 collective-permute-start.6
  102.0 4.0 %collective-permute-start.7 = (bf16[192,2048]{1,0:T(8,128)(2,1)S(1)}, bf16[192,2048]{1,0:T(8,128)(2,1)S(1)}, u32[]{:S(2)}, u32[]{:S(2)}) collective-permute-start(bf16[192,2048]{1,0:T(8,128)(2,1)S(1)} %copy-done.7), channel_id=1, source_target_pairs={{0,12},{1,13},{2,14},{3,15},{4,0},{5,1},{6,2},{7,3},{8,4},{9,5},{1... | collective-permute-start | bytes 2359304 | tf_op jit(solution)/shard_map/cond/branch_0_fun/ppermute | solution.py:452
  106.0 31.4 %collective-permute-done.6 = bf16[192,2048]{1,0:T(8,128)(2,1)S(1)} collective-permute-done((bf16[192,2048]{1,0:T(8,128)(2,1)S(1)}, bf16[192,2048]{1,0:T(8,128)(2,1)S(1)}, u32[]{:S(2)}, u32[]{:S(2)}) %collective-permute-start.6) | collective-permute-done | bytes 786464 | tf_op jit(solution)/shard_map/cond/branch_0_fun/ppermute | solution.py:452
  137.4 2.2 collective-permute-done.7
  139.7 2.4 collective-permute-start.8
  142.1 4.1 %collective-permute-start.9 = (bf16[192,1024]{1,0:T(8,128)(2,1)S(1)}, bf16[192,1024]{1,0:T(8,128)(2,1)S(1)}, u32[]{:S(2)}, u32[]{:S(2)}) collective-permute-start(bf16[192,1024]{1,0:T(8,128)(2,1)S(1)} %slice.19), channel_id=1, source_target_pairs={{0,12},{1,13},{2,14},{3,15},{4,0},{5,1},{6,2},{7,3},{8,4},{9,5},{1... | collective-permute-start | bytes 1179656 | tf_op jit(solution)/shard_map/cond/branch_0_fun/ppermute | solution.py:452
  146.3 3.2 %collective-permute-done.8 = bf16[192,1024]{1,0:T(8,128)(2,1)S(1)} collective-permute-done((bf16[192,1024]{1,0:T(8,128)(2,1)S(1)}, bf16[192,1024]{1,0:T(8,128)(2,1)S(1)}, u32[]{:S(2)}, u32[]{:S(2)}) %collective-permute-start.8) | collective-permute-done | bytes 393248 | tf_op jit(solution)/shard_map/cond/branch_0_fun/ppermute | solution.py:452
  151.7 7.2 %collective-permute-start.13 = (bf16[192,2048]{1,0:T(8,128)(2,1)}, bf16[192,2048]{1,0:T(8,128)(2,1)S(1)}, u32[]{:S(2)}, u32[]{:S(2)}) collective-permute-start(bf16[192,2048]{1,0:T(8,128)(2,1)} %bitcast.52), channel_id=1, source_target_pairs={{0,16},{16,0},{32,48},{48,32},{64,80},{80,64},{96,112},{112,96},{1... | collective-permute-start | bytes 2359304 | tf_op jit(solution)/shard_map/ppermute | solution.py:445
  158.9 1.9 collective-permute-start.11
  160.8 1.6 collective-permute-done.11
  164.2 1.3 collective-permute-start.16
  165.5 64.3 %collective-permute-done.16 = bf16[128,768]{1,0:T(8,128)(2,1)S(1)} collective-permute-done((bf16[128,768]{1,0:T(8,128)(2,1)}, bf16[128,768]{1,0:T(8,128)(2,1)S(1)}, u32[]{:S(2)}, u32[]{:S(2)}) %collective-permute-start.16) | collective-permute-done | bytes 196640 | tf_op jit(solution)/shard_map/ppermute | solution.py:650
  229.8 49.3 %conditional.8 = ((bf16[4,128,256]{2,1,0:T(8,128)(2,1)S(1)}, bf16[2,256,128]{2,1,0:T(8,128)(2,1)}, bf16[2,256,128]{2,1,0:T(8,128)(2,1)})) conditional(s32[]{:T(128)} %convert_element_type.14, (bf16[4,128,256]{2,1,0:T(8,128)(2,1)S(1)}, bf16[2,256,128]{2,1,0:T(8,128)(2,1)}, bf16[2,256,128]{2,1,0:T(8,128)(2,1)}) %tuple.57, ...), branch_computations={%region_6.7_spmd, %region_7.8_spmd} | conditional | bytes 21823660 | solution.py:651
  229.8 15.0 %all_to_all.86.x_ref = bf16[4,128,768]{2,1,0:T(8,128)(2,1)S(1)} all-to-all(bf16[4,128,768]{2,1,0:T(8,128)(2,1)S(1)} %broadcast_in_dim.16), channel_id=1, replica_groups={{0,1,2,3},{4,5,6,7},{8,9,10,11},{12,13,14,15},{16,17,18,19},{20,21,22,2..., dimensions={0} | all-to-all | bytes 1572864 | tf_op jit(solution)/shard_map/cond/branch_1_fun/all_to_all | solution.py:448
  244.9 4.5 %project.3 = (bf16[128,512]{1,0:T(8,128)(2,1)S(1)}, bf16[4,128,1024]{2,1,0:T(8,128)(2,1)S(1)}) custom-call(s32[1]{0:T(128)} %get-tuple-element.185.row_ref, bf16[4,128,768]{2,1,0:T(8,128)(2,1)S(1)} %all_to_all.86.x_ref, bf16[4,16,768]{2,1,0:T(8,128)(2,1)S(1)} %copy-done.24, bf16[3,4,4,192,128]{4,3,2,1,0:T(8,128)(2,1)S(1)} %bitcast.50, ...), custom_call_target="tpu_custom_call" | custom-call | tf_op jit(solution)/shard_map/cond/branch_1_fun/project/pallas_call | solution.py:48
  249.4 12.2 %all_to_all.87.kv_ref = bf16[4,128,1024]{2,1,0:T(8,128)(2,1)S(1)} all-to-all(bf16[4,128,1024]{2,1,0:T(8,128)(2,1)S(1)} %get-tuple-element.195), channel_id=1, replica_groups={{0,4,8,12},{1,5,9,13},{2,6,10,14},{3,7,11,15},{16,20,24,28},{17,21,25,2..., dimensions={0} | all-to-all | bytes 2097152 | tf_op jit(solution)/shard_map/cond/branch_1_fun/all_to_all | solution.py:448
  261.6 2.5 attend.3
  264.0 12.8 %all_to_all.88.mixed_ref = bf16[4,128,512]{2,1,0:T(8,128)(2,1)S(1)} all-to-all(bf16[4,128,512]{2,1,0:T(8,128)(2,1)S(1)} %get-tuple-element.197), channel_id=1, replica_groups={{0,1,2,3},{4,5,6,7},{8,9,10,11},{12,13,14,15},{16,17,18,19},{20,21,22,2..., dimensions={0} | all-to-all | bytes 1048576 | tf_op jit(solution)/shard_map/cond/branch_1_fun/all_to_all | solution.py:448
  276.8 2.3 update.3
  279.1 8.0 %conditional.9 = (bf16[4,64,256]{2,1,0:T(8,128)(2,1)S(1)}, bf16[4,64,256]{2,1,0:T(8,128)(2,1)S(1)}, bf16[2,256,128]{2,1,0:T(8,128)(2,1)}, bf16[2,256,128]{2,1,0:T(8,128)(2,1)}) conditional(s32[]{:T(128)} %convert_element_type.6, (bf16[4,128,256]{2,1,0:T(8,128)(2,1)S(1)}, bf16[2,256,128]{2,1,0:T(8,128)(2,1)}, ...), branch_computations={%region_8.9_spmd, %region_9.10_spmd} | conditional | flops 393217 | bytes 2359380 | solution.py:673
  279.1 7.9 %all_to_all.89 = bf16[4,128,256]{2,1,0:T(8,128)(2,1)S(1)} all-to-all(bf16[4,128,256]{2,1,0:T(8,128)(2,1)S(1)} %get-tuple-element.207), channel_id=1, replica_groups={{0,4,8,12},{1,5,9,13},{2,6,10,14},{3,7,11,15},{16,20,24,28},{17,21,25,2..., dimensions={0} | all-to-all | bytes 524288 | tf_op jit(solution)/shard_map/cond/branch_0_fun/all_to_all | solution.py:448
  287.0 1.8 finish.1
  (63 shorter events, 4.7 us)
Async XLA Ops:
  0.6 0.9 copy-start
  1.7 0.9 copy-start.1
  4.4 158.1 %collective-permute-start.12 = (bf16[3,3072,128]{2,1,0:T(8,128)(2,1)}, bf16[3,3072,128]{2,1,0:T(8,128)(2,1)}, u32[]{:S(2)}, u32[]{:S(2)}) collective-permute-start(bf16[3,3072,128]{2,1,0:T(8,128)(2,1)} %bitcast.40), channel_id=1, source_target_pairs={{0,16},{16,0},{32,48},{48,32},{64,80},{80,64},{96,112},{112,96},{1... | collective-permute-start | bytes 7077896 | tf_op jit(solution)/shard_map/ppermute | solution.py:445
  7.0 155.5 %copy-start.6 = (bf16[1,2048,192]{1,2,0:T(8,128)(2,1)S(1)}, bf16[1,2048,192]{1,2,0:T(8,128)(2,1)}, u32[]{:S(2)}) copy-start(bf16[1,2048,192]{1,2,0:T(8,128)(2,1)} %param.22) | copy-start | bytes 2359300
  7.0 155.5 %copy-start.16 = (bf16[1,2,512,128]{3,2,1,0:T(8,128)(2,1)S(1)}, bf16[1,2,512,128]{3,2,1,0:T(8,128)(2,1)}, u32[]{:S(2)}) copy-start(bf16[1,2,512,128]{3,2,1,0:T(8,128)(2,1)} %param.23) | copy-start | bytes 786436
  7.0 155.5 %copy-start.25 = (s32[8]{0:T(128)S(1)}, s32[8]{0:T(128)}, u32[]{:S(2)}) copy-start(s32[8]{0:T(128)} %order_ref.3) | copy-start | bytes 100
  7.1 85.4 %collective-permute-start.2 = (bf16[3,4,4,192,128]{4,3,2,1,0:T(8,128)(2,1)}, bf16[3,4,4,192,128]{4,3,2,1,0:T(8,128)(2,1)S(1)}, u32[]{:S(2)}, u32[]{:S(2)}) collective-permute-start(bf16[3,4,4,192,128]{4,3,2,1,0:T(8,128)(2,1)} %bitcast.45), channel_id=1, source_target_pairs={{0,4},{1,5},{2,6},{3,7},{4,8},{5,9},{6,10},{7,11},{8,12},{9,13},{1... | collective-permute-start | bytes 7077896 | tf_op jit(solution)/shard_map/cond/branch_0_fun/ppermute | solution.py:452
  10.3 82.1 %collective-permute-start.3 = (bf16[3,4,4,192,128]{4,3,2,1,0:T(8,128)(2,1)}, bf16[3,4,4,192,128]{4,3,2,1,0:T(8,128)(2,1)S(1)}, u32[]{:S(2)}, u32[]{:S(2)}) collective-permute-start(bf16[3,4,4,192,128]{4,3,2,1,0:T(8,128)(2,1)} %bitcast.46), channel_id=1, source_target_pairs={{0,12},{1,13},{2,14},{3,15},{4,0},{5,1},{6,2},{7,3},{8,4},{9,5},{1... | collective-permute-start | bytes 7077896 | tf_op jit(solution)/shard_map/cond/branch_0_fun/ppermute | solution.py:452
  92.4 4.2 %copy-start.4 = (bf16[3,4,4,192,128]{4,3,2,1,0:T(8,128)(2,1)}, bf16[3,4,4,192,128]{4,3,2,1,0:T(8,128)(2,1)S(1)}, u32[]{:S(2)}) copy-start(bf16[3,4,4,192,128]{4,3,2,1,0:T(8,128)(2,1)S(1)} %collective-permute-done.2) | copy-start | bytes 7077892 | tf_op jit(solution)/shard_map/cond
  92.4 4.2 %copy-start.5 = (bf16[3,4,4,192,128]{4,3,2,1,0:T(8,128)(2,1)}, bf16[3,4,4,192,128]{4,3,2,1,0:T(8,128)(2,1)S(1)}, u32[]{:S(2)}) copy-start(bf16[3,4,4,192,128]{4,3,2,1,0:T(8,128)(2,1)S(1)} %collective-permute-done.3) | copy-start | bytes 7077892 | tf_op jit(solution)/shard_map/cond
  92.5 6.9 %copy-start.7 = (bf16[192,2048]{1,0:T(8,128)(2,1)S(1)}, bf16[192,2048]{1,0:T(8,128)(2,1)}, u32[]{:S(2)}) copy-start(bf16[192,2048]{1,0:T(8,128)(2,1)} %get-tuple-element.151) | copy-start | bytes 2359300 | tf_op jit(solution)/shard_map/cond
  92.6 47.1 %collective-permute-start.4 = (bf16[3,2,4,192,128]{4,3,2,1,0:T(8,128)(2,1)S(1)}, bf16[3,2,4,192,128]{4,3,2,1,0:T(8,128)(2,1)S(1)}, u32[]{:S(2)}, u32[]{:S(2)}) collective-permute-start(bf16[3,2,4,192,128]{4,3,2,1,0:T(8,128)(2,1)S(1)} %slice.16), channel_id=1, source_target_pairs={{0,4},{1,5},{2,6},{3,7},{4,8},{5,9},{6,10},{7,11},{8,12},{9,13},{1... | collective-permute-start | bytes 3538952 | tf_op jit(solution)/shard_map/cond/branch_0_fun/ppermute | solution.py:452
  96.6 43.0 %collective-permute-start.5 = (bf16[3,2,4,192,128]{4,3,2,1,0:T(8,128)(2,1)S(1)}, bf16[3,2,4,192,128]{4,3,2,1,0:T(8,128)(2,1)S(1)}, u32[]{:S(2)}, u32[]{:S(2)}) collective-permute-start(bf16[3,2,4,192,128]{4,3,2,1,0:T(8,128)(2,1)S(1)} %slice.17), channel_id=1, source_target_pairs={{0,12},{1,13},{2,14},{3,15},{4,0},{5,1},{6,2},{7,3},{8,4},{9,5},{1... | collective-permute-start | bytes 3538952 | tf_op jit(solution)/shard_map/cond/branch_0_fun/ppermute | solution.py:452
  99.5 37.9 %collective-permute-start.6 = (bf16[192,2048]{1,0:T(8,128)(2,1)S(1)}, bf16[192,2048]{1,0:T(8,128)(2,1)S(1)}, u32[]{:S(2)}, u32[]{:S(2)}) collective-permute-start(bf16[192,2048]{1,0:T(8,128)(2,1)S(1)} %copy-done.7), channel_id=1, source_target_pairs={{0,4},{1,5},{2,6},{3,7},{4,8},{5,9},{6,10},{7,11},{8,12},{9,13},{1... | collective-permute-start | bytes 2359304 | tf_op jit(solution)/shard_map/cond/branch_0_fun/ppermute | solution.py:452
  102.0 37.7 %collective-permute-start.7 = (bf16[192,2048]{1,0:T(8,128)(2,1)S(1)}, bf16[192,2048]{1,0:T(8,128)(2,1)S(1)}, u32[]{:S(2)}, u32[]{:S(2)}) collective-permute-start(bf16[192,2048]{1,0:T(8,128)(2,1)S(1)} %copy-done.7), channel_id=1, source_target_pairs={{0,12},{1,13},{2,14},{3,15},{4,0},{5,1},{6,2},{7,3},{8,4},{9,5},{1... | collective-permute-start | bytes 2359304 | tf_op jit(solution)/shard_map/cond/branch_0_fun/ppermute | solution.py:452
  139.6 2.4 copy-start.8
  139.6 2.5 copy-start.11
  139.6 6.6 %copy-start.13 = (bf16[3,2,4,192,128]{4,3,2,1,0:T(8,128)(2,1)}, bf16[3,2,4,192,128]{4,3,2,1,0:T(8,128)(2,1)S(1)}, u32[]{:S(2)}) copy-start(bf16[3,2,4,192,128]{4,3,2,1,0:T(8,128)(2,1)S(1)} %collective-permute-done.5) | copy-start | bytes 3538948 | tf_op jit(solution)/shard_map/cond
  139.7 9.7 %collective-permute-start.8 = (bf16[192,1024]{1,0:T(8,128)(2,1)S(1)}, bf16[192,1024]{1,0:T(8,128)(2,1)S(1)}, u32[]{:S(2)}, u32[]{:S(2)}) collective-permute-start(bf16[192,1024]{1,0:T(8,128)(2,1)S(1)} %slice.18), channel_id=1, source_target_pairs={{0,4},{1,5},{2,6},{3,7},{4,8},{5,9},{6,10},{7,11},{8,12},{9,13},{1... | collective-permute-start | bytes 1179656 | tf_op jit(solution)/shard_map/cond/branch_0_fun/ppermute | solution.py:452
  142.1 8.8 %collective-permute-start.9 = (bf16[192,1024]{1,0:T(8,128)(2,1)S(1)}, bf16[192,1024]{1,0:T(8,128)(2,1)S(1)}, u32[]{:S(2)}, u32[]{:S(2)}) collective-permute-start(bf16[192,1024]{1,0:T(8,128)(2,1)S(1)} %slice.19), channel_id=1, source_target_pairs={{0,12},{1,13},{2,14},{3,15},{4,0},{5,1},{6,2},{7,3},{8,4},{9,5},{1... | collective-permute-start | bytes 1179656 | tf_op jit(solution)/shard_map/cond/branch_0_fun/ppermute | solution.py:452
  149.4 0.8 copy-start.17
  151.0 0.8 copy-start.20
  151.7 10.8 %collective-permute-start.13 = (bf16[192,2048]{1,0:T(8,128)(2,1)}, bf16[192,2048]{1,0:T(8,128)(2,1)S(1)}, u32[]{:S(2)}, u32[]{:S(2)}) collective-permute-start(bf16[192,2048]{1,0:T(8,128)(2,1)} %bitcast.52), channel_id=1, source_target_pairs={{0,16},{16,0},{32,48},{48,32},{64,80},{80,64},{96,112},{112,96},{1... | collective-permute-start | bytes 2359304 | tf_op jit(solution)/shard_map/ppermute | solution.py:445
  158.9 3.6 %collective-permute-start.11 = (bf16[1424,128]{1,0:T(8,128)(2,1)S(1)}, bf16[1424,128]{1,0:T(8,128)(2,1)S(1)}, u32[]{:S(2)}, u32[]{:S(2)}) collective-permute-start(bf16[1424,128]{1,0:T(8,128)(2,1)S(1)} %get-tuple-element.275), channel_id=1, source_target_pairs={{0,16},{16,0},{32,48},{48,32},{64,80},{80,64},{96,112},{112,96},{1... | collective-permute-start | bytes 1093640 | tf_op jit(solution)/shard_map/ppermute | solution.py:445
  162.7 1.4 collective-permute-start.14
  163.4 0.7 collective-permute-start.15
  164.2 65.6 %collective-permute-start.16 = (bf16[128,768]{1,0:T(8,128)(2,1)}, bf16[128,768]{1,0:T(8,128)(2,1)S(1)}, u32[]{:S(2)}, u32[]{:S(2)}) collective-permute-start(bf16[128,768]{1,0:T(8,128)(2,1)} %get-tuple-element.308), channel_id=1, source_target_pairs={{32,48},{96,112},{160,176},{224,240},{288,304},{352,368},{416,432}... | collective-permute-start | bytes 589832 | tf_op jit(solution)/shard_map/ppermute | solution.py:650
  229.8 15.1 %copy-start.3 = (bf16[3,3072,128]{2,1,0:T(8,128)(2,1)S(1)}, bf16[3,3072,128]{2,1,0:T(8,128)(2,1)}, u32[]{:S(2)}) copy-start(bf16[3,3072,128]{2,1,0:T(8,128)(2,1)} %get-tuple-element.189) | copy-start | bytes 7077892 | tf_op jit(solution)/shard_map/cond
  229.8 15.1 %copy-start.24 = (bf16[4,16,768]{2,1,0:T(8,128)(2,1)S(1)}, bf16[4,16,768]{2,1,0:T(8,128)(2,1)}, u32[]{:S(2)}) copy-start(bf16[4,16,768]{2,1,0:T(8,128)(2,1)} %get-tuple-element.188.mods_ref) | copy-start | bytes 294916 | tf_op jit(solution)/shard_map/cond
  261.5 15.2 %copy-start.10 = (bf16[192,2048]{1,0:T(8,128)(2,1)S(1)}, bf16[192,2048]{1,0:T(8,128)(2,1)}, u32[]{:S(2)}) copy-start(bf16[192,2048]{1,0:T(8,128)(2,1)} %get-tuple-element.200.above_ref) | copy-start | bytes 2359300 | tf_op jit(solution)/shard_map/cond
  261.5 15.2 %copy-start.19 = (bf16[192,1024]{1,0:T(8,128)(2,1)S(1)}, bf16[192,1024]{1,0:T(8,128)(2,1)}, u32[]{:S(2)}) copy-start(bf16[192,1024]{1,0:T(8,128)(2,1)} %get-tuple-element.201.refs_0_) | copy-start | bytes 1179652 | tf_op jit(solution)/shard_map/cond
  261.6 15.2 %copy-start.22 = (bf16[192,1024]{1,0:T(8,128)(2,1)S(1)}, bf16[192,1024]{1,0:T(8,128)(2,1)}, u32[]{:S(2)}) copy-start(bf16[192,1024]{1,0:T(8,128)(2,1)} %get-tuple-element.202.refs_1_) | copy-start | bytes 1179652 | tf_op jit(solution)/shard_map/cond

commit v4 on v3

--- a/solution.py
+++ b/solution.py
@@ -22,6 +22,7 @@
 HALF = ALL // 2
 QUARTER = HALF // 2
 PACK = HALF + QUARTER
+PIECE = ROWS + ROWS // 2
 MODS = 16
 CACHE = PACK + MODS
 GROUP = PATCHES // SIDE
@@ -43,13 +44,14 @@
     return jax.ShapeDtypeStruct(shape, dtype)
 
 
-def call(kernel, name, out_shape, in_specs, *args, scratch=(), mib=12):
+def call(kernel, name, out_shape, in_specs, *args, scratch=(), mib=12, outside=()):
     many = isinstance(out_shape, tuple)
+    spaces = [ANY if n in outside else VMEM for n in range(len(out_shape) if many else 1)]
     return pl.pallas_call(
         kernel,
         out_shape=out_shape,
         in_specs=in_specs,
-        out_specs=(VMEM,) * len(out_shape) if many else VMEM,
+        out_specs=tuple(spaces) if many else spaces[0],
         scratch_shapes=list(scratch),
         compiler_params=pltpu.CompilerParams(vmem_limit_bytes=mib * 1024 * 1024),
         name=name,
@@ -201,7 +203,17 @@
     kv_ref[1] = qkv[:, 2 * HEAD_DIM :]
 
 
-def attend_half_kernel(t, flag_ref, order_ref, q_ref, kv_ref, other_ref, own_ref, got_ref, out_ref):
+def attend_half_kernel(t, flag_ref, order_ref, q_ref, kv_ref, other_ref, own_ref, got_ref, *refs):
+    o_own_ref, o_peer_ref, out_ref, w_ref, sem = refs
+
+    @pl.when(flag_ref[t] == 1)
+    def _():
+        pltpu.make_async_copy(o_own_ref, w_ref, sem).start()
+
+    @pl.when(flag_ref[t] == 0)
+    def _():
+        pltpu.make_async_copy(o_peer_ref, w_ref, sem).start()
+
     mine = flag_ref[t] == 1
     core = flag_ref[2]
 
@@ -223,25 +235,17 @@
     for j, mixed in enumerate(softmax_mix(queries, keys, values)):
         for s in range(SIDE):
             out_ref[s, j * ROWS : (j + 1) * ROWS, :] = mixed
-
-
-def update_half_kernel(t, flag_ref, mixed_ref, own_ref, peer_ref, x_ref, send_ref, got_ref, rows_ref, *refs):
+    pltpu.make_async_copy(o_own_ref, w_ref, sem).wait()
+
+
+def update_half_kernel(t, flag_ref, mixed_ref, w_ref, x_ref, send_ref, got_ref, rows_out_ref, *refs):
     last = t == 1
     if last:
-        w_ref, held_ref, sem = refs
+        hand_out_ref, held_ref, rows_ref, hand_ref, sems = refs
     else:
-        new_ref, spread_ref, w_ref, held_ref, sem = refs
-
-    @pl.when(flag_ref[t] == 1)
-    def _():
-        pltpu.make_async_copy(own_ref, w_ref, sem).start()
-
-    @pl.when(flag_ref[t] == 0)
-    def _():
-        pltpu.make_async_copy(peer_ref, w_ref, sem).start()
+        new_ref, spread_ref, held_ref, rows_ref, _, sems = refs
 
     mixed = jnp.concatenate([mixed_ref[place(flag_ref, h)] for h in range(SEQ)], axis=1)
-    pltpu.make_async_copy(own_ref, w_ref, sem).wait()
     held_ref[:, :SHARD] = lax.dot_general(mixed, w_ref[...], TRANSPOSED, preferred_element_type=F32)
     mods = mods_of(flag_ref, t, send_ref, got_ref).astype(F32)
     gate_first = mods[8:9] + mods[9:10]
@@ -249,12 +253,25 @@
     first = (x_ref[:HALF, :].astype(F32) + gate_first * held_ref[:, :LANES]).astype(BF16)
     made = pair_lanes(low_lanes(QUARTER), held_ref[:QUARTER, LANES:], held_ref[QUARTER:, LANES:])
     rest = x_ref[HALF:, :].astype(F32) + gate_last * made
-    other = pltpu.roll(rest, REST, 1).astype(BF16)
+    other = pltpu.roll(rest, REST, 1)
+    if last:
+        for n in range(SIDE):
+            lines = (rest if n < 2 else other)[(n % 2) * ROWS : (n % 2 + 1) * ROWS]
+            hand_ref[n, :ROWS, :] = first[n * ROWS : (n + 1) * ROWS]
+            both = pair_lanes(low_lanes(ROWS // 2), lines[: ROWS // 2], lines[ROWS // 2 :])
+            hand_ref[n, ROWS:, :] = both.astype(BF16)
+        out = [pltpu.make_async_copy(hand_ref, hand_out_ref, sems.at[1])]
+        out[0].start()
+    else:
+        out = []
+    other = other.astype(BF16)
     rest = rest.astype(BF16)
     for n in range(SIDE):
         at = slice((n % 2) * ROWS, (n % 2 + 1) * ROWS)
         rows_ref[n, :, :LANES] = first[n * ROWS : (n + 1) * ROWS]
         rows_ref[n, :, LANES:] = rest[at] if n < 2 else other[at]
+    out.append(pltpu.make_async_copy(rows_ref, rows_out_ref, sems.at[0]))
+    out[-1].start()
     if not last:
         mods = mods_of(flag_ref, 1, send_ref, got_ref)
         new_ref[:HALF, :] = first
@@ -263,15 +280,8 @@
             spread_ref[s, :HALF, :] = first
             spread_ref[s, HALF:PACK, :] = rest
             spread_ref[s, PACK:, :] = mods
-
-
-def join_kernel(in_ref, out_ref):
-    low = low_lanes(ROWS)
-    for i in range(SIDE):
-        out_ref[:, tile(i)] = in_ref[i, :, :LANES]
-    for m in range(SIDE // 2):
-        even, odd = (in_ref[2 * m + k, :, LANES:].astype(F32) for k in range(2))
-        out_ref[:, tile(SIDE + m)] = pair_lanes(low, even, odd).astype(BF16)
+    for copy in out:
+        copy.wait()
 
 
 def mods_kernel(gathered_ref, out_ref):
@@ -290,16 +300,22 @@
     out_ref[...] = jnp.concatenate(lines, axis=0).astype(BF16)
 
 
-def spread_kernel(low_ref, high_ref, x_ref, out_ref):
-    x_ref[:ROWS, :] = low_ref[...]
-    x_ref[ROWS:, :] = high_ref[...]
-    for s in range(SIDE):
-        out_ref[s, :ROWS, :] = low_ref[...]
-        out_ref[s, ROWS:, :] = high_ref[...]
-
-
-def project_kernel(row_ref, x_ref, mods_ref, w_ref, below_ref, above_ref, *refs):
-    across_low_ref, across_high_ref, q_ref, kv_ref, wm_ref, wr_ref, nm_ref, nr_ref, sems = refs
+def spread_kernel(low_ref, high_ref, out_ref):
+    for s in range(SEQ):
+        out_ref[s, :PIECE, :] = low_ref[s // SIDE]
+        out_ref[s, PIECE:, :] = high_ref[s // SIDE]
+
+
+def unpack(even, odd):
+    low = low_lanes(ROWS // 2)
+    return jnp.concatenate([pair_lanes(low, even, odd), jnp.where(low, pltpu.roll(even, REST, 1), odd)], axis=0)
+
+
+def project_kernel(packed, row_ref, x_ref, mods_ref, w_ref, below_ref, above_ref, *refs):
+    across_low_ref, across_high_ref, q_ref, kv_ref, *refs = refs
+    if packed:
+        keep_out_ref, *refs = refs
+    wm_ref, wr_ref, nm_ref, nr_ref, keep_ref, sems = refs
     i = row_ref[0]
     half = SIDE // 2
     sources = (
@@ -322,12 +338,21 @@
     scale = [m[0:1] + m[1:2] for m in mods]
     shift = [m[2:3] + m[3:4] for m in mods]
     tiles = WIDE // LANES
+
+    def features(g, j, k):
+        if not packed:
+            return x_ref[j, g * ROWS : (g + 1) * ROWS, tile(k)].astype(F32)
+        if k < SIDE:
+            return x_ref[k * SIDE + j, g * PIECE : g * PIECE + ROWS, :].astype(F32)
+        pair = (2 * (k - SIDE) * SIDE + j, (2 * (k - SIDE) + 1) * SIDE + j)
+        return unpack(*(x_ref[s, g * PIECE + ROWS : (g + 1) * PIECE, :].astype(F32) for s in pair))
+
     for g in range(GROUP):
         mine = pl.ds(g * ROWS, ROWS)
         total, square = (jnp.zeros((ROWS, LANES), F32) for _ in range(2))
         for j in range(SIDE):
             for k in range(tiles):
-                x = x_ref[j, mine, tile(k)].astype(F32)
+                x = features(g, j, k)
                 total = total + x
                 square = square + x * x
         mean = jnp.sum(total, axis=1, keepdims=True) / WIDTH
@@ -335,12 +360,18 @@
         rstd = lax.rsqrt(var + EPSILON)
         for j in range(SIDE):
             for k in range(tiles):
-                x = x_ref[j, mine, tile(k)].astype(F32)
+                x = features(g, j, k)
                 normed = ((x - mean) * rstd * scale[j][:, tile(k)] + shift[j][:, tile(k)]).astype(BF16)
                 if k < SIDE:
                     nm_ref[mine, tile(k * SIDE + j)] = normed
                 else:
                     nr_ref[mine, tile(j * (SIDE // 2) + k - SIDE)] = normed
+        if packed:
+            for k in range(tiles):
+                keep_ref[mine, tile(k)] = features(g, row_ref[1], k).astype(BF16)
+    kept = [pltpu.make_async_copy(keep_ref, keep_out_ref, sems.at[len(copies)])] if packed else []
+    for copy in kept:
+        copy.start()
     each = len(copies) // 3
     for t in range(3):
         for copy in copies[t * each : (t + 1) * each]:
@@ -354,10 +385,42 @@
         else:
             for s in range(SIDE):
                 kv_ref[s, :, (t - 1) * HEADS : t * HEADS] = part
-
-
-def attend_kernel(row_ref, order_ref, q_ref, kv_ref, stale_ref, out_ref, low_ref, high_ref):
+    for copy in kept:
+        copy.wait()
+
+
+def load_out(i, w_ref, below_ref, above_ref, across_low_ref, across_high_ref, held_ref, sems):
+    width = SEQ * HEAD_DIM
+    sources = (
+        (w_ref, 0, width, i),
+        (below_ref, 0, width, lax.rem(i + 3, SIDE)),
+        (above_ref, 0, width, lax.rem(i + 1, SIDE)),
+        (across_low_ref, 0, width // 2, lax.rem(i + 2, SIDE)),
+        (across_high_ref, width // 2, width, lax.rem(i + 2, SIDE)),
+    )
+    copies = []
+    for source, begin, end, h in sources:
+        first = pl.ds(pl.multiple_of(h * LANES, LANES), LANES)
+        last = pl.ds(pl.multiple_of(SIDE * LANES + h * REST, REST), REST)
+        for taken, rows in ((slice(0, LANES), first), (slice(LANES, SHARD), last)):
+            held = held_ref.at[rows, begin:end]
+            copies.append(pltpu.make_async_copy(source.at[taken, :], held, sems.at[len(copies)]))
+    return copies
+
+
+def attend_kernel(row_ref, order_ref, q_ref, kv_ref, stale_ref, *refs):
+    *w_refs, out_ref, held_ref, low_ref, high_ref, sems = refs
     i = row_ref[0]
+    copies = load_out(i, *w_refs, held_ref, sems)
+    for part in range(2):
+        lanes = pl.ds(pl.multiple_of(part * HEADS + i * HEAD_DIM, HEAD_DIM), HEAD_DIM)
+        for n in range(SIDE):
+            for half, own_ref in enumerate((low_ref, high_ref)):
+                new = kv_ref.at[n, half * ROWS : (half + 1) * ROWS, lanes]
+                own = own_ref.at[part, n * ROWS : (n + 1) * ROWS, :]
+                copies.append(pltpu.make_async_copy(new, own, sems.at[len(copies)]))
+    for copy in copies:
+        copy.start()
     for pair in range(SIDE // 2):
         where, queries, keys, values = [], [], [], []
         for h in (2 * pair, 2 * pair + 1):
@@ -376,31 +439,17 @@
         for (rows, lanes), mixed in zip(where, softmax_mix(queries, keys, values), strict=True):
             for s in range(SIDE):
                 out_ref[s, rows, lanes] = mixed
-    for part in range(2):
-        lanes = pl.ds(pl.multiple_of(part * HEADS + i * HEAD_DIM, HEAD_DIM), HEAD_DIM)
-        for n in range(SIDE):
-            low_ref[part, n * ROWS : (n + 1) * ROWS, :] = kv_ref[n, :ROWS, lanes]
-            high_ref[part, n * ROWS : (n + 1) * ROWS, :] = kv_ref[n, ROWS:, lanes]
-
-
-def update_kernel(row_ref, mixed_ref, w_ref, below_ref, above_ref, *refs):
-    across_low_ref, across_high_ref, x_ref, mods_ref, out_ref, part_ref, held_ref, sems = refs
-    i = row_ref[0]
-    width = SEQ * HEAD_DIM
-    sources = (
-        (w_ref, 0, width, i),
-        (below_ref, 0, width, lax.rem(i + 3, SIDE)),
-        (above_ref, 0, width, lax.rem(i + 1, SIDE)),
-        (across_low_ref, 0, width // 2, lax.rem(i + 2, SIDE)),
-        (across_high_ref, width // 2, width, lax.rem(i + 2, SIDE)),
-    )
+    for copy in copies:
+        copy.wait()
+
+
+def update_kernel(last, mixed_ref, held_ref, x_in_ref, mods_in_ref, *refs):
+    if not last:
+        out_ref, *refs = refs
+    part_ref, x_ref, mods_ref, made_ref, cut_ref, sems = refs
     copies = []
-    for source, begin, end, h in sources:
-        first = pl.ds(pl.multiple_of(h * LANES, LANES), LANES)
-        last = pl.ds(pl.multiple_of(SIDE * LANES + h * REST, REST), REST)
-        for taken, rows in ((slice(0, LANES), first), (slice(LANES, SHARD), last)):
-            held = held_ref.at[rows, begin:end]
-            copies.append(pltpu.make_async_copy(source.at[taken, :], held, sems.at[len(copies)]))
+    copies.append(pltpu.make_async_copy(x_in_ref, x_ref, sems.at[len(copies)]))
+    copies.append(pltpu.make_async_copy(mods_in_ref, mods_ref, sems.at[len(copies)]))
     for copy in copies:
         copy.start()
     mixed = jnp.concatenate([mixed_ref[h % SIDE, :, tile(h // SIDE)] for h in range(SEQ)], axis=1)
@@ -409,11 +458,19 @@
     made = lax.dot_general(mixed, held_ref[...], TRANSPOSED, preferred_element_type=F32)
     mods = mods_ref[...].astype(F32)
     new = x_ref[...].astype(F32) + (mods[4:5] + mods[5:6]) * made
-    out_ref[...] = new.astype(BF16)
+    out = []
+    if not last:
+        made_ref[...] = new.astype(BF16)
+        out.append(pltpu.make_async_copy(made_ref, out_ref, sems.at[0]))
+        out[0].start()
     for n in range(SIDE):
         rest = new[:, tile(SIDE + n // 2)]
-        part_ref[n, :, :LANES] = new[:, tile(n)].astype(BF16)
-        part_ref[n, :, LANES:] = (rest if n % 2 == 0 else pltpu.roll(rest, REST, 1)).astype(BF16)
+        cut_ref[n, :, :LANES] = new[:, tile(n)].astype(BF16)
+        cut_ref[n, :, LANES:] = (rest if n % 2 == 0 else pltpu.roll(rest, REST, 1)).astype(BF16)
+    out.append(pltpu.make_async_copy(cut_ref, part_ref, sems.at[1]))
+    out[-1].start()
+    for copy in out:
+        copy.wait()
 
 
 def finish_kernel(order_ref, low_ref, high_ref, kv_low_ref, kv_high_ref, out_ref, cache_ref, rows_ref):
@@ -435,14 +492,15 @@
     section = lax.axis_index("section")
     position = section % CHAIN
     core = (section % 2).astype(jnp.int32)
-    row = (lax.axis_index("seq") // SIDE).astype(jnp.int32)[None]
+    seq = lax.axis_index("seq").astype(jnp.int32)
+    row = jnp.stack([seq // SIDE, seq % SIDE])
     w_own = jnp.transpose(w_qkv[0], (1, 0, 2))
     o_own = jnp.transpose(w_out[0], (1, 0))
     cache_own = kv_cache[0]
     mod_now = lax.dynamic_index_in_dim(mod_table, timestep[0], 0, keepdims=False)[0]
 
     def swap(value):
-        return lax.ppermute(value, "section", [(s, s ^ 1) for s in range(sections)])
+        return lax.ppermute(value, "section", [(s, s ^ 1) for s in range(sections) if s % CHAIN < 2])
 
     def exchange(value, groups):
         return lax.all_to_all(value, "seq", 0, 0, axis_index_groups=groups)
@@ -464,7 +522,7 @@
         return exchange(jnp.broadcast_to(value[None], (SIDE,) + value.shape), groups)
 
     rows_shape, kv_shape = shaped(SIDE, ROWS, 2 * LANES), shaped(2, HALF, HEAD_DIM)
-    patch_shape, x_shape, parts_shape = shaped(ROWS, WIDE), shaped(PART, WIDE), shaped(SIDE, PART, 2 * LANES)
+    hand_shape, x_shape, parts_shape = shaped(SIDE, PIECE, LANES), shaped(PART, WIDE), shaped(SIDE, PART, 2 * LANES)
 
     flags = jnp.stack([core == 0, core == 1, core]).astype(jnp.int32)
     flags, mod_now = lax.optimization_barrier((flags, mod_now))
@@ -483,11 +541,12 @@
     got, w_peer, o_peer = swap(send), swap(w_own), swap(o_own)
     got, w_peer, o_peer = lax.optimization_barrier((got, w_peer, o_peer))
 
+    spread_shape = shaped(SIDE, PACK + MODS, LANES)
+
     def first_blocks(own, send, got, w_peer, o_peer):
-        spread_shape = shaped(SIDE, PACK + MODS, LANES)
-        x, spread = call(
-            start_kernel, "start", (shaped(PACK, LANES), spread_shape), [SMEM, VMEM, VMEM, VMEM], flags, own, send, got
-        )
+        shapes = shaped(PACK, LANES), spread_shape
+        x, spread = call(start_kernel, "start", shapes, [SMEM, VMEM, VMEM, VMEM], flags, own, send, got)
+        gathered = gather_mixed(spread)
         kept = []
         for t in range(2):
             q, kv = call(
@@ -496,7 +555,7 @@
                 (shaped(HALF, HEAD_DIM), kv_shape),
                 [SMEM, VMEM, ANY, ANY],
                 flags,
-                gather_mixed(spread),
+                gathered,
                 w_own.reshape(3, SEQ, SHARD, HEAD_DIM),
                 w_peer.reshape(3, SEQ, SHARD, HEAD_DIM),
                 scratch=[
@@ -508,11 +567,11 @@
                 ],
             )
             kv_other = swap(kv)
-            mixed = call(
+            mixed, w_now = call(
                 functools.partial(attend_half_kernel, t),
                 "attend_half",
-                shaped(SIDE, HALF, HEAD_DIM),
-                [SMEM, SMEM, VMEM, VMEM, VMEM, VMEM, VMEM],
+                (shaped(SIDE, HALF, HEAD_DIM), shaped(*o_own.shape)),
+                [SMEM, SMEM, VMEM, VMEM, VMEM, VMEM, VMEM, ANY, ANY],
                 flags,
                 patch_order,
                 q,
@@ -520,45 +579,47 @@
                 kv_other,
                 cache_own,
                 got,
+                o_own,
+                o_peer,
+                scratch=[pltpu.SemaphoreType.DMA],
             )
             heads = gather_mixed(mixed)
             last = t == 1
             results = call(
                 functools.partial(update_half_kernel, t),
                 "update_half",
-                (rows_shape,) + (() if last else (shaped(PACK, LANES), spread_shape)),
-                [SMEM, VMEM, ANY, ANY, VMEM, VMEM, VMEM],
+                (rows_shape,) + ((hand_shape,) if last else (shaped(PACK, LANES), spread_shape)),
+                [SMEM, VMEM, VMEM, VMEM, VMEM, VMEM],
                 flags,
                 heads,
-                o_own,
-                o_peer,
+                w_now,
                 x,
                 send,
                 got,
                 scratch=[
-                    pltpu.VMEM(o_own.shape, BF16),
                     pltpu.VMEM((HALF, 2 * LANES), F32),
-                    pltpu.SemaphoreType.DMA,
+                    pltpu.VMEM(rows_shape.shape, BF16),
+                    pltpu.VMEM(hand_shape.shape, BF16),
+                    pltpu.SemaphoreType.DMA((2,)),
                 ],
+                outside=(0, 1) if last else (0,),
             )
             if not last:
-                x, spread = results[1:]
+                x, gathered = results[1], gather_mixed(results[2])
             kept.append((results[0], kv, kv_other))
-        patch = call(join_kernel, "join", patch_shape, [VMEM], exchange(kept[1][0], ALONG_X))
-        return patch, kept
+        return results[1], kept
 
     half_width = SEQ * HEAD_DIM // 2
 
     def prepare(small):
         w = w_own.reshape(3, SIDE, SIDE, SHARD, HEAD_DIM)
-        w_near = shift(w, 1), shift(w, -1)
-        small = gather(small, ALONG_X)
-        mods = call(mods_kernel, "mods", shaped(MODS, WIDE), [VMEM], small)
-        others = gather(mods, ALONG_Z), small, mods
-        w_near, o, others = lax.optimization_barrier((w_near, o_own, others))
+        w_near, o, small = lax.optimization_barrier(((shift(w, 1), shift(w, -1)), o_own, small))
         w_far = shift(w_near[0][:, : SIDE // 2], 1), shift(w_near[1][:, SIDE // 2 :], -1)
         o_near = shift(o, 1), shift(o, -1)
-        w_far, o_near = lax.optimization_barrier((w_far, o_near))
+        small = gather(small, ALONG_X)
+        mods = call(mods_kernel, "mods", shaped(MODS, WIDE), [VMEM], small, mib=4)
+        others = gather(mods, ALONG_Z), small, mods
+        w_far, o_near, others = lax.optimization_barrier((w_far, o_near, others))
         o_far = shift(o_near[0][:, :half_width], 1), shift(o_near[1][:, half_width:], -1)
         mods_all, small, mods = others
         return w_near + w_far, o_near + o_far, small, mods, mods_all
@@ -571,14 +632,15 @@
         made = blank(*shapes)
         return tuple(made[:4]), tuple(made[4:8]), *made[8:]
 
-    def later_block(x, spread, w_others, o_others, small, mods, mods_all):
-        q, kv = call(
-            project_kernel,
+    def later_block(x, gathered, w_others, o_others, small, mods, mods_all):
+        packed = x is None
+        q, kv, *keep = call(
+            functools.partial(project_kernel, packed),
             "project",
-            (shaped(PART, HEADS), shaped(SIDE, PART, 2 * HEADS)),
+            (shaped(PART, HEADS), shaped(SIDE, PART, 2 * HEADS)) + (x_shape,) * packed,
             [SMEM, VMEM, VMEM] + [ANY] * 5,
             row,
-            exchange(spread, ALONG_Z),
+            gathered,
             mods_all,
             w_own.reshape(3, SIDE, SIDE, SHARD, HEAD_DIM),
             *w_others,
@@ -587,56 +649,67 @@
                 pltpu.VMEM((SIDE, SIDE, REST, 3 * HEADS), BF16),
                 pltpu.VMEM((PART, SEQ * LANES), BF16),
                 pltpu.VMEM((PART, SEQ * REST), BF16),
-                pltpu.SemaphoreType.DMA((75,)),
+                pltpu.VMEM(x_shape.shape, BF16),
+                pltpu.SemaphoreType.DMA((76,)),
             ],
+            outside=(2,),
             mib=20,
         )
-        mixed, kv_low, kv_high = call(
+        x = keep[0] if packed else x
+        mixed, held, kv_low, kv_high = call(
             attend_kernel,
             "attend",
-            (shaped(SIDE, PART, HEADS), kv_shape, kv_shape),
-            [SMEM, SMEM, VMEM, VMEM, VMEM],
+            (shaped(SIDE, PART, HEADS), shaped(WIDE, SEQ * HEAD_DIM), kv_shape, kv_shape),
+            [SMEM, SMEM, VMEM, VMEM, VMEM] + [ANY] * 5,
             row,
             patch_order,
             q,
             exchange(kv, ALONG_X),
             small,
-        )
-        new, parts = call(
-            update_kernel,
-            "update",
-            (x_shape, parts_shape),
-            [SMEM, VMEM] + [ANY] * 5 + [VMEM, VMEM],
-            row,
-            exchange(mixed, ALONG_Z),
             o_own,
             *o_others,
+            scratch=[pltpu.SemaphoreType.DMA((26,))],
+            outside=(2, 3),
+        )
+        made = call(
+            functools.partial(update_kernel, not packed),
+            "update",
+            (x_shape,) * packed + (parts_shape,),
+            [VMEM, VMEM, ANY, ANY],
+            exchange(mixed, ALONG_Z),
+            held,
             x,
             mods,
-            scratch=[pltpu.VMEM((WIDE, SEQ * HEAD_DIM), BF16), pltpu.SemaphoreType.DMA((10,))],
+            scratch=[
+                pltpu.VMEM(x_shape.shape, BF16),
+                pltpu.VMEM((MODS, WIDE), BF16),
+                pltpu.VMEM(x_shape.shape, BF16),
+                pltpu.VMEM(parts_shape.shape, BF16),
+                pltpu.SemaphoreType.DMA((2,)),
+            ],
+            outside=(0, 1),
         )
-        return new, parts, kv_low, kv_high
+        return *made, kv_low, kv_high
 
     def second_block(low, high, weights):
-        spread_shape = shaped(SIDE, PART, WIDE)
-        x, spread = call(spread_kernel, "spread", (x_shape, spread_shape), [VMEM, VMEM], low, high)
-        return later_block(x, spread, *weights)
+        spread = call(spread_kernel, "spread", shaped(SEQ, 2 * PIECE, LANES), [VMEM, VMEM], low, high)
+        return later_block(None, lax.all_to_all(spread, "seq", 0, 0), *weights)
 
     def third_block(x, weights):
-        return later_block(x, jnp.broadcast_to(x[None], (SIDE,) + x.shape), *weights)
+        return later_block(x, gather(x, ALONG_Z), *weights)
 
     early = position < 2
     one = (rows_shape, kv_shape, kv_shape)
 
     def not_here(*_):
-        patch, *both = blank(patch_shape, *one, *one)
-        return patch, [tuple(both[:3]), tuple(both[3:])]
-
-    patch, kept = lax.cond(early, first_blocks, not_here, own, send, got, w_peer, o_peer)
+        hand, *both = blank(hand_shape, *one, *one)
+        return hand, [tuple(both[:3]), tuple(both[3:])]
+
+    hand, kept = lax.cond(early, first_blocks, not_here, own, send, got, w_peer, o_peer)
     weights = lax.cond(early, no_weights, prepare, send[PACK:])
-    patch, weights = lax.optimization_barrier((patch, weights))
-    low = lax.ppermute(patch, "section", [(s, s + 2) for s in range(sections) if s % CHAIN == 0])
-    high = lax.ppermute(patch, "section", [(s, s + 1) for s in range(sections) if s % CHAIN == 1])
+    hand, weights = lax.optimization_barrier((hand, weights))
+    low = lax.ppermute(hand, "section", [(s, s + 2) for s in range(sections) if s % CHAIN == 0])
+    high = lax.ppermute(hand, "section", [(s, s + 1) for s in range(sections) if s % CHAIN == 1])
     state = blank(x_shape, parts_shape, kv_shape, kv_shape)
     state = lax.cond(
         position == 2,
@@ -650,7 +723,7 @@
     arrived = lax.ppermute(state[0], "section", [(s, s + 1) for s in range(sections) if s % CHAIN == 2])
     state = lax.cond(
         position == 3,
-        lambda x, state, weights: third_block(x, weights)[1:],
+        lambda x, state, weights: third_block(x, weights),
         lambda x, state, weights: tuple(state),
         arrived,
         tuple(state[1:]),

time: 290 us -> 286 us (0.986)
  blocking collectives: 126 us -> 49 us
  waiting for transfers between devices: 104 us -> 166 us
  starting transfers between devices: 40.7 us -> 46 us
  local copies, waits for them, and re-layouts: 3.25 us -> 8.26 us
    all_to_all x6 -> x4, blocking collectives: 126 us -> 49 us  [exchange(): return lax.all_to_all(value, 'seq', 0, 0, axis_index_groups=groups)]
    ppermute x8, waiting for transfers between devices: 37.6 us -> 65.6 us  [shift(): return lax.ppermute(value, 'seq', pairs)]
    all_to_all x0 -> x2, waiting for transfers between devices: none -> 22.5 us  [exchange(): return lax.all_to_all(value, 'seq', 0, 0, axis_index_groups=groups)]
    ppermute x1, waiting for transfers between devices: 64.3 us -> 77.6 us  [body(): lax.ppermute(state[0], 'section', [(s, s + 1) for s in range(sections) if...]
    all_to_all x0 -> x2, starting transfers between devices: none -> 12.6 us  [exchange(): return lax.all_to_all(value, 'seq', 0, 0, axis_index_groups=groups)]
    ppermute x5, starting transfers between devices: 13 us -> 5.8 us  [the longest x3 4.29 us: swap(): lax.ppermute(value, 'section', [(s, s ^ 1) for s in range(sections) if s...]
  transfers between devices with their start and end apart: 14 -> 16, of which waited for: 6 -> 8; matrix products, arithmetic and copies ran while one was open for 0% -> 2% of each run, Pallas kernels for 0% -> 0%
where the time goes in v4:
time: 286 us; the launch traced here: 285 us
  waiting for transfers between devices  166 us (58%)
  blocking collectives  49 us (17%)
  starting transfers between devices  46 us (16%)
  Pallas kernels  14.1 us (5%)
  local copies, waits for them, and re-layouts  8.26 us (3%)
    ppermute x1, waiting for transfers between devices, body(): lax.ppermute(state[0], 'section', [(s, s + 1) for s in range(sections) if...  77.6 us
    ppermute x8, waiting for transfers between devices, shift(): return lax.ppermute(value, 'seq', pairs)  65.6 us
    all_to_all x4, blocking collectives, exchange(): return lax.all_to_all(value, 'seq', 0, 0, axis_index_groups=groups)  49 us
    ppermute x8, starting transfers between devices, shift(): return lax.ppermute(value, 'seq', pairs)  26.3 us
    all_to_all x2, waiting for transfers between devices, exchange(): return lax.all_to_all(value, 'seq', 0, 0, axis_index_groups=groups)  22.5 us
    pallas_call x6, Pallas kernels, call(): pl.pallas_call(kernel, out_shape=out_shape, in_specs=in_specs, out_specs=...  14.1 us
    all_to_all x2, starting transfers between devices, exchange(): return lax.all_to_all(value, 'seq', 0, 0, axis_index_groups=groups)  12.6 us
  transfers between devices with their start and end apart: 16, of which 8 were waited for; matrix products, arithmetic and copies ran while one was open for 2% of the time, Pallas kernels for 0%

profile of v4, /device:TPU:65, one launch (start us, length us, event | category | flops | bytes accessed | tf_op | source)
XLA Modules:
  0.0 284.9 jit_solution(6407096477659242944)
XLA Ops:
  2.6 1.8 pack.1
  4.4 2.1 collective-permute-start.12
  6.5 134.1 %conditional.6 = ((bf16[3,4,4,192,128]{4,3,2,1,0:T(8,128)(2,1)}, bf16[3,4,4,192,128]{4,3,2,1,0:T(8,128)(2,1)}, bf16[3,2,4,192,128]{4,3,2,1,0:T(8,128)(2,1)}, bf1...) conditional(s32[]{:T(128)} %convert_element_type.6, ...), branch_computations={%region_2.3_spmd, %region_3.4_spmd} | conditional | bytes 74682984 | solution.py:709
  6.5 3.2 %collective-permute-start.2 = (bf16[3,4,4,192,128]{4,3,2,1,0:T(8,128)(2,1)}, bf16[3,4,4,192,128]{4,3,2,1,0:T(8,128)(2,1)S(1)}, u32[]{:S(2)}, u32[]{:S(2)}) collective-permute-start(bf16[3,4,4,192,128]{4,3,2,1,0:T(8,128)(2,1)} %bitcast.46), channel_id=1, source_target_pairs={{0,4},{1,5},{2,6},{3,7},{4,8},{5,9},{6,10},{7,11},{8,12},{9,13},{1... | collective-permute-start | bytes 7077896 | tf_op jit(solution)/shard_map/cond/branch_0_fun/ppermute | solution.py:510
  9.7 3.4 %collective-permute-start.3 = (bf16[3,4,4,192,128]{4,3,2,1,0:T(8,128)(2,1)}, bf16[3,4,4,192,128]{4,3,2,1,0:T(8,128)(2,1)S(1)}, u32[]{:S(2)}, u32[]{:S(2)}) collective-permute-start(bf16[3,4,4,192,128]{4,3,2,1,0:T(8,128)(2,1)} %bitcast.47), channel_id=1, source_target_pairs={{0,12},{1,13},{2,14},{3,15},{4,0},{5,1},{6,2},{7,3},{8,4},{9,5},{1... | collective-permute-start | bytes 7077896 | tf_op jit(solution)/shard_map/cond/branch_0_fun/ppermute | solution.py:510
  13.2 48.9 %collective-permute-done.2 = bf16[3,4,4,192,128]{4,3,2,1,0:T(8,128)(2,1)S(1)} collective-permute-done((bf16[3,4,4,192,128]{4,3,2,1,0:T(8,128)(2,1)}, bf16[3,4,4,192,128]{4,3,2,1,0:T(8,128)(2,1)S(1)}, u32[]{:S(2)}, u32[]{:S(2)}) %collective-permute-start.2) | collective-permute-done | bytes 2359328 | tf_op jit(solution)/shard_map/cond/branch_0_fun/ppermute | solution.py:510
  62.0 1.6 collective-permute-done.3
  64.9 3.1 %collective-permute-start.4 = (bf16[3,2,4,192,128]{4,3,2,1,0:T(8,128)(2,1)}, bf16[3,2,4,192,128]{4,3,2,1,0:T(8,128)(2,1)}, u32[]{:S(2)}, u32[]{:S(2)}) collective-permute-start(bf16[3,2,4,192,128]{4,3,2,1,0:T(8,128)(2,1)} %slice.16), channel_id=1, source_target_pairs={{0,4},{1,5},{2,6},{3,7},{4,8},{5,9},{6,10},{7,11},{8,12},{9,13},{1... | collective-permute-start | bytes 3538952 | tf_op jit(solution)/shard_map/cond/branch_0_fun/ppermute | solution.py:510
  69.1 3.5 %collective-permute-start.5 = (bf16[3,2,4,192,128]{4,3,2,1,0:T(8,128)(2,1)}, bf16[3,2,4,192,128]{4,3,2,1,0:T(8,128)(2,1)}, u32[]{:S(2)}, u32[]{:S(2)}) collective-permute-start(bf16[3,2,4,192,128]{4,3,2,1,0:T(8,128)(2,1)} %slice.17), channel_id=1, source_target_pairs={{0,12},{1,13},{2,14},{3,15},{4,0},{5,1},{6,2},{7,3},{8,4},{9,5},{1... | collective-permute-start | bytes 3538952 | tf_op jit(solution)/shard_map/cond/branch_0_fun/ppermute | solution.py:510
  73.8 3.5 %all-to-all-start.8 = ((bf16[4,1040,128]{2,1,0:T(8,128)(2,1)}), bf16[4,1040,128]{2,1,0:T(8,128)(2,1)S(1)}, u32[]{:S(2)}, u32[]{:S(2)}) async-start(bf16[4,1040,128]{2,1,0:T(8,128)(2,1)} %broadcast_in_dim.12), calls=%async_computation.8 | async-start | bytes 2129920 | tf_op jit(solution)/shard_map/cond/branch_0_fun/all_to_all | solution.py:506
  77.4 3.3 %collective-permute-start.6 = (bf16[192,2048]{1,0:T(8,128)(2,1)S(1)}, bf16[192,2048]{1,0:T(8,128)(2,1)}, u32[]{:S(2)}, u32[]{:S(2)}) collective-permute-start(bf16[192,2048]{1,0:T(8,128)(2,1)S(1)} %copy-done.8), channel_id=1, source_target_pairs={{0,4},{1,5},{2,6},{3,7},{4,8},{5,9},{6,10},{7,11},{8,12},{9,13},{1... | collective-permute-start | bytes 2359304 | tf_op jit(solution)/shard_map/cond/branch_0_fun/ppermute | solution.py:510
  80.7 3.2 %collective-permute-start.7 = (bf16[192,2048]{1,0:T(8,128)(2,1)S(1)}, bf16[192,2048]{1,0:T(8,128)(2,1)}, u32[]{:S(2)}, u32[]{:S(2)}) collective-permute-start(bf16[192,2048]{1,0:T(8,128)(2,1)S(1)} %copy-done.8), channel_id=1, source_target_pairs={{0,12},{1,13},{2,14},{3,15},{4,0},{5,1},{6,2},{7,3},{8,4},{9,5},{1... | collective-permute-start | bytes 2359304 | tf_op jit(solution)/shard_map/cond/branch_0_fun/ppermute | solution.py:510
  83.9 22.5 %all-to-all-done.8.gathered_ref = bf16[4,1040,128]{2,1,0:T(8,128)(2,1)S(1)} async-done(((bf16[4,1040,128]{2,1,0:T(8,128)(2,1)}), bf16[4,1040,128]{2,1,0:T(8,128)(2,1)S(1)}, u32[]{:S(2)}, u32[]{:S(2)}) %all-to-all-start.8) | async-done | bytes 1064992 | tf_op jit(solution)/shard_map/cond/branch_0_fun/all_to_all | solution.py:506
  107.0 9.1 %all-to-all-start.9 = ((bf16[4,16,768]{2,1,0:T(8,128)(2,1)}), bf16[4,16,768]{2,1,0:T(8,128)(2,1)}, u32[]{:S(2)}, u32[]{:S(2)}) async-start(bf16[4,16,768]{2,1,0:T(8,128)(2,1)} %broadcast_in_dim.14), calls=%async_computation.9 | async-start | bytes 196608 | tf_op jit(solution)/shard_map/cond/branch_0_fun/all_to_all | solution.py:506
  116.1 6.0 %collective-permute-done.6 = bf16[192,2048]{1,0:T(8,128)(2,1)} collective-permute-done((bf16[192,2048]{1,0:T(8,128)(2,1)S(1)}, bf16[192,2048]{1,0:T(8,128)(2,1)}, u32[]{:S(2)}, u32[]{:S(2)}) %collective-permute-start.6) | collective-permute-done | bytes 786464 | tf_op jit(solution)/shard_map/cond/branch_0_fun/ppermute | solution.py:510
  122.1 2.9 %collective-permute-done.7 = bf16[192,2048]{1,0:T(8,128)(2,1)} collective-permute-done((bf16[192,2048]{1,0:T(8,128)(2,1)S(1)}, bf16[192,2048]{1,0:T(8,128)(2,1)}, u32[]{:S(2)}, u32[]{:S(2)}) %collective-permute-start.7) | collective-permute-done | bytes 786464 | tf_op jit(solution)/shard_map/cond/branch_0_fun/ppermute | solution.py:510
  126.1 3.9 %collective-permute-start.8 = (bf16[192,1024]{1,0:T(8,128)(2,1)S(1)}, bf16[192,1024]{1,0:T(8,128)(2,1)S(1)}, u32[]{:S(2)}, u32[]{:S(2)}) collective-permute-start(bf16[192,1024]{1,0:T(8,128)(2,1)S(1)} %slice.18), channel_id=1, source_target_pairs={{0,4},{1,5},{2,6},{3,7},{4,8},{5,9},{6,10},{7,11},{8,12},{9,13},{1... | collective-permute-start | bytes 1179656 | tf_op jit(solution)/shard_map/cond/branch_0_fun/ppermute | solution.py:510
  131.1 2.6 collective-permute-start.9
  133.6 2.2 collective-permute-done.8
  135.8 4.0 %collective-permute-done.9 = bf16[192,1024]{1,0:T(8,128)(2,1)S(1)} collective-permute-done((bf16[192,1024]{1,0:T(8,128)(2,1)S(1)}, bf16[192,1024]{1,0:T(8,128)(2,1)S(1)}, u32[]{:S(2)}, u32[]{:S(2)}) %collective-permute-start.9) | collective-permute-done | bytes 393248 | tf_op jit(solution)/shard_map/cond/branch_0_fun/ppermute | solution.py:510
  140.6 1.5 collective-permute-start.13
  145.9 77.6 %collective-permute-done.16 = bf16[128,768]{1,0:T(8,128)(2,1)S(1)} collective-permute-done((bf16[128,768]{1,0:T(8,128)(2,1)}, bf16[128,768]{1,0:T(8,128)(2,1)S(1)}, u32[]{:S(2)}, u32[]{:S(2)}) %collective-permute-start.16) | collective-permute-done | bytes 196640 | tf_op jit(solution)/shard_map/ppermute | solution.py:723
  223.5 50.6 %conditional.8 = ((bf16[4,128,256]{2,1,0:T(8,128)(2,1)}, bf16[2,256,128]{2,1,0:T(8,128)(2,1)}, bf16[2,256,128]{2,1,0:T(8,128)(2,1)})) conditional(s32[]{:T(128)} %convert_element_type.14, (bf16[4,128,256]{2,1,0:T(8,128)(2,1)}, bf16[2,256,128]{2,1,0:T(8,128)(2,1)}, bf16[2,256,128]{2,1,0:T(8,128)(2,1)}) %tuple.57, (bf16[128,768]{1,0:T(8,128)(2,1)S(1)}, ...), branch_computations={%region_6.7_spmd, %region_7.8_spmd} | conditional | bytes 18284660 | solution.py:724
  223.6 15.0 %all_to_all.79.x_ref = bf16[4,128,768]{2,1,0:T(8,128)(2,1)S(1)} all-to-all(bf16[4,128,768]{2,1,0:T(8,128)(2,1)S(1)} %broadcast_in_dim.15), channel_id=1, replica_groups={{0,1,2,3},{4,5,6,7},{8,9,10,11},{12,13,14,15},{16,17,18,19},{20,21,22,2..., dimensions={0} | all-to-all | bytes 1572864 | tf_op jit(solution)/shard_map/cond/branch_1_fun/all_to_all | solution.py:506
  238.6 5.4 %project.3 = (bf16[128,512]{1,0:T(8,128)(2,1)S(1)}, bf16[4,128,1024]{2,1,0:T(8,128)(2,1)S(1)}) custom-call(s32[2]{0:T(128)S(1)} %get-tuple-element.192.row_ref, bf16[4,128,768]{2,1,0:T(8,128)(2,1)S(1)} %all_to_all.79.x_ref, bf16[4,16,768]{2,1,0:T(8,128)(2,1)} %get-tuple-element.195.mods_ref, bf16[3,4,4,192,128]{4,3,2,1,0:T(8,128)(2,1)S(1)} %bitcast.51, ...), custom_call_target="tpu_custom_call" | custom-call | tf_op jit(solution)/shard_map/cond/branch_1_fun/project/pallas_call | solution.py:50
  244.0 12.3 %all_to_all.80.kv_ref = bf16[4,128,1024]{2,1,0:T(8,128)(2,1)S(1)} all-to-all(bf16[4,128,1024]{2,1,0:T(8,128)(2,1)S(1)} %get-tuple-element.202), channel_id=1, replica_groups={{0,4,8,12},{1,5,9,13},{2,6,10,14},{3,7,11,15},{16,20,24,28},{17,21,25,2..., dimensions={0} | all-to-all | bytes 2097152 | tf_op jit(solution)/shard_map/cond/branch_1_fun/all_to_all | solution.py:506
  256.3 2.7 attend.3
  259.1 12.8 %all_to_all.81.mixed_ref = bf16[4,128,512]{2,1,0:T(8,128)(2,1)S(1)} all-to-all(bf16[4,128,512]{2,1,0:T(8,128)(2,1)S(1)} %get-tuple-element.209), channel_id=1, replica_groups={{0,1,2,3},{4,5,6,7},{8,9,10,11},{12,13,14,15},{16,17,18,19},{20,21,22,2..., dimensions={0} | all-to-all | bytes 1048576 | tf_op jit(solution)/shard_map/cond/branch_1_fun/all_to_all | solution.py:506
  271.9 2.2 update.3
  274.1 8.9 %conditional.9 = (bf16[4,64,256]{2,1,0:T(8,128)(2,1)S(1)}, bf16[4,64,256]{2,1,0:T(8,128)(2,1)S(1)}, bf16[2,256,128]{2,1,0:T(8,128)(2,1)}, bf16[2,256,128]{2,1,0:T(8,128)(2,1)}) conditional(s32[]{:T(128)} %convert_element_type.6, (bf16[4,128,256]{2,1,0:T(8,128)(2,1)}, bf16[2,256,128]{2,1,0:T(8,128)(2,1)}, ...), branch_computations={%region_8.9_spmd, %region_9.10_spmd} | conditional | flops 393217 | bytes 2359380 | solution.py:746
  274.1 8.9 %all_to_all.82 = bf16[4,128,256]{2,1,0:T(8,128)(2,1)S(1)} all-to-all(bf16[4,128,256]{2,1,0:T(8,128)(2,1)} %get-tuple-element.214), channel_id=1, replica_groups={{0,4,8,12},{1,5,9,13},{2,6,10,14},{3,7,11,15},{16,20,24,28},{17,21,25,2..., dimensions={0} | all-to-all | bytes 524288 | tf_op jit(solution)/shard_map/cond/branch_0_fun/all_to_all | solution.py:506
  283.1 1.8 finish.1
  (56 shorter events, 12.0 us)
Async XLA Ops:
  0.6 0.9 copy-start
  1.7 0.9 copy-start.1
  4.4 138.5 %collective-permute-start.12 = (bf16[3,3072,128]{2,1,0:T(8,128)(2,1)}, bf16[3,3072,128]{2,1,0:T(8,128)(2,1)}, u32[]{:S(2)}, u32[]{:S(2)}) collective-permute-start(bf16[3,3072,128]{2,1,0:T(8,128)(2,1)} %bitcast.41), channel_id=1, source_target_pairs={{0,16},{16,0},{64,80},{80,64},{128,144},{144,128},{192,208},{208,1... | collective-permute-start | bytes 7077896 | tf_op jit(solution)/shard_map/ppermute | solution.py:503
  6.5 136.4 %copy-start.7 = (bf16[1,2048,192]{1,2,0:T(8,128)(2,1)S(1)}, bf16[1,2048,192]{1,2,0:T(8,128)(2,1)}, u32[]{:S(2)}) copy-start(bf16[1,2048,192]{1,2,0:T(8,128)(2,1)} %param.22) | copy-start | bytes 2359300
  6.5 136.4 %copy-start.9 = (bf16[1,2,512,128]{3,2,1,0:T(8,128)(2,1)S(1)}, bf16[1,2,512,128]{3,2,1,0:T(8,128)(2,1)}, u32[]{:S(2)}) copy-start(bf16[1,2,512,128]{3,2,1,0:T(8,128)(2,1)} %param.23) | copy-start | bytes 786436
  6.5 136.5 %copy-start.16 = (s32[8]{0:T(128)S(1)}, s32[8]{0:T(128)}, u32[]{:S(2)}) copy-start(s32[8]{0:T(128)} %order_ref.3) | copy-start | bytes 100
  6.5 55.6 %collective-permute-start.2 = (bf16[3,4,4,192,128]{4,3,2,1,0:T(8,128)(2,1)}, bf16[3,4,4,192,128]{4,3,2,1,0:T(8,128)(2,1)S(1)}, u32[]{:S(2)}, u32[]{:S(2)}) collective-permute-start(bf16[3,4,4,192,128]{4,3,2,1,0:T(8,128)(2,1)} %bitcast.46), channel_id=1, source_target_pairs={{0,4},{1,5},{2,6},{3,7},{4,8},{5,9},{6,10},{7,11},{8,12},{9,13},{1... | collective-permute-start | bytes 7077896 | tf_op jit(solution)/shard_map/cond/branch_0_fun/ppermute | solution.py:510
  9.7 53.9 %collective-permute-start.3 = (bf16[3,4,4,192,128]{4,3,2,1,0:T(8,128)(2,1)}, bf16[3,4,4,192,128]{4,3,2,1,0:T(8,128)(2,1)S(1)}, u32[]{:S(2)}, u32[]{:S(2)}) collective-permute-start(bf16[3,4,4,192,128]{4,3,2,1,0:T(8,128)(2,1)} %bitcast.47), channel_id=1, source_target_pairs={{0,12},{1,13},{2,14},{3,15},{4,0},{5,1},{6,2},{7,3},{8,4},{9,5},{1... | collective-permute-start | bytes 7077896 | tf_op jit(solution)/shard_map/cond/branch_0_fun/ppermute | solution.py:510
  62.0 7.1 %copy-start.5 = (bf16[3,4,4,192,128]{4,3,2,1,0:T(8,128)(2,1)}, bf16[3,4,4,192,128]{4,3,2,1,0:T(8,128)(2,1)S(1)}, u32[]{:S(2)}) copy-start(bf16[3,4,4,192,128]{4,3,2,1,0:T(8,128)(2,1)S(1)} %collective-permute-done.2) | copy-start | bytes 7077892 | tf_op jit(solution)/shard_map/cond
  63.6 5.5 %copy-start.6 = (bf16[3,4,4,192,128]{4,3,2,1,0:T(8,128)(2,1)}, bf16[3,4,4,192,128]{4,3,2,1,0:T(8,128)(2,1)S(1)}, u32[]{:S(2)}) copy-start(bf16[3,4,4,192,128]{4,3,2,1,0:T(8,128)(2,1)S(1)} %collective-permute-done.3) | copy-start | bytes 7077892 | tf_op jit(solution)/shard_map/cond
  64.9 60.2 %collective-permute-start.4 = (bf16[3,2,4,192,128]{4,3,2,1,0:T(8,128)(2,1)}, bf16[3,2,4,192,128]{4,3,2,1,0:T(8,128)(2,1)}, u32[]{:S(2)}, u32[]{:S(2)}) collective-permute-start(bf16[3,2,4,192,128]{4,3,2,1,0:T(8,128)(2,1)} %slice.16), channel_id=1, source_target_pairs={{0,4},{1,5},{2,6},{3,7},{4,8},{5,9},{6,10},{7,11},{8,12},{9,13},{1... | collective-permute-start | bytes 3538952 | tf_op jit(solution)/shard_map/cond/branch_0_fun/ppermute | solution.py:510
  69.1 8.2 %copy-start.8 = (bf16[192,2048]{1,0:T(8,128)(2,1)S(1)}, bf16[192,2048]{1,0:T(8,128)(2,1)}, u32[]{:S(2)}) copy-start(bf16[192,2048]{1,0:T(8,128)(2,1)} %get-tuple-element.157) | copy-start | bytes 2359300 | tf_op jit(solution)/shard_map/cond
  69.1 55.9 %collective-permute-start.5 = (bf16[3,2,4,192,128]{4,3,2,1,0:T(8,128)(2,1)}, bf16[3,2,4,192,128]{4,3,2,1,0:T(8,128)(2,1)}, u32[]{:S(2)}, u32[]{:S(2)}) collective-permute-start(bf16[3,2,4,192,128]{4,3,2,1,0:T(8,128)(2,1)} %slice.17), channel_id=1, source_target_pairs={{0,12},{1,13},{2,14},{3,15},{4,0},{5,1},{6,2},{7,3},{8,4},{9,5},{1... | collective-permute-start | bytes 3538952 | tf_op jit(solution)/shard_map/cond/branch_0_fun/ppermute | solution.py:510
  73.8 32.5 %all-to-all-start.8 = ((bf16[4,1040,128]{2,1,0:T(8,128)(2,1)}), bf16[4,1040,128]{2,1,0:T(8,128)(2,1)S(1)}, u32[]{:S(2)}, u32[]{:S(2)}) async-start(bf16[4,1040,128]{2,1,0:T(8,128)(2,1)} %broadcast_in_dim.12), calls=%async_computation.8 | async-start | bytes 2129920 | tf_op jit(solution)/shard_map/cond/branch_0_fun/all_to_all | solution.py:506
  77.4 44.8 %collective-permute-start.6 = (bf16[192,2048]{1,0:T(8,128)(2,1)S(1)}, bf16[192,2048]{1,0:T(8,128)(2,1)}, u32[]{:S(2)}, u32[]{:S(2)}) collective-permute-start(bf16[192,2048]{1,0:T(8,128)(2,1)S(1)} %copy-done.8), channel_id=1, source_target_pairs={{0,4},{1,5},{2,6},{3,7},{4,8},{5,9},{6,10},{7,11},{8,12},{9,13},{1... | collective-permute-start | bytes 2359304 | tf_op jit(solution)/shard_map/cond/branch_0_fun/ppermute | solution.py:510
  80.7 44.4 %collective-permute-start.7 = (bf16[192,2048]{1,0:T(8,128)(2,1)S(1)}, bf16[192,2048]{1,0:T(8,128)(2,1)}, u32[]{:S(2)}, u32[]{:S(2)}) collective-permute-start(bf16[192,2048]{1,0:T(8,128)(2,1)S(1)} %copy-done.8), channel_id=1, source_target_pairs={{0,12},{1,13},{2,14},{3,15},{4,0},{5,1},{6,2},{7,3},{8,4},{9,5},{1... | collective-permute-start | bytes 2359304 | tf_op jit(solution)/shard_map/cond/branch_0_fun/ppermute | solution.py:510
  107.0 18.0 %all-to-all-start.9 = ((bf16[4,16,768]{2,1,0:T(8,128)(2,1)}), bf16[4,16,768]{2,1,0:T(8,128)(2,1)}, u32[]{:S(2)}, u32[]{:S(2)}) async-start(bf16[4,16,768]{2,1,0:T(8,128)(2,1)} %broadcast_in_dim.14), calls=%async_computation.9 | async-start | bytes 196608 | tf_op jit(solution)/shard_map/cond/branch_0_fun/all_to_all | solution.py:506
  126.1 9.8 %collective-permute-start.8 = (bf16[192,1024]{1,0:T(8,128)(2,1)S(1)}, bf16[192,1024]{1,0:T(8,128)(2,1)S(1)}, u32[]{:S(2)}, u32[]{:S(2)}) collective-permute-start(bf16[192,1024]{1,0:T(8,128)(2,1)S(1)} %slice.18), channel_id=1, source_target_pairs={{0,4},{1,5},{2,6},{3,7},{4,8},{5,9},{6,10},{7,11},{8,12},{9,13},{1... | collective-permute-start | bytes 1179656 | tf_op jit(solution)/shard_map/cond/branch_0_fun/ppermute | solution.py:510
  131.1 8.8 %collective-permute-start.9 = (bf16[192,1024]{1,0:T(8,128)(2,1)S(1)}, bf16[192,1024]{1,0:T(8,128)(2,1)S(1)}, u32[]{:S(2)}, u32[]{:S(2)}) collective-permute-start(bf16[192,1024]{1,0:T(8,128)(2,1)S(1)} %slice.19), channel_id=1, source_target_pairs={{0,12},{1,13},{2,14},{3,15},{4,0},{5,1},{6,2},{7,3},{8,4},{9,5},{1... | collective-permute-start | bytes 1179656 | tf_op jit(solution)/shard_map/cond/branch_0_fun/ppermute | solution.py:510
  135.8 4.0 %copy-start.10 = (bf16[192,1024]{1,0:T(8,128)(2,1)}, bf16[192,1024]{1,0:T(8,128)(2,1)S(1)}, u32[]{:S(2)}) copy-start(bf16[192,1024]{1,0:T(8,128)(2,1)S(1)} %collective-permute-done.8) | copy-start | bytes 1179652 | tf_op jit(solution)/shard_map/cond
  139.9 0.7 copy-start.13
  140.6 2.3 collective-permute-start.13
  142.2 0.7 collective-permute-start.11
  143.0 1.6 collective-permute-start.14
  143.8 0.8 collective-permute-start.15
  144.6 78.9 %collective-permute-start.16 = (bf16[128,768]{1,0:T(8,128)(2,1)}, bf16[128,768]{1,0:T(8,128)(2,1)S(1)}, u32[]{:S(2)}, u32[]{:S(2)}) collective-permute-start(bf16[128,768]{1,0:T(8,128)(2,1)} %get-tuple-element.315), channel_id=1, source_target_pairs={{32,48},{96,112},{160,176},{224,240},{288,304},{352,368},{416,432}... | collective-permute-start | bytes 589832 | tf_op jit(solution)/shard_map/ppermute | solution.py:723
  223.5 15.1 %copy-start.4 = (bf16[3,3072,128]{2,1,0:T(8,128)(2,1)S(1)}, bf16[3,3072,128]{2,1,0:T(8,128)(2,1)}, u32[]{:S(2)}) copy-start(bf16[3,3072,128]{2,1,0:T(8,128)(2,1)} %get-tuple-element.196) | copy-start | bytes 7077892 | tf_op jit(solution)/shard_map/cond
  244.0 12.3 %copy-start.12 = (bf16[192,1024]{1,0:T(8,128)(2,1)S(1)}, bf16[192,1024]{1,0:T(8,128)(2,1)}, u32[]{:S(2)}) copy-start(bf16[192,1024]{1,0:T(8,128)(2,1)} %get-tuple-element.207.refs_3_) | copy-start | bytes 1179652 | tf_op jit(solution)/shard_map/cond
  244.0 12.3 %copy-start.15 = (bf16[192,1024]{1,0:T(8,128)(2,1)S(1)}, bf16[192,1024]{1,0:T(8,128)(2,1)}, u32[]{:S(2)}) copy-start(bf16[192,1024]{1,0:T(8,128)(2,1)} %get-tuple-element.208.refs_4_) | copy-start | bytes 1179652 | tf_op jit(solution)/shard_map/cond

commit v5 on v4

--- a/solution.py
+++ b/solution.py
@@ -204,7 +204,11 @@
 
 
 def attend_half_kernel(t, flag_ref, order_ref, q_ref, kv_ref, other_ref, own_ref, got_ref, *refs):
-    o_own_ref, o_peer_ref, out_ref, w_ref, sem = refs
+    o_own_ref, o_peer_ref, out_ref, w_ref, kv_out_ref, other_out_ref, sem, sems = refs
+    leaving = [pltpu.make_async_copy(kv_ref, kv_out_ref, sems.at[0])]
+    leaving.append(pltpu.make_async_copy(other_ref, other_out_ref, sems.at[1]))
+    for copy in leaving:
+        copy.start()
 
     @pl.when(flag_ref[t] == 1)
     def _():
@@ -236,6 +240,8 @@
         for s in range(SIDE):
             out_ref[s, j * ROWS : (j + 1) * ROWS, :] = mixed
     pltpu.make_async_copy(o_own_ref, w_ref, sem).wait()
+    for copy in leaving:
+        copy.wait()
 
 
 def update_half_kernel(t, flag_ref, mixed_ref, w_ref, x_ref, send_ref, got_ref, rows_out_ref, *refs):
@@ -311,11 +317,13 @@
     return jnp.concatenate([pair_lanes(low, even, odd), jnp.where(low, pltpu.roll(even, REST, 1), odd)], axis=0)
 
 
-def project_kernel(packed, row_ref, x_ref, mods_ref, w_ref, below_ref, above_ref, *refs):
+def project_kernel(packed, row_ref, x_ref, mods_in_ref, w_ref, below_ref, above_ref, *refs):
     across_low_ref, across_high_ref, q_ref, kv_ref, *refs = refs
     if packed:
         keep_out_ref, *refs = refs
-    wm_ref, wr_ref, nm_ref, nr_ref, keep_ref, sems = refs
+    wm_ref, wr_ref, nm_ref, nr_ref, keep_ref, mods_ref, sems = refs
+    mods_copy = pltpu.make_async_copy(mods_in_ref, mods_ref, sems.at[76])
+    mods_copy.start()
     i = row_ref[0]
     half = SIDE // 2
     sources = (
@@ -334,6 +342,7 @@
             copies += [pltpu.make_async_copy(a, b, sems.at[len(copies) + n]) for n, (a, b) in enumerate(pairs)]
     for copy in copies:
         copy.start()
+    mods_copy.wait()
     mods = [mods_ref[j].astype(F32) for j in range(SIDE)]
     scale = [m[0:1] + m[1:2] for m in mods]
     shift = [m[2:3] + m[3:4] for m in mods]
@@ -567,10 +576,10 @@
                 ],
             )
             kv_other = swap(kv)
-            mixed, w_now = call(
+            mixed, w_now, kv_kept, other_kept = call(
                 functools.partial(attend_half_kernel, t),
                 "attend_half",
-                (shaped(SIDE, HALF, HEAD_DIM), shaped(*o_own.shape)),
+                (shaped(SIDE, HALF, HEAD_DIM), shaped(*o_own.shape), kv_shape, kv_shape),
                 [SMEM, SMEM, VMEM, VMEM, VMEM, VMEM, VMEM, ANY, ANY],
                 flags,
                 patch_order,
@@ -581,7 +590,8 @@
                 got,
                 o_own,
                 o_peer,
-                scratch=[pltpu.SemaphoreType.DMA],
+                scratch=[pltpu.SemaphoreType.DMA, pltpu.SemaphoreType.DMA((2,))],
+                outside=(2, 3),
             )
             heads = gather_mixed(mixed)
             last = t == 1
@@ -606,7 +616,7 @@
             )
             if not last:
                 x, gathered = results[1], gather_mixed(results[2])
-            kept.append((results[0], kv, kv_other))
+            kept.append((results[0], kv_kept, other_kept))
         return results[1], kept
 
     half_width = SEQ * HEAD_DIM // 2
@@ -638,7 +648,7 @@
             functools.partial(project_kernel, packed),
             "project",
             (shaped(PART, HEADS), shaped(SIDE, PART, 2 * HEADS)) + (x_shape,) * packed,
-            [SMEM, VMEM, VMEM] + [ANY] * 5,
+            [SMEM, VMEM] + [ANY] * 6,
             row,
             gathered,
             mods_all,
@@ -650,7 +660,8 @@
                 pltpu.VMEM((PART, SEQ * LANES), BF16),
                 pltpu.VMEM((PART, SEQ * REST), BF16),
                 pltpu.VMEM(x_shape.shape, BF16),
-                pltpu.SemaphoreType.DMA((76,)),
+                pltpu.VMEM((SIDE, MODS, WIDE), BF16),
+                pltpu.SemaphoreType.DMA((77,)),
             ],
             outside=(2,),
             mib=20,

time: 286 us -> 285 us (level)
  the two profiles are of different devices: /device:TPU:65 before, /device:TPU:97 now
where the time goes in v5:
time: 285 us; the launch traced here: 284 us
  waiting for transfers between devices  165 us (58%)
  blocking collectives  49 us (17%)
  starting transfers between devices  46 us (16%)
  Pallas kernels  13.7 us (5%)
  local copies, waits for them, and re-layouts  8.26 us (3%)
    ppermute x1, waiting for transfers between devices, body(): lax.ppermute(state[0], 'section', [(s, s + 1) for s in range(sections) if...  76.8 us
    ppermute x8, waiting for transfers between devices, shift(): return lax.ppermute(value, 'seq', pairs)  65.6 us
    all_to_all x4, blocking collectives, exchange(): return lax.all_to_all(value, 'seq', 0, 0, axis_index_groups=groups)  49 us
    ppermute x8, starting transfers between devices, shift(): return lax.ppermute(value, 'seq', pairs)  26.3 us
    all_to_all x2, waiting for transfers between devices, exchange(): return lax.all_to_all(value, 'seq', 0, 0, axis_index_groups=groups)  22.5 us
    pallas_call x6, Pallas kernels, call(): pl.pallas_call(kernel, out_shape=out_shape, in_specs=in_specs, out_specs=...  13.7 us
    all_to_all x2, starting transfers between devices, exchange(): return lax.all_to_all(value, 'seq', 0, 0, axis_index_groups=groups)  12.6 us
  transfers between devices with their start and end apart: 16, of which 8 were waited for; matrix products, arithmetic and copies ran while one was open for 2% of the time, Pallas kernels for 0%

profile of v5, /device:TPU:97, one launch (start us, length us, event | category | flops | bytes accessed | tf_op | source)
XLA Modules:
  0.0 283.8 jit_solution(11314525006688109344)
XLA Ops:
  2.6 1.8 pack.1
  4.4 2.1 collective-permute-start.12
  6.5 134.1 %conditional.6 = ((bf16[3,4,4,192,128]{4,3,2,1,0:T(8,128)(2,1)}, bf16[3,4,4,192,128]{4,3,2,1,0:T(8,128)(2,1)}, bf16[3,2,4,192,128]{4,3,2,1,0:T(8,128)(2,1)}, bf1...) conditional(s32[]{:T(128)} %convert_element_type.6, ...), branch_computations={%region_2.3_spmd, %region_3.4_spmd} | conditional | bytes 74682984 | solution.py:720
  6.5 3.2 %collective-permute-start.2 = (bf16[3,4,4,192,128]{4,3,2,1,0:T(8,128)(2,1)}, bf16[3,4,4,192,128]{4,3,2,1,0:T(8,128)(2,1)S(1)}, u32[]{:S(2)}, u32[]{:S(2)}) collective-permute-start(bf16[3,4,4,192,128]{4,3,2,1,0:T(8,128)(2,1)} %bitcast.46), channel_id=1, source_target_pairs={{0,4},{1,5},{2,6},{3,7},{4,8},{5,9},{6,10},{7,11},{8,12},{9,13},{1... | collective-permute-start | bytes 7077896 | tf_op jit(solution)/shard_map/cond/branch_0_fun/ppermute | solution.py:519
  9.7 3.4 %collective-permute-start.3 = (bf16[3,4,4,192,128]{4,3,2,1,0:T(8,128)(2,1)}, bf16[3,4,4,192,128]{4,3,2,1,0:T(8,128)(2,1)S(1)}, u32[]{:S(2)}, u32[]{:S(2)}) collective-permute-start(bf16[3,4,4,192,128]{4,3,2,1,0:T(8,128)(2,1)} %bitcast.47), channel_id=1, source_target_pairs={{0,12},{1,13},{2,14},{3,15},{4,0},{5,1},{6,2},{7,3},{8,4},{9,5},{1... | collective-permute-start | bytes 7077896 | tf_op jit(solution)/shard_map/cond/branch_0_fun/ppermute | solution.py:519
  13.2 48.9 %collective-permute-done.2 = bf16[3,4,4,192,128]{4,3,2,1,0:T(8,128)(2,1)S(1)} collective-permute-done((bf16[3,4,4,192,128]{4,3,2,1,0:T(8,128)(2,1)}, bf16[3,4,4,192,128]{4,3,2,1,0:T(8,128)(2,1)S(1)}, u32[]{:S(2)}, u32[]{:S(2)}) %collective-permute-start.2) | collective-permute-done | bytes 2359328 | tf_op jit(solution)/shard_map/cond/branch_0_fun/ppermute | solution.py:519
  62.0 1.6 collective-permute-done.3
  64.9 3.1 %collective-permute-start.4 = (bf16[3,2,4,192,128]{4,3,2,1,0:T(8,128)(2,1)}, bf16[3,2,4,192,128]{4,3,2,1,0:T(8,128)(2,1)}, u32[]{:S(2)}, u32[]{:S(2)}) collective-permute-start(bf16[3,2,4,192,128]{4,3,2,1,0:T(8,128)(2,1)} %slice.16), channel_id=1, source_target_pairs={{0,4},{1,5},{2,6},{3,7},{4,8},{5,9},{6,10},{7,11},{8,12},{9,13},{1... | collective-permute-start | bytes 3538952 | tf_op jit(solution)/shard_map/cond/branch_0_fun/ppermute | solution.py:519
  69.1 3.5 %collective-permute-start.5 = (bf16[3,2,4,192,128]{4,3,2,1,0:T(8,128)(2,1)}, bf16[3,2,4,192,128]{4,3,2,1,0:T(8,128)(2,1)}, u32[]{:S(2)}, u32[]{:S(2)}) collective-permute-start(bf16[3,2,4,192,128]{4,3,2,1,0:T(8,128)(2,1)} %slice.17), channel_id=1, source_target_pairs={{0,12},{1,13},{2,14},{3,15},{4,0},{5,1},{6,2},{7,3},{8,4},{9,5},{1... | collective-permute-start | bytes 3538952 | tf_op jit(solution)/shard_map/cond/branch_0_fun/ppermute | solution.py:519
  73.8 3.5 %all-to-all-start.8 = ((bf16[4,1040,128]{2,1,0:T(8,128)(2,1)}), bf16[4,1040,128]{2,1,0:T(8,128)(2,1)S(1)}, u32[]{:S(2)}, u32[]{:S(2)}) async-start(bf16[4,1040,128]{2,1,0:T(8,128)(2,1)} %broadcast_in_dim.12), calls=%async_computation.8 | async-start | bytes 2129920 | tf_op jit(solution)/shard_map/cond/branch_0_fun/all_to_all | solution.py:515
  77.4 3.3 %collective-permute-start.6 = (bf16[192,2048]{1,0:T(8,128)(2,1)S(1)}, bf16[192,2048]{1,0:T(8,128)(2,1)}, u32[]{:S(2)}, u32[]{:S(2)}) collective-permute-start(bf16[192,2048]{1,0:T(8,128)(2,1)S(1)} %copy-done.8), channel_id=1, source_target_pairs={{0,4},{1,5},{2,6},{3,7},{4,8},{5,9},{6,10},{7,11},{8,12},{9,13},{1... | collective-permute-start | bytes 2359304 | tf_op jit(solution)/shard_map/cond/branch_0_fun/ppermute | solution.py:519
  80.7 3.2 %collective-permute-start.7 = (bf16[192,2048]{1,0:T(8,128)(2,1)S(1)}, bf16[192,2048]{1,0:T(8,128)(2,1)}, u32[]{:S(2)}, u32[]{:S(2)}) collective-permute-start(bf16[192,2048]{1,0:T(8,128)(2,1)S(1)} %copy-done.8), channel_id=1, source_target_pairs={{0,12},{1,13},{2,14},{3,15},{4,0},{5,1},{6,2},{7,3},{8,4},{9,5},{1... | collective-permute-start | bytes 2359304 | tf_op jit(solution)/shard_map/cond/branch_0_fun/ppermute | solution.py:519
  83.9 22.5 %all-to-all-done.8.gathered_ref = bf16[4,1040,128]{2,1,0:T(8,128)(2,1)S(1)} async-done(((bf16[4,1040,128]{2,1,0:T(8,128)(2,1)}), bf16[4,1040,128]{2,1,0:T(8,128)(2,1)S(1)}, u32[]{:S(2)}, u32[]{:S(2)}) %all-to-all-start.8) | async-done | bytes 1064992 | tf_op jit(solution)/shard_map/cond/branch_0_fun/all_to_all | solution.py:515
  107.0 9.1 %all-to-all-start.9 = ((bf16[4,16,768]{2,1,0:T(8,128)(2,1)}), bf16[4,16,768]{2,1,0:T(8,128)(2,1)}, u32[]{:S(2)}, u32[]{:S(2)}) async-start(bf16[4,16,768]{2,1,0:T(8,128)(2,1)} %broadcast_in_dim.14), calls=%async_computation.9 | async-start | bytes 196608 | tf_op jit(solution)/shard_map/cond/branch_0_fun/all_to_all | solution.py:515
  116.1 6.0 %collective-permute-done.6 = bf16[192,2048]{1,0:T(8,128)(2,1)} collective-permute-done((bf16[192,2048]{1,0:T(8,128)(2,1)S(1)}, bf16[192,2048]{1,0:T(8,128)(2,1)}, u32[]{:S(2)}, u32[]{:S(2)}) %collective-permute-start.6) | collective-permute-done | bytes 786464 | tf_op jit(solution)/shard_map/cond/branch_0_fun/ppermute | solution.py:519
  122.1 2.9 %collective-permute-done.7 = bf16[192,2048]{1,0:T(8,128)(2,1)} collective-permute-done((bf16[192,2048]{1,0:T(8,128)(2,1)S(1)}, bf16[192,2048]{1,0:T(8,128)(2,1)}, u32[]{:S(2)}, u32[]{:S(2)}) %collective-permute-start.7) | collective-permute-done | bytes 786464 | tf_op jit(solution)/shard_map/cond/branch_0_fun/ppermute | solution.py:519
  126.1 3.9 %collective-permute-start.8 = (bf16[192,1024]{1,0:T(8,128)(2,1)S(1)}, bf16[192,1024]{1,0:T(8,128)(2,1)S(1)}, u32[]{:S(2)}, u32[]{:S(2)}) collective-permute-start(bf16[192,1024]{1,0:T(8,128)(2,1)S(1)} %slice.18), channel_id=1, source_target_pairs={{0,4},{1,5},{2,6},{3,7},{4,8},{5,9},{6,10},{7,11},{8,12},{9,13},{1... | collective-permute-start | bytes 1179656 | tf_op jit(solution)/shard_map/cond/branch_0_fun/ppermute | solution.py:519
  131.1 2.6 collective-permute-start.9
  133.6 2.2 collective-permute-done.8
  135.8 4.0 %collective-permute-done.9 = bf16[192,1024]{1,0:T(8,128)(2,1)S(1)} collective-permute-done((bf16[192,1024]{1,0:T(8,128)(2,1)S(1)}, bf16[192,1024]{1,0:T(8,128)(2,1)S(1)}, u32[]{:S(2)}, u32[]{:S(2)}) %collective-permute-start.9) | collective-permute-done | bytes 393248 | tf_op jit(solution)/shard_map/cond/branch_0_fun/ppermute | solution.py:519
  140.6 1.5 collective-permute-start.13
  145.9 76.8 %collective-permute-done.16 = bf16[128,768]{1,0:T(8,128)(2,1)S(1)} collective-permute-done((bf16[128,768]{1,0:T(8,128)(2,1)}, bf16[128,768]{1,0:T(8,128)(2,1)S(1)}, u32[]{:S(2)}, u32[]{:S(2)}) %collective-permute-start.16) | collective-permute-done | bytes 196640 | tf_op jit(solution)/shard_map/ppermute | solution.py:734
  222.7 50.3 %conditional.8 = ((bf16[4,128,256]{2,1,0:T(8,128)(2,1)}, bf16[2,256,128]{2,1,0:T(8,128)(2,1)}, bf16[2,256,128]{2,1,0:T(8,128)(2,1)})) conditional(s32[]{:T(128)} %convert_element_type.14, (bf16[4,128,256]{2,1,0:T(8,128)(2,1)}, bf16[2,256,128]{2,1,0:T(8,128)(2,1)}, bf16[2,256,128]{2,1,0:T(8,128)(2,1)}) %tuple.57, (bf16[128,768]{1,0:T(8,128)(2,1)S(1)}, ...), branch_computations={%region_6.7_spmd, %region_7.8_spmd} | conditional | bytes 18284660 | solution.py:735
  222.7 15.0 %all_to_all.79.x_ref = bf16[4,128,768]{2,1,0:T(8,128)(2,1)S(1)} all-to-all(bf16[4,128,768]{2,1,0:T(8,128)(2,1)S(1)} %broadcast_in_dim.15), channel_id=1, replica_groups={{0,1,2,3},{4,5,6,7},{8,9,10,11},{12,13,14,15},{16,17,18,19},{20,21,22,2..., dimensions={0} | all-to-all | bytes 1572864 | tf_op jit(solution)/shard_map/cond/branch_1_fun/all_to_all | solution.py:515
  237.8 5.1 %project.3 = (bf16[128,512]{1,0:T(8,128)(2,1)S(1)}, bf16[4,128,1024]{2,1,0:T(8,128)(2,1)S(1)}) custom-call(s32[2]{0:T(128)S(1)} %get-tuple-element.196.row_ref, bf16[4,128,768]{2,1,0:T(8,128)(2,1)S(1)} %all_to_all.79.x_ref, bf16[4,16,768]{2,1,0:T(8,128)(2,1)} %get-tuple-element.199.mods_in_ref, bf16[3,4,4,192,128]{4,3,2,1,0:T(8,128)(2,1)S(1)} %bitcast.51, ...), custom_call_target="tpu_custom_call" | custom-call | tf_op jit(solution)/shard_map/cond/branch_1_fun/project/pallas_call | solution.py:50
  242.9 12.3 %all_to_all.80.kv_ref = bf16[4,128,1024]{2,1,0:T(8,128)(2,1)S(1)} all-to-all(bf16[4,128,1024]{2,1,0:T(8,128)(2,1)S(1)} %get-tuple-element.206), channel_id=1, replica_groups={{0,4,8,12},{1,5,9,13},{2,6,10,14},{3,7,11,15},{16,20,24,28},{17,21,25,2..., dimensions={0} | all-to-all | bytes 2097152 | tf_op jit(solution)/shard_map/cond/branch_1_fun/all_to_all | solution.py:515
  255.2 2.7 attend.3
  257.9 12.8 %all_to_all.81.mixed_ref = bf16[4,128,512]{2,1,0:T(8,128)(2,1)S(1)} all-to-all(bf16[4,128,512]{2,1,0:T(8,128)(2,1)S(1)} %get-tuple-element.213), channel_id=1, replica_groups={{0,1,2,3},{4,5,6,7},{8,9,10,11},{12,13,14,15},{16,17,18,19},{20,21,22,2..., dimensions={0} | all-to-all | bytes 1048576 | tf_op jit(solution)/shard_map/cond/branch_1_fun/all_to_all | solution.py:515
  270.7 2.2 update.3
  272.9 8.9 %conditional.9 = (bf16[4,64,256]{2,1,0:T(8,128)(2,1)S(1)}, bf16[4,64,256]{2,1,0:T(8,128)(2,1)S(1)}, bf16[2,256,128]{2,1,0:T(8,128)(2,1)}, bf16[2,256,128]{2,1,0:T(8,128)(2,1)}) conditional(s32[]{:T(128)} %convert_element_type.6, (bf16[4,128,256]{2,1,0:T(8,128)(2,1)}, bf16[2,256,128]{2,1,0:T(8,128)(2,1)}, ...), branch_computations={%region_8.9_spmd, %region_9.10_spmd} | conditional | flops 393217 | bytes 2359380 | solution.py:757
  273.0 8.9 %all_to_all.82 = bf16[4,128,256]{2,1,0:T(8,128)(2,1)S(1)} all-to-all(bf16[4,128,256]{2,1,0:T(8,128)(2,1)} %get-tuple-element.218), channel_id=1, replica_groups={{0,4,8,12},{1,5,9,13},{2,6,10,14},{3,7,11,15},{16,20,24,28},{17,21,25,2..., dimensions={0} | all-to-all | bytes 524288 | tf_op jit(solution)/shard_map/cond/branch_0_fun/all_to_all | solution.py:515
  281.9 1.8 finish.1
  (56 shorter events, 12.0 us)
Async XLA Ops:
  0.6 0.9 copy-start
  1.7 0.9 copy-start.1
  4.4 138.5 %collective-permute-start.12 = (bf16[3,3072,128]{2,1,0:T(8,128)(2,1)}, bf16[3,3072,128]{2,1,0:T(8,128)(2,1)}, u32[]{:S(2)}, u32[]{:S(2)}) collective-permute-start(bf16[3,3072,128]{2,1,0:T(8,128)(2,1)} %bitcast.41), channel_id=1, source_target_pairs={{0,16},{16,0},{64,80},{80,64},{128,144},{144,128},{192,208},{208,1... | collective-permute-start | bytes 7077896 | tf_op jit(solution)/shard_map/ppermute | solution.py:512
  6.5 136.4 %copy-start.7 = (bf16[1,2048,192]{1,2,0:T(8,128)(2,1)S(1)}, bf16[1,2048,192]{1,2,0:T(8,128)(2,1)}, u32[]{:S(2)}) copy-start(bf16[1,2048,192]{1,2,0:T(8,128)(2,1)} %param.22) | copy-start | bytes 2359300
  6.5 136.4 %copy-start.9 = (bf16[1,2,512,128]{3,2,1,0:T(8,128)(2,1)S(1)}, bf16[1,2,512,128]{3,2,1,0:T(8,128)(2,1)}, u32[]{:S(2)}) copy-start(bf16[1,2,512,128]{3,2,1,0:T(8,128)(2,1)} %param.23) | copy-start | bytes 786436
  6.5 136.5 %copy-start.16 = (s32[8]{0:T(128)S(1)}, s32[8]{0:T(128)}, u32[]{:S(2)}) copy-start(s32[8]{0:T(128)} %order_ref.3) | copy-start | bytes 100
  6.5 55.6 %collective-permute-start.2 = (bf16[3,4,4,192,128]{4,3,2,1,0:T(8,128)(2,1)}, bf16[3,4,4,192,128]{4,3,2,1,0:T(8,128)(2,1)S(1)}, u32[]{:S(2)}, u32[]{:S(2)}) collective-permute-start(bf16[3,4,4,192,128]{4,3,2,1,0:T(8,128)(2,1)} %bitcast.46), channel_id=1, source_target_pairs={{0,4},{1,5},{2,6},{3,7},{4,8},{5,9},{6,10},{7,11},{8,12},{9,13},{1... | collective-permute-start | bytes 7077896 | tf_op jit(solution)/shard_map/cond/branch_0_fun/ppermute | solution.py:519
  9.7 53.9 %collective-permute-start.3 = (bf16[3,4,4,192,128]{4,3,2,1,0:T(8,128)(2,1)}, bf16[3,4,4,192,128]{4,3,2,1,0:T(8,128)(2,1)S(1)}, u32[]{:S(2)}, u32[]{:S(2)}) collective-permute-start(bf16[3,4,4,192,128]{4,3,2,1,0:T(8,128)(2,1)} %bitcast.47), channel_id=1, source_target_pairs={{0,12},{1,13},{2,14},{3,15},{4,0},{5,1},{6,2},{7,3},{8,4},{9,5},{1... | collective-permute-start | bytes 7077896 | tf_op jit(solution)/shard_map/cond/branch_0_fun/ppermute | solution.py:519
  62.0 7.1 %copy-start.5 = (bf16[3,4,4,192,128]{4,3,2,1,0:T(8,128)(2,1)}, bf16[3,4,4,192,128]{4,3,2,1,0:T(8,128)(2,1)S(1)}, u32[]{:S(2)}) copy-start(bf16[3,4,4,192,128]{4,3,2,1,0:T(8,128)(2,1)S(1)} %collective-permute-done.2) | copy-start | bytes 7077892 | tf_op jit(solution)/shard_map/cond
  63.6 5.5 %copy-start.6 = (bf16[3,4,4,192,128]{4,3,2,1,0:T(8,128)(2,1)}, bf16[3,4,4,192,128]{4,3,2,1,0:T(8,128)(2,1)S(1)}, u32[]{:S(2)}) copy-start(bf16[3,4,4,192,128]{4,3,2,1,0:T(8,128)(2,1)S(1)} %collective-permute-done.3) | copy-start | bytes 7077892 | tf_op jit(solution)/shard_map/cond
  64.9 60.2 %collective-permute-start.4 = (bf16[3,2,4,192,128]{4,3,2,1,0:T(8,128)(2,1)}, bf16[3,2,4,192,128]{4,3,2,1,0:T(8,128)(2,1)}, u32[]{:S(2)}, u32[]{:S(2)}) collective-permute-start(bf16[3,2,4,192,128]{4,3,2,1,0:T(8,128)(2,1)} %slice.16), channel_id=1, source_target_pairs={{0,4},{1,5},{2,6},{3,7},{4,8},{5,9},{6,10},{7,11},{8,12},{9,13},{1... | collective-permute-start | bytes 3538952 | tf_op jit(solution)/shard_map/cond/branch_0_fun/ppermute | solution.py:519
  69.1 8.2 %copy-start.8 = (bf16[192,2048]{1,0:T(8,128)(2,1)S(1)}, bf16[192,2048]{1,0:T(8,128)(2,1)}, u32[]{:S(2)}) copy-start(bf16[192,2048]{1,0:T(8,128)(2,1)} %get-tuple-element.161) | copy-start | bytes 2359300 | tf_op jit(solution)/shard_map/cond
  69.1 55.9 %collective-permute-start.5 = (bf16[3,2,4,192,128]{4,3,2,1,0:T(8,128)(2,1)}, bf16[3,2,4,192,128]{4,3,2,1,0:T(8,128)(2,1)}, u32[]{:S(2)}, u32[]{:S(2)}) collective-permute-start(bf16[3,2,4,192,128]{4,3,2,1,0:T(8,128)(2,1)} %slice.17), channel_id=1, source_target_pairs={{0,12},{1,13},{2,14},{3,15},{4,0},{5,1},{6,2},{7,3},{8,4},{9,5},{1... | collective-permute-start | bytes 3538952 | tf_op jit(solution)/shard_map/cond/branch_0_fun/ppermute | solution.py:519
  73.8 32.5 %all-to-all-start.8 = ((bf16[4,1040,128]{2,1,0:T(8,128)(2,1)}), bf16[4,1040,128]{2,1,0:T(8,128)(2,1)S(1)}, u32[]{:S(2)}, u32[]{:S(2)}) async-start(bf16[4,1040,128]{2,1,0:T(8,128)(2,1)} %broadcast_in_dim.12), calls=%async_computation.8 | async-start | bytes 2129920 | tf_op jit(solution)/shard_map/cond/branch_0_fun/all_to_all | solution.py:515
  77.4 44.8 %collective-permute-start.6 = (bf16[192,2048]{1,0:T(8,128)(2,1)S(1)}, bf16[192,2048]{1,0:T(8,128)(2,1)}, u32[]{:S(2)}, u32[]{:S(2)}) collective-permute-start(bf16[192,2048]{1,0:T(8,128)(2,1)S(1)} %copy-done.8), channel_id=1, source_target_pairs={{0,4},{1,5},{2,6},{3,7},{4,8},{5,9},{6,10},{7,11},{8,12},{9,13},{1... | collective-permute-start | bytes 2359304 | tf_op jit(solution)/shard_map/cond/branch_0_fun/ppermute | solution.py:519
  80.7 44.4 %collective-permute-start.7 = (bf16[192,2048]{1,0:T(8,128)(2,1)S(1)}, bf16[192,2048]{1,0:T(8,128)(2,1)}, u32[]{:S(2)}, u32[]{:S(2)}) collective-permute-start(bf16[192,2048]{1,0:T(8,128)(2,1)S(1)} %copy-done.8), channel_id=1, source_target_pairs={{0,12},{1,13},{2,14},{3,15},{4,0},{5,1},{6,2},{7,3},{8,4},{9,5},{1... | collective-permute-start | bytes 2359304 | tf_op jit(solution)/shard_map/cond/branch_0_fun/ppermute | solution.py:519
  107.0 18.0 %all-to-all-start.9 = ((bf16[4,16,768]{2,1,0:T(8,128)(2,1)}), bf16[4,16,768]{2,1,0:T(8,128)(2,1)}, u32[]{:S(2)}, u32[]{:S(2)}) async-start(bf16[4,16,768]{2,1,0:T(8,128)(2,1)} %broadcast_in_dim.14), calls=%async_computation.9 | async-start | bytes 196608 | tf_op jit(solution)/shard_map/cond/branch_0_fun/all_to_all | solution.py:515
  126.1 9.8 %collective-permute-start.8 = (bf16[192,1024]{1,0:T(8,128)(2,1)S(1)}, bf16[192,1024]{1,0:T(8,128)(2,1)S(1)}, u32[]{:S(2)}, u32[]{:S(2)}) collective-permute-start(bf16[192,1024]{1,0:T(8,128)(2,1)S(1)} %slice.18), channel_id=1, source_target_pairs={{0,4},{1,5},{2,6},{3,7},{4,8},{5,9},{6,10},{7,11},{8,12},{9,13},{1... | collective-permute-start | bytes 1179656 | tf_op jit(solution)/shard_map/cond/branch_0_fun/ppermute | solution.py:519
  131.1 8.8 %collective-permute-start.9 = (bf16[192,1024]{1,0:T(8,128)(2,1)S(1)}, bf16[192,1024]{1,0:T(8,128)(2,1)S(1)}, u32[]{:S(2)}, u32[]{:S(2)}) collective-permute-start(bf16[192,1024]{1,0:T(8,128)(2,1)S(1)} %slice.19), channel_id=1, source_target_pairs={{0,12},{1,13},{2,14},{3,15},{4,0},{5,1},{6,2},{7,3},{8,4},{9,5},{1... | collective-permute-start | bytes 1179656 | tf_op jit(solution)/shard_map/cond/branch_0_fun/ppermute | solution.py:519
  135.8 4.0 %copy-start.10 = (bf16[192,1024]{1,0:T(8,128)(2,1)}, bf16[192,1024]{1,0:T(8,128)(2,1)S(1)}, u32[]{:S(2)}) copy-start(bf16[192,1024]{1,0:T(8,128)(2,1)S(1)} %collective-permute-done.8) | copy-start | bytes 1179652 | tf_op jit(solution)/shard_map/cond
  139.9 0.7 copy-start.13
  140.6 2.3 collective-permute-start.13
  142.2 0.7 collective-permute-start.11
  143.0 1.6 collective-permute-start.14
  143.8 0.8 collective-permute-start.15
  144.6 78.1 %collective-permute-start.16 = (bf16[128,768]{1,0:T(8,128)(2,1)}, bf16[128,768]{1,0:T(8,128)(2,1)S(1)}, u32[]{:S(2)}, u32[]{:S(2)}) collective-permute-start(bf16[128,768]{1,0:T(8,128)(2,1)} %get-tuple-element.319), channel_id=1, source_target_pairs={{32,48},{96,112},{160,176},{224,240},{288,304},{352,368},{416,432}... | collective-permute-start | bytes 589832 | tf_op jit(solution)/shard_map/ppermute | solution.py:734
  222.7 15.1 %copy-start.4 = (bf16[3,3072,128]{2,1,0:T(8,128)(2,1)S(1)}, bf16[3,3072,128]{2,1,0:T(8,128)(2,1)}, u32[]{:S(2)}) copy-start(bf16[3,3072,128]{2,1,0:T(8,128)(2,1)} %get-tuple-element.200) | copy-start | bytes 7077892 | tf_op jit(solution)/shard_map/cond
  242.8 12.3 %copy-start.12 = (bf16[192,1024]{1,0:T(8,128)(2,1)S(1)}, bf16[192,1024]{1,0:T(8,128)(2,1)}, u32[]{:S(2)}) copy-start(bf16[192,1024]{1,0:T(8,128)(2,1)} %get-tuple-element.211.refs_3_) | copy-start | bytes 1179652 | tf_op jit(solution)/shard_map/cond
  242.9 12.3 %copy-start.15 = (bf16[192,1024]{1,0:T(8,128)(2,1)S(1)}, bf16[192,1024]{1,0:T(8,128)(2,1)}, u32[]{:S(2)}) copy-start(bf16[192,1024]{1,0:T(8,128)(2,1)} %get-tuple-element.212.refs_4_) | copy-start | bytes 1179652 | tf_op jit(solution)/shard_map/cond

commit v6 on v5

--- a/solution.py
+++ b/solution.py
@@ -204,11 +204,15 @@
 
 
 def attend_half_kernel(t, flag_ref, order_ref, q_ref, kv_ref, other_ref, own_ref, got_ref, *refs):
-    o_own_ref, o_peer_ref, out_ref, w_ref, kv_out_ref, other_out_ref, sem, sems = refs
-    leaving = [pltpu.make_async_copy(kv_ref, kv_out_ref, sems.at[0])]
-    leaving.append(pltpu.make_async_copy(other_ref, other_out_ref, sems.at[1]))
-    for copy in leaving:
-        copy.start()
+    o_own_ref, o_peer_ref, out_ref, w_ref, cache_ref, sem, sems = refs
+    leaving = []
+    for whose, new_ref in enumerate((kv_ref, other_ref)):
+        first = (flag_ref[2] if whose == 0 else 1 - flag_ref[2]) * SIDE
+        for part in range(2):
+            for n in range(SIDE):
+                here = cache_ref.at[part, patch_at(order_ref, first + n), :]
+                new = new_ref.at[part, n * ROWS : (n + 1) * ROWS, :]
+                leaving.append(pltpu.make_async_copy(new, here, sems.at[len(leaving)]))
 
     @pl.when(flag_ref[t] == 1)
     def _():
@@ -217,6 +221,9 @@
     @pl.when(flag_ref[t] == 0)
     def _():
         pltpu.make_async_copy(o_peer_ref, w_ref, sem).start()
+
+    for copy in leaving:
+        copy.start()
 
     mine = flag_ref[t] == 1
     core = flag_ref[2]
@@ -418,15 +425,15 @@
 
 
 def attend_kernel(row_ref, order_ref, q_ref, kv_ref, stale_ref, *refs):
-    *w_refs, out_ref, held_ref, low_ref, high_ref, sems = refs
+    *w_refs, out_ref, held_ref, cache_ref, sems = refs
     i = row_ref[0]
     copies = load_out(i, *w_refs, held_ref, sems)
     for part in range(2):
         lanes = pl.ds(pl.multiple_of(part * HEADS + i * HEAD_DIM, HEAD_DIM), HEAD_DIM)
         for n in range(SIDE):
-            for half, own_ref in enumerate((low_ref, high_ref)):
+            for half in range(GROUP):
                 new = kv_ref.at[n, half * ROWS : (half + 1) * ROWS, lanes]
-                own = own_ref.at[part, n * ROWS : (n + 1) * ROWS, :]
+                own = cache_ref.at[part, patch_at(order_ref, half * SIDE + n), :]
                 copies.append(pltpu.make_async_copy(new, own, sems.at[len(copies)]))
     for copy in copies:
         copy.start()
@@ -482,13 +489,10 @@
         copy.wait()
 
 
-def finish_kernel(order_ref, low_ref, high_ref, kv_low_ref, kv_high_ref, out_ref, cache_ref, rows_ref):
-    for half, (x_ref, kv_ref) in enumerate(((low_ref, kv_low_ref), (high_ref, kv_high_ref))):
+def finish_kernel(order_ref, low_ref, high_ref, out_ref, rows_ref):
+    for half, x_ref in enumerate((low_ref, high_ref)):
         for n in range(SIDE):
-            at = patch_at(order_ref, half * SIDE + n)
-            rows_ref[at, :] = x_ref[n].astype(F32)
-            for part in range(2):
-                cache_ref[part, at, :] = kv_ref[part, n * ROWS : (n + 1) * ROWS, :]
+            rows_ref[patch_at(order_ref, half * SIDE + n), :] = x_ref[n].astype(F32)
     out_ref[...] = rows_ref[...].T[:SHARD, :].astype(BF16)
 
 
@@ -530,6 +534,7 @@
     def gather(value, groups):
         return exchange(jnp.broadcast_to(value[None], (SIDE,) + value.shape), groups)
 
+    cache_shape = shaped(2, ALL, HEAD_DIM)
     rows_shape, kv_shape = shaped(SIDE, ROWS, 2 * LANES), shaped(2, HALF, HEAD_DIM)
     hand_shape, x_shape, parts_shape = shaped(SIDE, PIECE, LANES), shaped(PART, WIDE), shaped(SIDE, PART, 2 * LANES)
 
@@ -576,10 +581,10 @@
                 ],
             )
             kv_other = swap(kv)
-            mixed, w_now, kv_kept, other_kept = call(
+            mixed, w_now, cache = call(
                 functools.partial(attend_half_kernel, t),
                 "attend_half",
-                (shaped(SIDE, HALF, HEAD_DIM), shaped(*o_own.shape), kv_shape, kv_shape),
+                (shaped(SIDE, HALF, HEAD_DIM), shaped(*o_own.shape), cache_shape),
                 [SMEM, SMEM, VMEM, VMEM, VMEM, VMEM, VMEM, ANY, ANY],
                 flags,
                 patch_order,
@@ -590,8 +595,8 @@
                 got,
                 o_own,
                 o_peer,
-                scratch=[pltpu.SemaphoreType.DMA, pltpu.SemaphoreType.DMA((2,))],
-                outside=(2, 3),
+                scratch=[pltpu.SemaphoreType.DMA, pltpu.SemaphoreType.DMA((4 * SIDE,))],
+                outside=(2,),
             )
             heads = gather_mixed(mixed)
             last = t == 1
@@ -616,7 +621,7 @@
             )
             if not last:
                 x, gathered = results[1], gather_mixed(results[2])
-            kept.append((results[0], kv_kept, other_kept))
+            kept.append((results[0], cache))
         return results[1], kept
 
     half_width = SEQ * HEAD_DIM // 2
@@ -667,10 +672,10 @@
             mib=20,
         )
         x = keep[0] if packed else x
-        mixed, held, kv_low, kv_high = call(
+        mixed, held, cache = call(
             attend_kernel,
             "attend",
-            (shaped(SIDE, PART, HEADS), shaped(WIDE, SEQ * HEAD_DIM), kv_shape, kv_shape),
+            (shaped(SIDE, PART, HEADS), shaped(WIDE, SEQ * HEAD_DIM), cache_shape),
             [SMEM, SMEM, VMEM, VMEM, VMEM] + [ANY] * 5,
             row,
             patch_order,
@@ -680,7 +685,7 @@
             o_own,
             *o_others,
             scratch=[pltpu.SemaphoreType.DMA((26,))],
-            outside=(2, 3),
+            outside=(2,),
         )
         made = call(
             functools.partial(update_kernel, not packed),
@@ -700,7 +705,7 @@
             ],
             outside=(0, 1),
         )
-        return *made, kv_low, kv_high
+        return *made, cache
 
     def second_block(low, high, weights):
         spread = call(spread_kernel, "spread", shaped(SEQ, 2 * PIECE, LANES), [VMEM, VMEM], low, high)
@@ -710,18 +715,16 @@
         return later_block(x, gather(x, ALONG_Z), *weights)
 
     early = position < 2
-    one = (rows_shape, kv_shape, kv_shape)
-
     def not_here(*_):
-        hand, *both = blank(hand_shape, *one, *one)
-        return hand, [tuple(both[:3]), tuple(both[3:])]
+        hand, *both = blank(hand_shape, rows_shape, cache_shape, rows_shape, cache_shape)
+        return hand, [tuple(both[:2]), tuple(both[2:])]
 
     hand, kept = lax.cond(early, first_blocks, not_here, own, send, got, w_peer, o_peer)
     weights = lax.cond(early, no_weights, prepare, send[PACK:])
     hand, weights = lax.optimization_barrier((hand, weights))
     low = lax.ppermute(hand, "section", [(s, s + 2) for s in range(sections) if s % CHAIN == 0])
     high = lax.ppermute(hand, "section", [(s, s + 1) for s in range(sections) if s % CHAIN == 1])
-    state = blank(x_shape, parts_shape, kv_shape, kv_shape)
+    state = blank(x_shape, parts_shape, cache_shape)
     state = lax.cond(
         position == 2,
         lambda low, high, state, weights: second_block(low, high, weights),
@@ -742,29 +745,26 @@
     )
 
     def finish_early(state, kept):
-        (rows0, kv0, other0), (rows1, kv1, other1) = kept
+        (rows0, cache0), (rows1, cache1) = kept
         first = core == 0
         mine, theirs = jnp.where(first, rows0, rows1), jnp.where(first, rows1, rows0)
         other = swap(theirs)
-        rows = jnp.where(first, mine, other), jnp.where(first, other, mine)
-        return rows + (jnp.where(first, kv0, other1), jnp.where(first, other0, kv1))
+        return jnp.where(first, mine, other), jnp.where(first, other, mine), jnp.where(first, cache0, cache1)
 
     def finish_late(state, kept):
-        parts, kv_low, kv_high = state
+        parts, cache = state
         rows = exchange(parts, ALONG_X)
-        return rows[:, :ROWS], rows[:, ROWS:], kv_low, kv_high
-
-    rows_low, rows_high, kv_low, kv_high = lax.cond(early, finish_early, finish_late, state, kept)
-    out_t, cache = call(
+        return rows[:, :ROWS], rows[:, ROWS:], cache
+
+    rows_low, rows_high, cache = lax.cond(early, finish_early, finish_late, state, kept)
+    out_t = call(
         finish_kernel,
         "finish",
-        (shaped(SHARD, ALL), shaped(2, ALL, HEAD_DIM)),
-        [SMEM, VMEM, VMEM, VMEM, VMEM],
+        shaped(SHARD, ALL),
+        [SMEM, VMEM, VMEM],
         patch_order,
         rows_low,
         rows_high,
-        kv_low,
-        kv_high,
         scratch=[pltpu.VMEM((ALL, 2 * LANES), F32)],
     )
     return jnp.transpose(out_t, (1, 0))[None], cache[None]

time: 285 us -> 284 us (level)
  the two profiles are of different devices: /device:TPU:97 before, /device:TPU:73 now
where the time goes in v6:
time: 284 us; the launch traced here: 283 us
  waiting for transfers between devices  165 us (58%)
  blocking collectives  49 us (17%)
  starting transfers between devices  45.8 us (16%)
  Pallas kernels  13.3 us (5%)
  local copies, waits for them, and re-layouts  8.25 us (3%)
    ppermute x1, waiting for transfers between devices, body(): lax.ppermute(state[0], 'section', [(s, s + 1) for s in range(sections) if...  76.9 us
    ppermute x8, waiting for transfers between devices, shift(): return lax.ppermute(value, 'seq', pairs)  65.6 us
    all_to_all x4, blocking collectives, exchange(): return lax.all_to_all(value, 'seq', 0, 0, axis_index_groups=groups)  49 us
    ppermute x8, starting transfers between devices, shift(): return lax.ppermute(value, 'seq', pairs)  26.3 us
    all_to_all x2, waiting for transfers between devices, exchange(): return lax.all_to_all(value, 'seq', 0, 0, axis_index_groups=groups)  22.5 us
    pallas_call x6, Pallas kernels, call(): pl.pallas_call(kernel, out_shape=out_shape, in_specs=in_specs, out_specs=...  13.3 us
    all_to_all x2, starting transfers between devices, exchange(): return lax.all_to_all(value, 'seq', 0, 0, axis_index_groups=groups)  12.6 us
  transfers between devices with their start and end apart: 16, of which 8 were waited for; matrix products, arithmetic and copies ran while one was open for 2% of the time, Pallas kernels for 0%

profile of v6, /device:TPU:73, one launch (start us, length us, event | category | flops | bytes accessed | tf_op | source)
XLA Modules:
  0.0 283.5 jit_solution(8651826127934035127)
XLA Ops:
  2.6 1.8 pack.1
  4.4 2.1 collective-permute-start.12
  6.5 134.1 %conditional.6 = ((bf16[3,4,4,192,128]{4,3,2,1,0:T(8,128)(2,1)}, bf16[3,4,4,192,128]{4,3,2,1,0:T(8,128)(2,1)}, bf16[3,2,4,192,128]{4,3,2,1,0:T(8,128)(2,1)}, bf1...) conditional(s32[]{:T(128)} %convert_element_type.6, ...), branch_computations={%region_2.3_spmd, %region_3.4_spmd} | conditional | bytes 74682984 | solution.py:723
  6.5 3.2 %collective-permute-start.2 = (bf16[3,4,4,192,128]{4,3,2,1,0:T(8,128)(2,1)}, bf16[3,4,4,192,128]{4,3,2,1,0:T(8,128)(2,1)S(1)}, u32[]{:S(2)}, u32[]{:S(2)}) collective-permute-start(bf16[3,4,4,192,128]{4,3,2,1,0:T(8,128)(2,1)} %bitcast.46), channel_id=1, source_target_pairs={{0,4},{1,5},{2,6},{3,7},{4,8},{5,9},{6,10},{7,11},{8,12},{9,13},{1... | collective-permute-start | bytes 7077896 | tf_op jit(solution)/shard_map/cond/branch_0_fun/ppermute | solution.py:523
  9.7 3.4 %collective-permute-start.3 = (bf16[3,4,4,192,128]{4,3,2,1,0:T(8,128)(2,1)}, bf16[3,4,4,192,128]{4,3,2,1,0:T(8,128)(2,1)S(1)}, u32[]{:S(2)}, u32[]{:S(2)}) collective-permute-start(bf16[3,4,4,192,128]{4,3,2,1,0:T(8,128)(2,1)} %bitcast.47), channel_id=1, source_target_pairs={{0,12},{1,13},{2,14},{3,15},{4,0},{5,1},{6,2},{7,3},{8,4},{9,5},{1... | collective-permute-start | bytes 7077896 | tf_op jit(solution)/shard_map/cond/branch_0_fun/ppermute | solution.py:523
  13.1 48.9 %collective-permute-done.2 = bf16[3,4,4,192,128]{4,3,2,1,0:T(8,128)(2,1)S(1)} collective-permute-done((bf16[3,4,4,192,128]{4,3,2,1,0:T(8,128)(2,1)}, bf16[3,4,4,192,128]{4,3,2,1,0:T(8,128)(2,1)S(1)}, u32[]{:S(2)}, u32[]{:S(2)}) %collective-permute-start.2) | collective-permute-done | bytes 2359328 | tf_op jit(solution)/shard_map/cond/branch_0_fun/ppermute | solution.py:523
  62.0 1.6 collective-permute-done.3
  64.8 3.1 %collective-permute-start.4 = (bf16[3,2,4,192,128]{4,3,2,1,0:T(8,128)(2,1)}, bf16[3,2,4,192,128]{4,3,2,1,0:T(8,128)(2,1)}, u32[]{:S(2)}, u32[]{:S(2)}) collective-permute-start(bf16[3,2,4,192,128]{4,3,2,1,0:T(8,128)(2,1)} %slice.16), channel_id=1, source_target_pairs={{0,4},{1,5},{2,6},{3,7},{4,8},{5,9},{6,10},{7,11},{8,12},{9,13},{1... | collective-permute-start | bytes 3538952 | tf_op jit(solution)/shard_map/cond/branch_0_fun/ppermute | solution.py:523
  69.1 3.5 %collective-permute-start.5 = (bf16[3,2,4,192,128]{4,3,2,1,0:T(8,128)(2,1)}, bf16[3,2,4,192,128]{4,3,2,1,0:T(8,128)(2,1)}, u32[]{:S(2)}, u32[]{:S(2)}) collective-permute-start(bf16[3,2,4,192,128]{4,3,2,1,0:T(8,128)(2,1)} %slice.17), channel_id=1, source_target_pairs={{0,12},{1,13},{2,14},{3,15},{4,0},{5,1},{6,2},{7,3},{8,4},{9,5},{1... | collective-permute-start | bytes 3538952 | tf_op jit(solution)/shard_map/cond/branch_0_fun/ppermute | solution.py:523
  73.8 3.5 %all-to-all-start.8 = ((bf16[4,1040,128]{2,1,0:T(8,128)(2,1)}), bf16[4,1040,128]{2,1,0:T(8,128)(2,1)S(1)}, u32[]{:S(2)}, u32[]{:S(2)}) async-start(bf16[4,1040,128]{2,1,0:T(8,128)(2,1)} %broadcast_in_dim.12), calls=%async_computation.8 | async-start | bytes 2129920 | tf_op jit(solution)/shard_map/cond/branch_0_fun/all_to_all | solution.py:519
  77.3 3.3 %collective-permute-start.6 = (bf16[192,2048]{1,0:T(8,128)(2,1)S(1)}, bf16[192,2048]{1,0:T(8,128)(2,1)}, u32[]{:S(2)}, u32[]{:S(2)}) collective-permute-start(bf16[192,2048]{1,0:T(8,128)(2,1)S(1)} %copy-done.8), channel_id=1, source_target_pairs={{0,4},{1,5},{2,6},{3,7},{4,8},{5,9},{6,10},{7,11},{8,12},{9,13},{1... | collective-permute-start | bytes 2359304 | tf_op jit(solution)/shard_map/cond/branch_0_fun/ppermute | solution.py:523
  80.6 3.2 %collective-permute-start.7 = (bf16[192,2048]{1,0:T(8,128)(2,1)S(1)}, bf16[192,2048]{1,0:T(8,128)(2,1)}, u32[]{:S(2)}, u32[]{:S(2)}) collective-permute-start(bf16[192,2048]{1,0:T(8,128)(2,1)S(1)} %copy-done.8), channel_id=1, source_target_pairs={{0,12},{1,13},{2,14},{3,15},{4,0},{5,1},{6,2},{7,3},{8,4},{9,5},{1... | collective-permute-start | bytes 2359304 | tf_op jit(solution)/shard_map/cond/branch_0_fun/ppermute | solution.py:523
  83.8 22.5 %all-to-all-done.8.gathered_ref = bf16[4,1040,128]{2,1,0:T(8,128)(2,1)S(1)} async-done(((bf16[4,1040,128]{2,1,0:T(8,128)(2,1)}), bf16[4,1040,128]{2,1,0:T(8,128)(2,1)S(1)}, u32[]{:S(2)}, u32[]{:S(2)}) %all-to-all-start.8) | async-done | bytes 1064992 | tf_op jit(solution)/shard_map/cond/branch_0_fun/all_to_all | solution.py:519
  107.0 9.1 %all-to-all-start.9 = ((bf16[4,16,768]{2,1,0:T(8,128)(2,1)}), bf16[4,16,768]{2,1,0:T(8,128)(2,1)}, u32[]{:S(2)}, u32[]{:S(2)}) async-start(bf16[4,16,768]{2,1,0:T(8,128)(2,1)} %broadcast_in_dim.14), calls=%async_computation.9 | async-start | bytes 196608 | tf_op jit(solution)/shard_map/cond/branch_0_fun/all_to_all | solution.py:519
  116.1 6.0 %collective-permute-done.6 = bf16[192,2048]{1,0:T(8,128)(2,1)} collective-permute-done((bf16[192,2048]{1,0:T(8,128)(2,1)S(1)}, bf16[192,2048]{1,0:T(8,128)(2,1)}, u32[]{:S(2)}, u32[]{:S(2)}) %collective-permute-start.6) | collective-permute-done | bytes 786464 | tf_op jit(solution)/shard_map/cond/branch_0_fun/ppermute | solution.py:523
  122.1 2.9 %collective-permute-done.7 = bf16[192,2048]{1,0:T(8,128)(2,1)} collective-permute-done((bf16[192,2048]{1,0:T(8,128)(2,1)S(1)}, bf16[192,2048]{1,0:T(8,128)(2,1)}, u32[]{:S(2)}, u32[]{:S(2)}) %collective-permute-start.7) | collective-permute-done | bytes 786464 | tf_op jit(solution)/shard_map/cond/branch_0_fun/ppermute | solution.py:523
  126.1 3.9 %collective-permute-start.8 = (bf16[192,1024]{1,0:T(8,128)(2,1)S(1)}, bf16[192,1024]{1,0:T(8,128)(2,1)S(1)}, u32[]{:S(2)}, u32[]{:S(2)}) collective-permute-start(bf16[192,1024]{1,0:T(8,128)(2,1)S(1)} %slice.18), channel_id=1, source_target_pairs={{0,4},{1,5},{2,6},{3,7},{4,8},{5,9},{6,10},{7,11},{8,12},{9,13},{1... | collective-permute-start | bytes 1179656 | tf_op jit(solution)/shard_map/cond/branch_0_fun/ppermute | solution.py:523
  131.0 2.6 collective-permute-start.9
  133.6 2.2 collective-permute-done.8
  135.8 4.0 %collective-permute-done.9 = bf16[192,1024]{1,0:T(8,128)(2,1)S(1)} collective-permute-done((bf16[192,1024]{1,0:T(8,128)(2,1)S(1)}, bf16[192,1024]{1,0:T(8,128)(2,1)S(1)}, u32[]{:S(2)}, u32[]{:S(2)}) %collective-permute-start.9) | collective-permute-done | bytes 393248 | tf_op jit(solution)/shard_map/cond/branch_0_fun/ppermute | solution.py:523
  140.6 1.5 collective-permute-start.13
  145.9 76.9 %collective-permute-done.16 = bf16[128,768]{1,0:T(8,128)(2,1)S(1)} collective-permute-done((bf16[128,768]{1,0:T(8,128)(2,1)}, bf16[128,768]{1,0:T(8,128)(2,1)S(1)}, u32[]{:S(2)}, u32[]{:S(2)}) %collective-permute-start.16) | collective-permute-done | bytes 196640 | tf_op jit(solution)/shard_map/ppermute | solution.py:737
  222.8 50.3 %conditional.8 = ((bf16[4,128,256]{2,1,0:T(8,128)(2,1)}, bf16[2,512,128]{2,1,0:T(8,128)(2,1)})) conditional(s32[]{:T(128)} %convert_element_type.14, (bf16[4,128,256]{2,1,0:T(8,128)(2,1)}, bf16[2,512,128]{2,1,0:T(8,128)(2,1)}) %tuple.57, (bf16[128,768]{1,0:T(8,128)(2,1)S(1)}, bf16[3,3072,128]{2,1,0:T(8,128)(2,1)}, s32[2]{0:T(128)S(1)}, ...), branch_computations={%region_6.7_spmd, %region_7.8_spmd} | conditional | bytes 18284652 | solution.py:738
  222.9 15.0 %all_to_all.79.x_ref = bf16[4,128,768]{2,1,0:T(8,128)(2,1)S(1)} all-to-all(bf16[4,128,768]{2,1,0:T(8,128)(2,1)S(1)} %broadcast_in_dim.15), channel_id=1, replica_groups={{0,1,2,3},{4,5,6,7},{8,9,10,11},{12,13,14,15},{16,17,18,19},{20,21,22,2..., dimensions={0} | all-to-all | bytes 1572864 | tf_op jit(solution)/shard_map/cond/branch_1_fun/all_to_all | solution.py:519
  237.9 5.1 %project.3 = (bf16[128,512]{1,0:T(8,128)(2,1)S(1)}, bf16[4,128,1024]{2,1,0:T(8,128)(2,1)S(1)}) custom-call(s32[2]{0:T(128)S(1)} %get-tuple-element.183.row_ref, bf16[4,128,768]{2,1,0:T(8,128)(2,1)S(1)} %all_to_all.79.x_ref, bf16[4,16,768]{2,1,0:T(8,128)(2,1)} %get-tuple-element.186.mods_in_ref, bf16[3,4,4,192,128]{4,3,2,1,0:T(8,128)(2,1)S(1)} %bitcast.51, ...), custom_call_target="tpu_custom_call" | custom-call | tf_op jit(solution)/shard_map/cond/branch_1_fun/project/pallas_call | solution.py:50
  243.0 12.3 %all_to_all.80.kv_ref = bf16[4,128,1024]{2,1,0:T(8,128)(2,1)S(1)} all-to-all(bf16[4,128,1024]{2,1,0:T(8,128)(2,1)S(1)} %get-tuple-element.193), channel_id=1, replica_groups={{0,4,8,12},{1,5,9,13},{2,6,10,14},{3,7,11,15},{16,20,24,28},{17,21,25,2..., dimensions={0} | all-to-all | bytes 2097152 | tf_op jit(solution)/shard_map/cond/branch_1_fun/all_to_all | solution.py:519
  255.3 2.7 attend.3
  258.1 12.8 %all_to_all.81.mixed_ref = bf16[4,128,512]{2,1,0:T(8,128)(2,1)S(1)} all-to-all(bf16[4,128,512]{2,1,0:T(8,128)(2,1)S(1)} %get-tuple-element.200), channel_id=1, replica_groups={{0,1,2,3},{4,5,6,7},{8,9,10,11},{12,13,14,15},{16,17,18,19},{20,21,22,2..., dimensions={0} | all-to-all | bytes 1048576 | tf_op jit(solution)/shard_map/cond/branch_1_fun/all_to_all | solution.py:519
  270.9 2.3 update.3
  273.1 8.9 %conditional.9 = (bf16[4,64,256]{2,1,0:T(8,128)(2,1)S(1)}, bf16[4,64,256]{2,1,0:T(8,128)(2,1)S(1)}, bf16[2,512,128]{2,1,0:T(8,128)(2,1)}) conditional(s32[]{:T(128)} %convert_element_type.6, (bf16[4,128,256]{2,1,0:T(8,128)(2,1)}, bf16[2,512,128]{2,1,0:T(8,128)(2,1)}) %get-tuple-element.358, (s32[]{:T(128)}, bf16[4,64,256]{2,1,0:T(8,128)(2,1)}, ...), branch_computations={%region_8.9_spmd, %region_9.10_spmd} | conditional | flops 393217 | bytes 2359372 | solution.py:759
  273.1 8.9 %all_to_all.82 = bf16[4,128,256]{2,1,0:T(8,128)(2,1)S(1)} all-to-all(bf16[4,128,256]{2,1,0:T(8,128)(2,1)} %get-tuple-element.204), channel_id=1, replica_groups={{0,4,8,12},{1,5,9,13},{2,6,10,14},{3,7,11,15},{16,20,24,28},{17,21,25,2..., dimensions={0} | all-to-all | bytes 524288 | tf_op jit(solution)/shard_map/cond/branch_0_fun/all_to_all | solution.py:519
  282.1 1.4 finish.1
  (56 shorter events, 11.9 us)
Async XLA Ops:
  0.6 0.9 copy-start
  1.7 0.9 copy-start.1
  4.4 138.5 %collective-permute-start.12 = (bf16[3,3072,128]{2,1,0:T(8,128)(2,1)}, bf16[3,3072,128]{2,1,0:T(8,128)(2,1)}, u32[]{:S(2)}, u32[]{:S(2)}) collective-permute-start(bf16[3,3072,128]{2,1,0:T(8,128)(2,1)} %bitcast.41), channel_id=1, source_target_pairs={{0,16},{16,0},{64,80},{80,64},{128,144},{144,128},{192,208},{208,1... | collective-permute-start | bytes 7077896 | tf_op jit(solution)/shard_map/ppermute | solution.py:516
  6.5 136.4 %copy-start.7 = (bf16[1,2048,192]{1,2,0:T(8,128)(2,1)S(1)}, bf16[1,2048,192]{1,2,0:T(8,128)(2,1)}, u32[]{:S(2)}) copy-start(bf16[1,2048,192]{1,2,0:T(8,128)(2,1)} %param.22) | copy-start | bytes 2359300
  6.5 136.4 %copy-start.9 = (bf16[1,2,512,128]{3,2,1,0:T(8,128)(2,1)S(1)}, bf16[1,2,512,128]{3,2,1,0:T(8,128)(2,1)}, u32[]{:S(2)}) copy-start(bf16[1,2,512,128]{3,2,1,0:T(8,128)(2,1)} %param.23) | copy-start | bytes 786436
  6.5 136.5 %copy-start.16 = (s32[8]{0:T(128)S(1)}, s32[8]{0:T(128)}, u32[]{:S(2)}) copy-start(s32[8]{0:T(128)} %order_ref.3) | copy-start | bytes 100
  6.5 55.6 %collective-permute-start.2 = (bf16[3,4,4,192,128]{4,3,2,1,0:T(8,128)(2,1)}, bf16[3,4,4,192,128]{4,3,2,1,0:T(8,128)(2,1)S(1)}, u32[]{:S(2)}, u32[]{:S(2)}) collective-permute-start(bf16[3,4,4,192,128]{4,3,2,1,0:T(8,128)(2,1)} %bitcast.46), channel_id=1, source_target_pairs={{0,4},{1,5},{2,6},{3,7},{4,8},{5,9},{6,10},{7,11},{8,12},{9,13},{1... | collective-permute-start | bytes 7077896 | tf_op jit(solution)/shard_map/cond/branch_0_fun/ppermute | solution.py:523
  9.7 53.9 %collective-permute-start.3 = (bf16[3,4,4,192,128]{4,3,2,1,0:T(8,128)(2,1)}, bf16[3,4,4,192,128]{4,3,2,1,0:T(8,128)(2,1)S(1)}, u32[]{:S(2)}, u32[]{:S(2)}) collective-permute-start(bf16[3,4,4,192,128]{4,3,2,1,0:T(8,128)(2,1)} %bitcast.47), channel_id=1, source_target_pairs={{0,12},{1,13},{2,14},{3,15},{4,0},{5,1},{6,2},{7,3},{8,4},{9,5},{1... | collective-permute-start | bytes 7077896 | tf_op jit(solution)/shard_map/cond/branch_0_fun/ppermute | solution.py:523
  62.0 7.1 %copy-start.5 = (bf16[3,4,4,192,128]{4,3,2,1,0:T(8,128)(2,1)}, bf16[3,4,4,192,128]{4,3,2,1,0:T(8,128)(2,1)S(1)}, u32[]{:S(2)}) copy-start(bf16[3,4,4,192,128]{4,3,2,1,0:T(8,128)(2,1)S(1)} %collective-permute-done.2) | copy-start | bytes 7077892 | tf_op jit(solution)/shard_map/cond
  63.6 5.5 %copy-start.6 = (bf16[3,4,4,192,128]{4,3,2,1,0:T(8,128)(2,1)}, bf16[3,4,4,192,128]{4,3,2,1,0:T(8,128)(2,1)S(1)}, u32[]{:S(2)}) copy-start(bf16[3,4,4,192,128]{4,3,2,1,0:T(8,128)(2,1)S(1)} %collective-permute-done.3) | copy-start | bytes 7077892 | tf_op jit(solution)/shard_map/cond
  64.8 60.2 %collective-permute-start.4 = (bf16[3,2,4,192,128]{4,3,2,1,0:T(8,128)(2,1)}, bf16[3,2,4,192,128]{4,3,2,1,0:T(8,128)(2,1)}, u32[]{:S(2)}, u32[]{:S(2)}) collective-permute-start(bf16[3,2,4,192,128]{4,3,2,1,0:T(8,128)(2,1)} %slice.16), channel_id=1, source_target_pairs={{0,4},{1,5},{2,6},{3,7},{4,8},{5,9},{6,10},{7,11},{8,12},{9,13},{1... | collective-permute-start | bytes 3538952 | tf_op jit(solution)/shard_map/cond/branch_0_fun/ppermute | solution.py:523
  69.1 8.2 %copy-start.8 = (bf16[192,2048]{1,0:T(8,128)(2,1)S(1)}, bf16[192,2048]{1,0:T(8,128)(2,1)}, u32[]{:S(2)}) copy-start(bf16[192,2048]{1,0:T(8,128)(2,1)} %get-tuple-element.149) | copy-start | bytes 2359300 | tf_op jit(solution)/shard_map/cond
  69.1 55.9 %collective-permute-start.5 = (bf16[3,2,4,192,128]{4,3,2,1,0:T(8,128)(2,1)}, bf16[3,2,4,192,128]{4,3,2,1,0:T(8,128)(2,1)}, u32[]{:S(2)}, u32[]{:S(2)}) collective-permute-start(bf16[3,2,4,192,128]{4,3,2,1,0:T(8,128)(2,1)} %slice.17), channel_id=1, source_target_pairs={{0,12},{1,13},{2,14},{3,15},{4,0},{5,1},{6,2},{7,3},{8,4},{9,5},{1... | collective-permute-start | bytes 3538952 | tf_op jit(solution)/shard_map/cond/branch_0_fun/ppermute | solution.py:523
  73.8 32.5 %all-to-all-start.8 = ((bf16[4,1040,128]{2,1,0:T(8,128)(2,1)}), bf16[4,1040,128]{2,1,0:T(8,128)(2,1)S(1)}, u32[]{:S(2)}, u32[]{:S(2)}) async-start(bf16[4,1040,128]{2,1,0:T(8,128)(2,1)} %broadcast_in_dim.12), calls=%async_computation.8 | async-start | bytes 2129920 | tf_op jit(solution)/shard_map/cond/branch_0_fun/all_to_all | solution.py:519
  77.3 44.8 %collective-permute-start.6 = (bf16[192,2048]{1,0:T(8,128)(2,1)S(1)}, bf16[192,2048]{1,0:T(8,128)(2,1)}, u32[]{:S(2)}, u32[]{:S(2)}) collective-permute-start(bf16[192,2048]{1,0:T(8,128)(2,1)S(1)} %copy-done.8), channel_id=1, source_target_pairs={{0,4},{1,5},{2,6},{3,7},{4,8},{5,9},{6,10},{7,11},{8,12},{9,13},{1... | collective-permute-start | bytes 2359304 | tf_op jit(solution)/shard_map/cond/branch_0_fun/ppermute | solution.py:523
  80.6 44.4 %collective-permute-start.7 = (bf16[192,2048]{1,0:T(8,128)(2,1)S(1)}, bf16[192,2048]{1,0:T(8,128)(2,1)}, u32[]{:S(2)}, u32[]{:S(2)}) collective-permute-start(bf16[192,2048]{1,0:T(8,128)(2,1)S(1)} %copy-done.8), channel_id=1, source_target_pairs={{0,12},{1,13},{2,14},{3,15},{4,0},{5,1},{6,2},{7,3},{8,4},{9,5},{1... | collective-permute-start | bytes 2359304 | tf_op jit(solution)/shard_map/cond/branch_0_fun/ppermute | solution.py:523
  107.0 18.0 %all-to-all-start.9 = ((bf16[4,16,768]{2,1,0:T(8,128)(2,1)}), bf16[4,16,768]{2,1,0:T(8,128)(2,1)}, u32[]{:S(2)}, u32[]{:S(2)}) async-start(bf16[4,16,768]{2,1,0:T(8,128)(2,1)} %broadcast_in_dim.14), calls=%async_computation.9 | async-start | bytes 196608 | tf_op jit(solution)/shard_map/cond/branch_0_fun/all_to_all | solution.py:519
  126.1 9.8 %collective-permute-start.8 = (bf16[192,1024]{1,0:T(8,128)(2,1)S(1)}, bf16[192,1024]{1,0:T(8,128)(2,1)S(1)}, u32[]{:S(2)}, u32[]{:S(2)}) collective-permute-start(bf16[192,1024]{1,0:T(8,128)(2,1)S(1)} %slice.18), channel_id=1, source_target_pairs={{0,4},{1,5},{2,6},{3,7},{4,8},{5,9},{6,10},{7,11},{8,12},{9,13},{1... | collective-permute-start | bytes 1179656 | tf_op jit(solution)/shard_map/cond/branch_0_fun/ppermute | solution.py:523
  131.0 8.8 %collective-permute-start.9 = (bf16[192,1024]{1,0:T(8,128)(2,1)S(1)}, bf16[192,1024]{1,0:T(8,128)(2,1)S(1)}, u32[]{:S(2)}, u32[]{:S(2)}) collective-permute-start(bf16[192,1024]{1,0:T(8,128)(2,1)S(1)} %slice.19), channel_id=1, source_target_pairs={{0,12},{1,13},{2,14},{3,15},{4,0},{5,1},{6,2},{7,3},{8,4},{9,5},{1... | collective-permute-start | bytes 1179656 | tf_op jit(solution)/shard_map/cond/branch_0_fun/ppermute | solution.py:523
  135.8 4.0 %copy-start.10 = (bf16[192,1024]{1,0:T(8,128)(2,1)}, bf16[192,1024]{1,0:T(8,128)(2,1)S(1)}, u32[]{:S(2)}) copy-start(bf16[192,1024]{1,0:T(8,128)(2,1)S(1)} %collective-permute-done.8) | copy-start | bytes 1179652 | tf_op jit(solution)/shard_map/cond
  139.8 0.7 copy-start.13
  140.6 2.3 collective-permute-start.13
  142.1 0.7 collective-permute-start.11
  143.1 1.4 collective-permute-start.14
  143.8 0.8 collective-permute-start.15
  144.6 78.2 %collective-permute-start.16 = (bf16[128,768]{1,0:T(8,128)(2,1)}, bf16[128,768]{1,0:T(8,128)(2,1)S(1)}, u32[]{:S(2)}, u32[]{:S(2)}) collective-permute-start(bf16[128,768]{1,0:T(8,128)(2,1)} %get-tuple-element.295), channel_id=1, source_target_pairs={{32,48},{96,112},{160,176},{224,240},{288,304},{352,368},{416,432}... | collective-permute-start | bytes 589832 | tf_op jit(solution)/shard_map/ppermute | solution.py:737
  222.8 15.1 %copy-start.4 = (bf16[3,3072,128]{2,1,0:T(8,128)(2,1)S(1)}, bf16[3,3072,128]{2,1,0:T(8,128)(2,1)}, u32[]{:S(2)}) copy-start(bf16[3,3072,128]{2,1,0:T(8,128)(2,1)} %get-tuple-element.187) | copy-start | bytes 7077892 | tf_op jit(solution)/shard_map/cond
  243.0 12.3 %copy-start.12 = (bf16[192,1024]{1,0:T(8,128)(2,1)S(1)}, bf16[192,1024]{1,0:T(8,128)(2,1)}, u32[]{:S(2)}) copy-start(bf16[192,1024]{1,0:T(8,128)(2,1)} %get-tuple-element.198.refs_3_) | copy-start | bytes 1179652 | tf_op jit(solution)/shard_map/cond
  243.0 12.3 %copy-start.15 = (bf16[192,1024]{1,0:T(8,128)(2,1)S(1)}, bf16[192,1024]{1,0:T(8,128)(2,1)}, u32[]{:S(2)}) copy-start(bf16[192,1024]{1,0:T(8,128)(2,1)} %get-tuple-element.199.refs_4_) | copy-start | bytes 1179652 | tf_op jit(solution)/shard_map/cond
